TPU v7x, 32 devices: a whole 2x2x4 slice. The times are simulated.
32 devices in a mesh: ctx: 8 (over y, x, core), fsdp: 4 (over z).
Axes of the slice: x: 2, y: 2, z: 4, core: 2. Of those that a mesh axis runs over, the one named last changes fastest.
Arguments:
- tokens: bfloat16 [4096, 4096], P(('ctx', 'fsdp')), may hold values from -360 to 360
- norm_gain: float32 [4096], replicated, may hold values from 0.1 to 1.9
- qkv_weight: bfloat16 [3, 4096, 2048], P(None, 'ctx', 'fsdp'), may hold values from -1 to 1
- out_weight: bfloat16 [2048, 4096], P('fsdp', 'ctx'), may hold values from -1 to 1
- layout: int32 [32, 16], replicated, may hold values from 0 to 31, as said below
Outputs:
- branch_out: bfloat16 [4096, 4096], P(('ctx', 'fsdp'))
Inputs may be any that keep to these rules, and one draw needn't show every extreme that they name: `layout`: every entry of query block i names a block of 0 to i. With the blocks taken in spans of 4, the query blocks of one span name at most 2 distinct blocks of any other span, and some pair of spans reaches 2 in every draw.
All inputs are finite; a program needn't handle non-finite values.
Results may differ from a plain program's by a relative error of at most 0.015.
Values may be sent and summed in bfloat16 or wider, within the bound.
No kernel may reach another device: no remote copies, remote signals or barrier semaphores. Data moves between devices by JAX's collectives and lax.ppermute only.
A program may use at most 128 MiB of HBM per device.

v0:
```python
import math

import jax
import jax.numpy as jnp
from jax import lax
from jax.sharding import PartitionSpec as P

HEAD_DIM = 128
BLK = 128
SUMMARY = 16


EPSILON = 1e-05


def normalize(tokens, norm_gain):
    features = tokens.astype(jnp.float32)
    mean_square = jnp.mean(features * features, axis=-1, keepdims=True)
    return (features * lax.rsqrt(mean_square + EPSILON) * norm_gain).astype(jnp.bfloat16)


def shards(tokens, norm_gain, qkv_weight, out_weight, layout):
    normed = normalize(tokens, norm_gain)
    gathered = lax.all_gather(normed, "fsdp", axis=0, tiled=True)
    span_rows = gathered.shape[0]
    local_width = qkv_weight.shape[2]
    heads_here = local_width // HEAD_DIM
    projected = jnp.einsum(
        "td,cdi->cti",
        gathered,
        lax.all_gather(qkv_weight, "ctx", axis=1, tiled=True),
        preferred_element_type=jnp.float32,
    ).astype(jnp.bfloat16)
    queries, key_rows, value_rows = (projected[0], projected[1], projected[2])
    ctx_index = lax.axis_index("ctx")
    span_blocks = span_rows // BLK
    key_slots = 2 + SUMMARY
    first_block = ctx_index * span_blocks
    own_blocks = first_block + jnp.arange(span_blocks, dtype=jnp.int32)
    listed = lax.dynamic_slice_in_dim(layout, first_block, span_blocks, 0)
    key_index = jnp.concatenate([own_blocks[:, None], own_blocks[:, None] - 1, listed], axis=1)
    every_key, every_value = (
        lax.all_gather(key_rows, "ctx", axis=0, tiled=True),
        lax.all_gather(value_rows, "ctx", axis=0, tiled=True),
    )
    total_blocks = every_key.shape[0] // BLK
    pool_keys = every_key.reshape(total_blocks, BLK, local_width)
    pool_values = every_value.reshape(total_blocks, BLK, local_width)
    gather_index = jnp.maximum(key_index, 0)
    group_size = math.gcd(span_blocks, max(1, 512 // BLK))
    group_count = span_blocks // group_size
    score_scale = HEAD_DIM ** (-0.5)
    offsets = jnp.arange(BLK, dtype=jnp.int32)

    def attend(packed):
        group_queries, group_index, group_slots, group_blocks = packed
        key_blocks = pool_keys[group_index].reshape(
            group_size, key_slots, BLK, heads_here, HEAD_DIM
        )
        value_blocks = pool_values[group_index].reshape(
            group_size, key_slots, BLK, heads_here, HEAD_DIM
        )
        scores = (
            jnp.einsum(
                "bqhd,bnkhd->bhqnk", group_queries, key_blocks, preferred_element_type=jnp.float32
            )
            * score_scale
        )
        query_pos = group_blocks[:, None] * BLK + offsets[None, :]
        key_pos = group_slots[:, :, None] * BLK + offsets[None, None, :]
        allowed = (key_pos[:, None, :, :] <= query_pos[:, :, None, None]) & (
            key_pos[:, None, :, :] >= 0
        )
        allowed = allowed[:, None]
        scores = jnp.where(allowed, scores, -1e30)
        row_max = jnp.max(scores, axis=(3, 4), keepdims=True)
        weights = jnp.where(allowed, jnp.exp(scores - row_max), 0.0)
        denominator = jnp.sum(weights, axis=(3, 4), keepdims=True)
        weights = (weights / denominator).astype(jnp.bfloat16)
        blended = jnp.einsum(
            "bhqnk,bnkhd->bqhd", weights, value_blocks, preferred_element_type=jnp.float32
        )
        return blended.astype(jnp.bfloat16)

    packed_inputs = (
        queries.reshape(group_count, group_size, BLK, heads_here, HEAD_DIM),
        gather_index.reshape(group_count, group_size, key_slots),
        key_index.reshape(group_count, group_size, key_slots),
        own_blocks.reshape(group_count, group_size),
    )
    blended_all = lax.map(attend, packed_inputs)
    attended = blended_all.reshape(span_rows, local_width)
    projection = lax.all_gather(out_weight, "ctx", axis=1, tiled=True)
    return lax.psum_scatter(
        jnp.dot(attended, projection, preferred_element_type=jnp.float32).astype(jnp.bfloat16),
        "fsdp",
        scatter_dimension=0,
        tiled=True,
    )


def solution(mesh):
    placed = (P(("ctx", "fsdp"), None), P(), P(None, "ctx", "fsdp"), P("fsdp", "ctx"), P())
    return jax.shard_map(
        shards, mesh=mesh, in_specs=placed, out_specs=P(("ctx", "fsdp"), None), check_vma=False
    )
```

profile of v0, /device:TPU:0, one launch (start us, length us, event | category | flops | bytes accessed | tf_op | source)
XLA Modules:
  0.0 395.5 jit_solution(267538399377155814)
XLA Ops:
  6.5 0.0 copy-start
  6.5 0.0 all-gather.8.cloned.1.call-start
  6.5 1.5 fusion.7
  8.1 2.5 fusion.9
  10.6 0.0 all-gather.8.cloned.1.call-update
  10.6 0.0 all-gather.10.cloned.1.call-start
  10.7 0.7 all-gather.10.cloned.1.call-update
  11.4 0.0 all-gather.16.cloned.1.call-start
  11.4 82.8 %all-gather.8.cloned.1.call-done = bf16[512,4096]{1,0:T(8,128)(2,1)} async-done(((bf16[128,4096]{1,0:T(8,128)(2,1)}), bf16[512,4096]{1,0:T(8,128)(2,1)}) %all-gather.8.cloned.1.call-update) | async-done | bytes 4194320 | tf_op jit(solution)/shard_map/all_gather | solution.py:24
  94.2 72.6 %all-gather.10.cloned.1.call-done = bf16[3,4096,512]{2,1,0:T(8,128)(2,1)} async-done(((bf16[3,512,512]{2,1,0:T(8,128)(2,1)}), bf16[3,4096,512]{2,1,0:T(8,128)(2,1)}) %all-gather.10.cloned.1.call-update) | async-done | bytes 12582928 | tf_op jit(solution)/shard_map/all_gather | solution.py:31
  166.8 10.9 %fusion.13 = bf16[3,512,512]{2,1,0:T(8,128)(2,1)S(1)} fusion(bf16[3,4096,512]{2,1,0:T(8,128)(2,1)} %all-gather.10.cloned.1.call-done, bf16[512,4096]{1,0:T(8,128)(2,1)} %all-gather.8.cloned.1.call-done), kind=kOutput, calls=%fused_computation.20 | convolution fusion | flops 6443237376 | bytes 18350080 | tf_op jit(solution)/shard_map/td,cdi->cti/dot_general | solution.py:28
  177.7 1.1 fusion.35
  178.9 0.0 all-gather.16.cloned.1.call-update
  178.9 0.0 all-gather.14.cloned.1.call-start
  178.9 0.5 all-gather.14.cloned.1.call-update
  179.5 0.0 all-gather.12.cloned.1.call-start
  179.5 0.5 all-gather.12.cloned.1.call-update
  180.0 0.2 reduce-scatter.2.cloned.1.call-start
  180.3 0.0 copy-done
  180.3 0.1 constant_dynamic-slice_fusion
  180.4 0.1 copy.44
  180.5 0.1 add_multiply_fusion
  180.5 0.1 iota_add_fusion
  180.6 0.1 broadcast_compare_fusion
  180.7 0.1 iota_add_fusion.1
  180.8 0.1 add_maximum_fusion
  180.9 0.1 reshape.128
  181.0 3.5 compare_and_fusion
  184.5 0.1 squeeze.20
  184.6 31.1 %all-gather.16.cloned.1.call-done = bf16[1,4096,512]{2,1,0:T(8,128)(2,1)} async-done(((bf16[1,512,512]{2,1,0:T(8,128)(2,1)}), bf16[1,4096,512]{2,1,0:T(8,128)(2,1)}) %all-gather.16.cloned.1.call-update) | async-done | bytes 4194320 | tf_op jit(solution)/shard_map/all_gather | solution.py:43
  215.7 8.1 %gather_fusion.1 = bf16[72,128,512]{2,1,0:T(8,128)(2,1)} fusion(bf16[32,128,512]{2,1,0:T(8,128)(2,1)} %bitcast.46, s32[1024]{0:T(1024)S(1)} %pad_clamp_fusion), kind=kCustom, calls=%fused_computation.1 | custom fusion | bytes 18874656 | tf_op jit(solution)/shard_map/while/body/eval_jaxpr/gather | solution.py:57
  223.9 12.7 %copy.36 = bf16[72,128,512]{1,2,0:T(8,128)(2,1)} copy(bf16[72,128,512]{2,1,0:T(8,128)(2,1)} %gather_fusion.1) | data formatting | bytes 18874368 | tf_op jit(solution)/shard_map/while/body/eval_jaxpr/gather | solution.py:57
  236.5 12.0 %copy.38 = bf16[4,18,128,4,128]{4,2,1,3,0:T(8,128)(2,1)} copy(bf16[4,18,128,4,128]{2,4,3,1,0:T(8,128)(2,1)} %bitcast.45) | data formatting | bytes 18874368 | tf_op jit(solution)/shard_map/while/body/eval_jaxpr/reshape | solution.py:57
  248.6 5.7 %all-gather.14.cloned.1.call-done = bf16[1,4096,512]{2,1,0:T(8,128)(2,1)} async-done(((bf16[1,512,512]{2,1,0:T(8,128)(2,1)}), bf16[1,4096,512]{2,1,0:T(8,128)(2,1)}) %all-gather.14.cloned.1.call-update) | async-done | bytes 4194320 | tf_op jit(solution)/shard_map/all_gather | solution.py:44
  254.2 8.1 %gather_fusion = bf16[72,128,512]{2,1,0:T(8,128)(2,1)} fusion(bf16[32,128,512]{2,1,0:T(8,128)(2,1)} %bitcast.47, s32[1024]{0:T(1024)S(1)} %pad_clamp_fusion), kind=kCustom, calls=%fused_computation | custom fusion | bytes 18874656 | tf_op jit(solution)/shard_map/while/body/eval_jaxpr/gather | solution.py:60
  262.3 12.8 %copy.35 = bf16[72,128,512]{1,2,0:T(8,128)(2,1)} copy(bf16[72,128,512]{2,1,0:T(8,128)(2,1)} %gather_fusion) | data formatting | bytes 18874368 | tf_op jit(solution)/shard_map/while/body/eval_jaxpr/gather | solution.py:60
  275.1 5.7 %fusion.27 = f32[4,4,128,2304]{2,3,1,0:S(1)} fusion(bf16[4,4,128,2304]{2,3,1,0:T(8,128)(2,1)} %bitcast.44, bf16[4,128,4,128]{3,2,1,0:T(4,128)(2,1)S(1)} %squeeze.20), kind=kOutput, calls=%fused_computation.26 | convolution fusion | flops 1207959552 | bytes 28835840
  280.8 0.0 copy-start.2
  280.8 2.7 fusion
  283.5 3.7 copy-done.2
  287.3 4.7 %fusion.1 = f32[4,4,128]{2,1,0:T(4,128)S(1)} fusion(f32[4,4,128,18,128]{2,4,3,1,0:T(8,128)S(1)} %bitcast.42, f32[4,4,128]{2,1,0:T(4,128)S(1)} %fusion, pred[4,128,18,128]{1,3,2,0:T(8,128)(4,1)S(1)} %compare_and_fusion), kind=kLoop, calls=%fused_computation.6 | loop fusion | flops 23590912 | bytes 20070400 | tf_op jit(solution)/shard_map/while/body/eval_jaxpr/reduce_sum | solution.py:78
  292.0 0.0 copy-start.1
  292.0 12.9 %fusion.22 = bf16[4,128,4,128]{1,3,2,0:T(8,128)(2,1)S(1)} fusion(f32[4,4,128,18,128]{2,4,3,1,0:T(8,128)} %bitcast.43, f32[4,4,128]{2,1,0:T(4,128)S(1)} %fusion.1, f32[4,4,128]{2,1,0:T(4,128)S(1)} %fusion, pred[4,128,18,128]{1,3,2,0:T(8,128)(4,1)S(1)} %compare_and_fusion, bf16[4,18,128,4,128]{2,4,3,1,0:T(8,128)(2,1)} %bitcast.48), kind=kOutput, calls=%fused_computation.23 | convolution fusion | flops 1236533248 | bytes 30031872 | tf_op jit(solution)/shard_map/while/body/eval_jaxpr/bhqnk,bnkhd->bqhd/dot_general | solution.py:80
  304.9 0.3 copy.41
  305.2 0.0 all-gather.12.cloned.1.call-done
  305.2 6.5 %convolution_convert_fusion = bf16[512,4096]{1,0:T(8,128)(2,1)} fusion(bf16[512,4096]{1,0:T(8,128)(2,1)} %all-gather.12.cloned.1.call-done, bf16[64,8,4,128]{3,2,1,0:T(4,128)(2,1)S(1)} %bitcast.49), kind=kOutput, calls=%fused_computation.10 | convolution fusion | flops 2149580800 | bytes 8912896 | tf_op jit(solution)/shard_map/dot_general | solution.py:95
  311.7 0.0 reduce-scatter.2.cloned.1.call-update
  311.7 76.9 %reduce-scatter.2.cloned.1.call-done = bf16[128,4096]{1,0:T(8,128)(2,1)} async-done(((bf16[512,4096]{1,0:T(8,128)(2,1)}), bf16[128,4096]{1,0:T(8,128)(2,1)}) %reduce-scatter.2.cloned.1.call-update) | async-done | bytes 1048592 | tf_op jit(solution)/shard_map/reduce_scatter | solution.py:94
  388.6 0.0 copy-done.1
  (5 shorter events, 0.0 us)
Async XLA Ops:
  6.5 173.8 %copy-start = (s32[32,16]{0,1:T(8,128)S(1)}, s32[32,16]{0,1:T(8,128)}, u32[]{:S(2)}) copy-start(s32[32,16]{0,1:T(8,128)} %param.9) | copy-start | bytes 6148
  6.5 87.7 %all-gather.8.cloned.1.call-start = ((), (), s32[]{:S(2)}) async-start(), calls=%async_computation.1 | async-start | bytes 5242880 | tf_op jit(solution)/shard_map/all_gather | solution.py:24
  10.6 156.2 %all-gather.10.cloned.1.call-start = ((), (), s32[]{:S(2)}) async-start(), calls=%async_computation.2 | async-start | bytes 14155776 | tf_op jit(solution)/shard_map/all_gather | solution.py:31
  11.4 204.4 %all-gather.16.cloned.1.call-start = ((), (), s32[]{:S(2)}) async-start(), calls=%async_computation.6 | async-start | bytes 4718592 | tf_op jit(solution)/shard_map/all_gather | solution.py:43
  178.9 75.4 %all-gather.14.cloned.1.call-start = ((), (), s32[]{:S(2)}) async-start(), calls=%async_computation.5 | async-start | bytes 4718592 | tf_op jit(solution)/shard_map/all_gather | solution.py:44
  179.5 125.8 %all-gather.12.cloned.1.call-start = ((), (), s32[]{:S(2)}) async-start(), calls=%async_computation.3 | async-start | bytes 4718592 | tf_op jit(solution)/shard_map/all_gather | solution.py:93
  180.0 208.6 %reduce-scatter.2.cloned.1.call-start = ((), (), s32[]{:S(2)}) async-start(), calls=%async_computation.4 | async-start | bytes 5242880 | tf_op jit(solution)/shard_map/reduce_scatter | solution.py:94
  280.8 6.5 %copy-start.2 = (f32[4,4,128,2304]{2,3,1,0}, f32[4,4,128,2304]{2,3,1,0:S(1)}, u32[]{:S(2)}) copy-start(f32[4,4,128,2304]{2,3,1,0:S(1)} %fusion.27) | copy-start | bytes 56623108
  292.0 96.7 %copy-start.1 = (s32[32,16]{0,1:T(8,128)S(1)}, s32[32,16]{0,1:T(8,128)}, u32[]{:S(2)}) copy-start(s32[32,16]{0,1:T(8,128)} %param.9) | copy-start | bytes 6148
Sparse Core Ops, SparseCore 0:
  10.8 83.4 all-gather.7
  96.1 70.6 all-gather.9
  179.0 36.7 all-gather.15
  217.5 36.7 all-gather.13
  256.0 37.4 all-gather.11
  311.9 76.7 reduce-scatter.1
where the time goes:
time: 397 us; the launch traced here: 395 us
  waiting for transfers between devices  271 us (68%)
  local copies, waits for them, and re-layouts  59.2 us (15%)
  matrix products  36 us (9%)
  other arithmetic  15.4 us (4%)
  between operations  13.6 us (3%)
    all_gather x1, waiting for transfers between devices, shards(): gathered = lax.all_gather(normed, 'fsdp', axis=0, tiled=True)  82.8 us
    reduce_scatter x1, waiting for transfers between devices, shards(): lax.psum_scatter(jnp.dot(attended, projection, preferred_element_type=jnp...  76.9 us
    all_gather x1, waiting for transfers between devices, shards(): lax.all_gather(qkv_weight, 'ctx', axis=1, tiled=True)  72.6 us
    all_gather x1, waiting for transfers between devices, shards(): lax.all_gather(key_rows, 'ctx', axis=0, tiled=True)  31.1 us
    gather x2, local copies, waits for them, and re-layouts, attend(): pool_values[group_index]  20.8 us
    gather x2, local copies, waits for them, and re-layouts, attend(): pool_keys[group_index]  20.8 us
    dot_general x1, matrix products, attend(): jnp.einsum('bhqnk,bnkhd->bqhd', weights, value_blocks, preferred_element_...  12.9 us
    reshape x1, local copies, waits for them, and re-layouts, attend(): pool_keys[group_index]  12 us
  transfers between devices with their start and end apart: 6, of which 5 were waited for; matrix products, arithmetic and copies ran while one was open for 21% of the time, Pallas kernels for 0%

commit v1 on v0

v1 whole, which is shorter than its diff:
```python
import functools
import math

import jax
import jax.numpy as jnp
import numpy as np
from jax import lax
from jax.experimental import pallas as pl
from jax.experimental.pallas import tpu as pltpu
from jax.sharding import Mesh
from jax.sharding import PartitionSpec as P

HEAD_DIM = 128
BLK = 128
EPSILON = 1e-05
MASKED = -1e30
F32 = jnp.float32
BF16 = jnp.bfloat16


def xor_pairs(size, bit):
    return [(i, i ^ bit) for i in range(size)]


def line_order(size):
    if size != 4:
        return [list(range(size))] * size
    return [[0, 1, 2, 3], [1, 2, 3, 0], [2, 1, 0, 3], [3, 2, 1, 0]]


def line_gather(part, axis, size):
    if size != 4:
        whole = lax.all_gather(part, axis, axis=0)
        return [whole[i] for i in range(size)]
    low = lax.axis_index(axis) < 2
    up = lax.ppermute(part, axis, [(0, 1), (1, 2), (2, 3)])
    down = lax.ppermute(part, axis, [(1, 0), (2, 1), (3, 2)])
    up2 = lax.ppermute(up, axis, [(1, 2), (2, 3)])
    down2 = lax.ppermute(down, axis, [(2, 1), (1, 0)])
    second = jnp.where(low, down2, up2)
    ends = lax.ppermute(second, axis, [(2, 3), (1, 0)])
    near = jnp.where(low, down, up)
    inner = jnp.where(low, up, down)
    at = lax.axis_index(axis)
    last = jnp.where((at == 1) | (at == 2), inner, ends)
    return [part, near, second, last]


def plane_order(size, at):
    return [at ^ r if size == 4 else jnp.int32(r) for r in range(size)]


def plane_gather(part, axis, size):
    if size != 4:
        whole = lax.all_gather(part, axis, axis=0)
        return [whole[i] for i in range(size)]
    one = lax.ppermute(part, axis, xor_pairs(4, 1))
    two = lax.ppermute(part, axis, xor_pairs(4, 2))
    half = part.shape[-2] // 2
    first = lax.ppermute(two[..., :half, :], axis, xor_pairs(4, 1))
    other = lax.ppermute(one[..., half:, :], axis, xor_pairs(4, 2))
    return [part, one, two, jnp.concatenate([first, other], axis=-2)]


def pair_order(size, at):
    return [at ^ r if size == 2 else jnp.int32(r) for r in range(size)]


def pair_gather(part, axis, size):
    if size != 2:
        whole = lax.all_gather(part, axis, axis=0)
        return [whole[i] for i in range(size)]
    return [part, lax.ppermute(part, axis, xor_pairs(2, 1))]


def normalize_kernel(order, tokens, gain, out):
    features = tokens[...].astype(F32)
    mean_square = jnp.mean(features * features, axis=-1, keepdims=True)
    scale = lax.rsqrt(mean_square + EPSILON)
    count = order.shape[0]
    width = tokens.shape[1] // count
    for r in range(count):
        source = pl.ds(pl.multiple_of(order[r] * width, width), width)
        out[:, r * width : (r + 1) * width] = (
            tokens[:, source].astype(F32) * scale * gain[:, source]
        ).astype(BF16)


def normalize(tokens, norm_gain, order):
    return pl.pallas_call(
        normalize_kernel,
        out_shape=jax.ShapeDtypeStruct(tokens.shape, BF16),
        in_specs=[
            pl.BlockSpec(memory_space=pltpu.SMEM),
            pl.BlockSpec(memory_space=pltpu.VMEM),
            pl.BlockSpec(memory_space=pltpu.VMEM),
        ],
        out_specs=pl.BlockSpec(memory_space=pltpu.VMEM),
        compiler_params=pltpu.CompilerParams(vmem_limit_bytes=16 << 20),
        name="normalize",
    )(order, tokens, norm_gain.reshape(1, -1))


def attention_kernel(
    sizes, places, biases, copies, targets, *refs
):
    groups, reps, heads, spans, slots = sizes
    total = sum(groups)
    queries = refs[: len(groups)]
    pairs = refs[len(groups) : len(groups) * (1 + reps)]
    out, held, asked, sems = refs[len(groups) * (1 + reps) :]
    waits = []
    at = 0
    for g, size in enumerate(groups):
        waits.append(pltpu.make_async_copy(queries[g], asked.at[:, at : at + size], sems.at[len(waits)]))
        for r in range(reps):
            waits.append(
                pltpu.make_async_copy(
                    pairs[g * reps + r], held.at[r, :, :, at : at + size], sems.at[len(waits)]
                )
            )
        at += size
    for copy in waits:
        copy.start()
    for copy in waits:
        copy.wait()
    flat = held.reshape(reps * heads * 2 * total, BLK, HEAD_DIM)
    wanted = asked.reshape(heads * total, BLK, HEAD_DIM)
    factor = HEAD_DIM ** (-0.5) * math.log2(math.e)
    rows = lax.broadcasted_iota(jnp.int32, (BLK, BLK), 0)
    columns = lax.broadcasted_iota(jnp.int32, (BLK, BLK), 1)

    def one_block(j, carry):
        query = wanted[j]
        index = [places[j, n] for n in range(slots)]
        keys = jnp.concatenate([flat[index[n]] for n in range(slots)], axis=0)
        scores = lax.dot_general(
            query, keys, (((1,), (1,)), ((), ())), preferred_element_type=F32
        )
        parts = []
        for n in range(slots):
            part = scores[:, n * BLK : (n + 1) * BLK] * factor
            parts.append(jnp.where(columns <= rows, part, MASKED) if n == 0 else part + biases[j, n])
        top = parts[0]
        for n in range(1, slots):
            top = jnp.maximum(top, parts[n])
        top = jnp.max(top, axis=1, keepdims=True)
        weights = [jnp.exp2(part - top) for part in parts]
        weights[0] = weights[0] * copies[j]
        below = weights[0]
        for n in range(1, slots):
            below = below + weights[n]
        below = jnp.sum(below, axis=1, keepdims=True)
        values = jnp.concatenate([flat[index[n] + total] for n in range(slots)], axis=0)
        blended = jnp.dot(
            jnp.concatenate([w.astype(BF16) for w in weights], axis=1), values, preferred_element_type=F32
        )
        out[targets[j]] = (blended / below).astype(BF16)
        return carry

    lax.fori_loop(0, heads * total, one_block, 0)


def attention(queries, pairs, places, biases, copies, targets, sizes):
    groups, reps, heads, spans, slots = sizes
    total = sum(groups)
    smem = pl.BlockSpec(memory_space=pltpu.SMEM)
    hbm = pl.BlockSpec(memory_space=pl.ANY)
    blocks = heads * total
    return pl.pallas_call(
        functools.partial(attention_kernel, sizes),
        out_shape=jax.ShapeDtypeStruct((blocks, BLK, HEAD_DIM), BF16),
        in_specs=[smem] * 4 + [hbm] * (len(queries) + len(pairs)),
        out_specs=pl.BlockSpec(memory_space=pltpu.VMEM),
        scratch_shapes=[
            pltpu.VMEM((reps, heads, 2, total, BLK, HEAD_DIM), BF16),
            pltpu.VMEM((heads, total, BLK, HEAD_DIM), BF16),
            pltpu.SemaphoreType.DMA((len(groups) * (1 + reps),)),
        ],
        compiler_params=pltpu.CompilerParams(vmem_limit_bytes=40 << 20),
        name="attention",
    )(places, biases, copies, targets, *queries, *pairs)


def shards(heads, reps, lines, tokens, norm_gain, qkv_weight, out_weight, layout):
    head_at, rep_at, line_at = (lax.axis_index(a) for a in ("head", "rep", "line"))
    rows = tokens.shape[0]
    assert rows == BLK
    width = qkv_weight.shape[2]
    spans = heads * reps
    order = jnp.asarray(line_order(lines), jnp.int32)[line_at]
    planes = plane_order(heads, head_at)
    sides = pair_order(reps, rep_at)
    feature_order = jnp.stack([h * reps + r for r in sides for h in planes]).astype(jnp.int32)

    by_plane = plane_gather(qkv_weight, "head", heads)
    by_side = [pair_gather(w, "rep", reps) for w in by_plane]
    weight = jnp.concatenate([by_side[h][r] for r in range(reps) for h in range(heads)], axis=1)

    normed = normalize(tokens, norm_gain, feature_order)
    half = rows // 2
    lower = line_gather(normed[:half], "line", lines)
    upper = line_gather(normed[half:], "line", lines)
    chunks = [jnp.concatenate(pair, axis=0) for pair in zip(lower, upper)]

    groups = (lines - 1, 1)
    queries, pairs = [], []
    at = 0
    for size in groups:
        rows_here = jnp.concatenate(chunks[at : at + size], axis=0)
        at += size
        projected = jnp.einsum("td,cdi->cti", rows_here, weight, preferred_element_type=F32).astype(BF16)
        split = projected.reshape(3, size, BLK, heads, HEAD_DIM).transpose(3, 0, 1, 2, 4)
        mine = lax.all_to_all(split, "head", 0, 0, tiled=True)
        queries.append(mine[:, 0])
        pairs += pair_gather(mine[:, 1:], "rep", reps)

    blocks = spans * lines
    names = jnp.arange(blocks, dtype=jnp.int32)
    slot_of = jnp.argmax(order[None, :] == jnp.arange(lines, dtype=jnp.int32)[:, None], axis=1).astype(jnp.int32)
    span_of = names // lines
    rep_of, head_of = span_of % reps, span_of // reps
    side_of = rep_of ^ rep_at if reps == 2 else rep_of
    place_of = ((side_of * heads + head_of) * 2) * lines + slot_of[names % lines]
    own = (
        (jnp.arange(heads, dtype=jnp.int32)[:, None] * reps + rep_at) * lines + order[None, :]
    ).reshape(-1)
    listed = layout[own]
    before = own - 1
    others = jnp.concatenate([before[:, None], listed], axis=1)
    index = jnp.concatenate([own[:, None], others], axis=1)
    places = place_of[jnp.maximum(index, 0)]
    off = (others < 0) | (others == own[:, None])
    biases = jnp.concatenate([jnp.zeros((own.shape[0], 1), F32), jnp.where(off, MASKED, 0.0)], axis=1)
    copies = 1.0 + jnp.sum(others == own[:, None], axis=1).astype(F32)
    targets = (jnp.arange(heads, dtype=jnp.int32)[:, None] * lines + order[None, :]).reshape(-1)
    attended = attention(
        queries, pairs, places, biases, copies, targets, (groups, reps, heads, spans, index.shape[1])
    )
    landed = lax.all_to_all(attended, ("head", "line"), 0, 0, tiled=True)
    landed = landed.reshape(heads, lines, BLK, HEAD_DIM)[:, order]
    landed = landed.transpose(2, 1, 0, 3).reshape(BLK, lines * heads * HEAD_DIM)
    everyone = jnp.concatenate(pair_gather(landed, "rep", reps), axis=0)

    by_line = line_gather(out_weight, "line", lines)
    projection = jnp.concatenate(
        [jnp.concatenate(plane_gather(w, "head", heads), axis=1) for w in by_line], axis=0
    )
    product = jnp.dot(everyone, projection, preferred_element_type=F32).astype(BF16)
    product = product.reshape(reps, BLK, heads, -1)
    if reps == 2:
        sides_out = [product[0], lax.ppermute(product[1], "rep", xor_pairs(2, 1))]
        columns = [jnp.where(rep_at == k, sides_out[0], sides_out[1]) for k in range(2)]
        columns = jnp.stack(columns, axis=2)
    else:
        columns = lax.all_to_all(product, "rep", 0, 0).transpose(1, 2, 0, 3)
    columns = columns[:, jnp.stack(planes)]
    return columns.reshape(BLK, -1)


def solution(mesh):
    spans, lines = mesh.shape["ctx"], mesh.shape["fsdp"]

    def run(tokens, norm_gain, qkv_weight, out_weight, layout):
        heads = qkv_weight.shape[2] // lines // HEAD_DIM
        reps = spans // heads
        fine = Mesh(mesh.devices.reshape(heads, reps, lines), ("head", "rep", "line"))
        ctx = ("head", "rep")
        rows = P(("head", "rep", "line"), None)
        placed = (rows, P(), P(None, ctx, "line"), P("line", ctx), P())
        return jax.shard_map(
            functools.partial(shards, heads, reps, lines),
            mesh=fine,
            in_specs=placed,
            out_specs=rows,
            check_vma=False,
        )(tokens, norm_gain, qkv_weight, out_weight, layout)

    return run
```

time: 397 us -> 280 us (0.71)
  waiting for transfers between devices: 271 us -> 90 us
  starting transfers between devices: 0.38 us -> 72.1 us
  local copies, waits for them, and re-layouts: 59.2 us -> 42.4 us
  Pallas kernels: 0 us -> 15.9 us
  between operations: 13.6 us -> 0.67 us
  matrix products: 36 us -> 40 us
    all_gather x5 -> x0, waiting for transfers between devices: 192 us -> none  [the longest x1 82.8 us: shards(): gathered = lax.all_gather(normed, 'fsdp', axis=0, tiled=True)]
    ppermute x0 -> x43, waiting for transfers between devices: none -> 88.7 us  [the longest x5 26.4 us: plane_gather(): one = lax.ppermute(part, axis, xor_pairs(4, 1))]
    reduce_scatter x1 -> x0, waiting for transfers between devices: 76.9 us -> none  [shards(): lax.psum_scatter(jnp.dot(attended, projection, preferred_element_type=jnp...]
    ppermute x0 -> x43, starting transfers between devices: none -> 54.5 us  [the longest x3 16.1 us: line_gather(): up = lax.ppermute(part, axis, [(0, 1), (1, 2), (2, 3)])]
    gather x4 -> x7, local copies, waits for them, and re-layouts: 41.6 us -> 5.58 us  [the longest x2 2.44 us: shards(): places = place_of[jnp.maximum(index, 0)]]
    all_to_all x0 -> x3, starting transfers between devices: none -> 17.6 us  [the longest x1 10.5 us: shards(): landed = lax.all_to_all(attended, ('head', 'line'), 0, 0, tiled=True)]
    pallas_call x0 -> x2, Pallas kernels: none -> 15.9 us  [the longest x1 14.8 us: attention(): pl.pallas_call(functools.partial(attention_kernel, sizes), out_shape=jax....]
    unnamed x7 -> x39, local copies, waits for them, and re-layouts: 3.82 us -> 19.3 us
  transfers between devices with their start and end apart: 6 -> 46, of which waited for: 5 -> 19; matrix products, arithmetic and copies ran while one was open for 21% -> 21% of each run, Pallas kernels for 0% -> 5%
where the time goes in v1:
time: 280 us; the launch traced here: 278 us
  waiting for transfers between devices  90 us (32%)
  starting transfers between devices  72.1 us (26%)
  local copies, waits for them, and re-layouts  42.4 us (15%)
  matrix products  40 us (14%)
  other arithmetic  17 us (6%)
  Pallas kernels  15.9 us (6%)
    dot_general x1, matrix products, shards(): jnp.dot(everyone, projection, preferred_element_type=F32).astype(BF16)  26.5 us
    ppermute x5, waiting for transfers between devices, plane_gather(): one = lax.ppermute(part, axis, xor_pairs(4, 1))  26.4 us
    ppermute x5, waiting for transfers between devices, plane_gather(): first = lax.ppermute(two[..., :half, :], axis, xor_pairs(4, 1))  21.8 us
    unnamed x39, local copies, waits for them, and re-layouts  19.3 us
    ppermute x3, starting transfers between devices, line_gather(): up = lax.ppermute(part, axis, [(0, 1), (1, 2), (2, 3)])  16.1 us
    pallas_call x1, Pallas kernels, attention(): pl.pallas_call(functools.partial(attention_kernel, sizes), out_shape=jax....  14.8 us
    dot_general x2, matrix products, shards(): jnp.einsum('td,cdi->cti', rows_here, weight, preferred_element_type=F32)  13.5 us
    ppermute x3, waiting for transfers between devices, line_gather(): down2 = lax.ppermute(down, axis, [(2, 1), (1, 0)])  12 us
  transfers between devices with their start and end apart: 46, of which 19 were waited for; matrix products, arithmetic and copies ran while one was open for 21% of the time, Pallas kernels for 5%

profile of v1, /device:TPU:0, one launch (start us, length us, event | category | flops | bytes accessed | tf_op | source)
XLA Modules:
  0.0 278.1 jit_solution(16085625099541215132)
XLA Ops:
  4.2 1.3 collective-permute-start.8
  5.4 6.4 %collective-permute-start.9 = (bf16[64,4096]{1,0:T(8,128)(2,1)}, bf16[64,4096]{1,0:T(8,128)(2,1)}, u32[]{:S(2)}, u32[]{:S(2)}) collective-permute-start(bf16[64,4096]{1,0:T(8,128)(2,1)} %get-tuple-element.16), channel_id=1, source_target_pairs={{0,1},{1,2},{2,3},{4,5},{5,6},{6,7},{8,9},{9,10},{10,11},{12,13},{... | collective-permute-start | bytes 1572872 | tf_op jit(solution)/shard_map/ppermute | solution.py:36
  11.8 1.3 collective-permute-start.10
  13.1 5.3 %collective-permute-start.11 = (bf16[64,4096]{1,0:T(8,128)(2,1)}, bf16[64,4096]{1,0:T(8,128)(2,1)}, u32[]{:S(2)}, u32[]{:S(2)}) collective-permute-start(bf16[64,4096]{1,0:T(8,128)(2,1)} %get-tuple-element.15), channel_id=1, source_target_pairs={{0,1},{1,2},{2,3},{4,5},{5,6},{6,7},{8,9},{9,10},{10,11},{12,13},{... | collective-permute-start | bytes 1572872 | tf_op jit(solution)/shard_map/ppermute | solution.py:36
  18.4 1.7 copy.40
  20.2 2.0 collective-permute-start
  25.8 1.6 collective-permute-start.1
  28.6 4.0 %collective-permute-done.10 = bf16[64,4096]{1,0:T(8,128)(2,1)} collective-permute-done((bf16[64,4096]{1,0:T(8,128)(2,1)}, bf16[64,4096]{1,0:T(8,128)(2,1)}, u32[]{:S(2)}, u32[]{:S(2)}) %collective-permute-start.10) | collective-permute-done | bytes 524320 | tf_op jit(solution)/shard_map/ppermute | solution.py:37
  32.5 1.3 collective-permute-start.12
  35.7 12.0 %collective-permute-done.12 = bf16[64,4096]{1,0:T(8,128)(2,1)S(1)} collective-permute-done((bf16[64,4096]{1,0:T(8,128)(2,1)}, bf16[64,4096]{1,0:T(8,128)(2,1)S(1)}, u32[]{:S(2)}, u32[]{:S(2)}) %collective-permute-start.12) | collective-permute-done | bytes 524320 | tf_op jit(solution)/shard_map/ppermute | solution.py:39
  47.7 1.3 collective-permute-start.14
  50.7 9.9 %collective-permute-done.1 = bf16[3,512,512]{1,2,0:T(8,128)(2,1)S(1)} collective-permute-done((bf16[3,512,512]{1,2,0:T(8,128)(2,1)S(1)}, bf16[3,512,512]{1,2,0:T(8,128)(2,1)S(1)}, u32[]{:S(2)}, u32[]{:S(2)}) %collective-permute-start.1) | collective-permute-done | bytes 1572896 | tf_op jit(solution)/shard_map/ppermute | solution.py:58
  60.6 1.3 collective-permute-start.25
  63.2 2.1 slice.89
  65.3 1.7 collective-permute-start.3
  67.9 1.6 copy-done.3
  69.6 1.3 collective-permute-start.17
  71.7 8.4 %collective-permute-done.2 = bf16[3,256,512]{1,2,0:T(8,128)(2,1)} collective-permute-done((bf16[3,256,512]{1,2,0:T(8,128)(2,1)}, bf16[3,256,512]{1,2,0:T(8,128)(2,1)}, u32[]{:S(2)}, u32[]{:S(2)}) %collective-permute-start.2) | collective-permute-done | bytes 786464 | tf_op jit(solution)/shard_map/ppermute | solution.py:60
  80.1 2.4 collective-permute-done.3
  82.5 1.5 pad_maximum_fusion
  84.0 1.3 collective-permute-done.17
  85.4 2.1 select_select_fusion.1
  87.4 1.6 constant_dynamic-update-slice_fusion.7
  89.3 4.4 %collective-permute-start.26 = (bf16[512,512]{1,0:T(8,128)(2,1)}, bf16[512,512]{1,0:T(8,128)(2,1)}, u32[]{:S(2)}, u32[]{:S(2)}) collective-permute-start(bf16[512,512]{1,0:T(8,128)(2,1)} %param.9), channel_id=1, source_target_pairs={{0,1},{1,2},{2,3},{4,5},{5,6},{6,7},{8,9},{9,10},{10,11},{12,13},{... | collective-permute-start | bytes 1572872 | tf_op jit(solution)/shard_map/ppermute | solution.py:36
  96.2 1.6 constant_dynamic-update-slice_fusion.3
  97.8 1.5 collective-permute-start.22
  99.5 1.6 collective-permute-start.21
  101.1 3.5 %collective-permute-done.26 = bf16[512,512]{1,0:T(8,128)(2,1)} collective-permute-done((bf16[512,512]{1,0:T(8,128)(2,1)}, bf16[512,512]{1,0:T(8,128)(2,1)}, u32[]{:S(2)}, u32[]{:S(2)}) %collective-permute-start.26) | collective-permute-done | bytes 524320 | tf_op jit(solution)/shard_map/ppermute | solution.py:36
  104.6 1.3 collective-permute-start.31
  105.9 1.5 collective-permute-start.32
  107.6 1.3 collective-permute-start.16
  109.1 4.6 %copy-done.5 = bf16[3,4096,512]{1,2,0:T(8,128)(2,1)} copy-done((bf16[3,4096,512]{1,2,0:T(8,128)(2,1)}, bf16[3,4096,512]{1,2,0:T(8,128)(2,1)S(1)}, u32[]{:S(2)}) %copy-start.5) | copy-done | bytes 12582936
  113.7 6.9 %fusion.48 = bf16[3,384,512]{1,2,0:T(8,128)(2,1)S(1)} fusion(bf16[3,4096,512]{1,2,0:T(8,128)(2,1)S(1)} %constant_dynamic-update-slice_fusion, bf16[384,4096]{1,0:T(8,128)(2,1)S(1)} %copy-done.4), kind=kOutput, calls=%fused_computation.49 | convolution fusion | flops 4832428032 | bytes 16908288 | tf_op jit(solution)/shard_map/td,cdi->cti/dot_general | solution.py:212
  121.0 1.9 copy.42
  123.0 3.7 %all-to-all-start = ((bf16[4,3,3,128,128]{4,3,2,1,0:T(8,128)(2,1)}), bf16[4,3,3,128,128]{4,3,2,1,0:T(8,128)(2,1)S(1)}, u32[]{:S(2)}, u32[]{:S(2)}) async-start(bf16[4,3,3,128,128]{4,3,2,1,0:T(8,128)(2,1)} %bitcast.20), calls=%async_computation | async-start | bytes 2359296 | tf_op jit(solution)/shard_map/all_to_all | solution.py:214
  126.7 5.1 %collective-permute-done.16 = bf16[64,4096]{1,0:T(8,128)(2,1)} collective-permute-done((bf16[64,4096]{1,0:T(8,128)(2,1)}, bf16[64,4096]{1,0:T(8,128)(2,1)}, u32[]{:S(2)}, u32[]{:S(2)}) %collective-permute-start.16) | collective-permute-done | bytes 524320 | tf_op jit(solution)/shard_map/ppermute | solution.py:41
  131.8 1.3 select_select_fusion.2
  133.0 6.5 %convolution_convert_fusion = bf16[3,512,128]{2,1,0:T(8,128)(2,1)S(1)} fusion(bf16[3,4096,512]{1,2,0:T(8,128)(2,1)} %copy-done.5, bf16[64,4096]{1,0:T(8,128)(2,1)S(1)} %copy-done.2, bf16[64,4096]{1,0:T(8,128)(2,1)S(1)} %select_select_fusion.2), kind=kOutput, calls=%fused_computation.50 | convolution fusion | flops 1612906496 | bytes 14024704 | tf_op jit(solution)/shard_map/td,cdi->cti/dot_general | solution.py:212
  141.1 3.5 %all-to-all-start.1 = ((bf16[4,3,1,128,128]{4,3,2,1,0:T(8,128)(2,1)}), bf16[4,3,1,128,128]{4,3,2,1,0:T(8,128)(2,1)S(1)}, u32[]{:S(2)}, u32[]{:S(2)}) async-start(bf16[4,3,1,128,128]{4,3,2,1,0:T(8,128)(2,1)} %bitcast.25), calls=%async_computation.1 | async-start | bytes 786432 | tf_op jit(solution)/shard_map/all_to_all | solution.py:214
  144.8 2.5 fusion.62
  147.3 2.4 gather_fusion.1
  150.7 1.9 broadcast_select_fusion
  152.6 1.3 collective-permute-start.37
  153.9 1.8 collective-permute-start.34
  155.8 14.8 %attention.1 = bf16[16,128,128]{2,1,0:T(8,128)(2,1)} custom-call(s32[16,18]{1,0:T(8,128)S(1)} %reshape.398.places, f32[16,18]{1,0:T(8,128)S(1)} %concatenate.91.biases, f32[16]{0:T(128)S(1)} %convert_add_fusion.copies, s32[16]{0:T(128)S(1)} %add.201.targets, bf16[4,3,128,128]{3,2,1,0:T(8,128)(2,1)S(1)} %slice_bitcast_fusion.refs_0_, ...), custom_call_target="tpu_custom_call" | custom-call | tf_op jit(solution)/shard_map/attention/pallas_call | solution.py:170
  170.6 10.5 %all-to-all-start.2 = ((bf16[16,128,128]{2,1,0:T(8,128)(2,1)}), bf16[16,128,128]{2,1,0:T(8,128)(2,1)S(1)}, u32[]{:S(2)}, u32[]{:S(2)}) async-start(bf16[16,128,128]{2,1,0:T(8,128)(2,1)} %attention.1), calls=%async_computation.2 | async-start | bytes 1048576 | tf_op jit(solution)/shard_map/all_to_all | solution.py:240
  181.1 1.9 collective-permute-start.33
  183.1 1.4 broadcast_select_fusion.1
  184.5 1.5 collective-permute-start.28
  186.8 1.9 collective-permute-start.38
  192.3 9.1 %collective-permute-done.33 = bf16[512,512]{1,0:T(8,128)(2,1)S(1)} collective-permute-done((bf16[512,512]{1,0:T(8,128)(2,1)}, bf16[512,512]{1,0:T(8,128)(2,1)S(1)}, u32[]{:S(2)}, u32[]{:S(2)}) %collective-permute-start.33) | collective-permute-done | bytes 524320 | tf_op jit(solution)/shard_map/ppermute | solution.py:57
  203.1 1.5 collective-permute-start.24
  204.7 8.0 %collective-permute-done.27 = bf16[512,512]{1,0:T(8,128)(2,1)} collective-permute-done((bf16[512,512]{1,0:T(8,128)(2,1)S(1)}, bf16[512,512]{1,0:T(8,128)(2,1)}, u32[]{:S(2)}, u32[]{:S(2)}) %collective-permute-start.27) | collective-permute-done | bytes 524320 | tf_op jit(solution)/shard_map/ppermute | solution.py:57
  213.2 1.5 collective-permute-start.36
  214.7 9.3 %collective-permute-done.38 = bf16[512,512]{1,0:T(8,128)(2,1)} collective-permute-done((bf16[512,512]{1,0:T(8,128)(2,1)S(1)}, bf16[512,512]{1,0:T(8,128)(2,1)}, u32[]{:S(2)}, u32[]{:S(2)}) %collective-permute-start.38) | collective-permute-done | bytes 524320 | tf_op jit(solution)/shard_map/ppermute | solution.py:57
  227.8 1.6 collective-permute-done.23
  229.6 1.9 collective-permute-start.30
  231.4 3.6 %collective-permute-done.35 = bf16[256,512]{1,0:T(8,128)(2,1)S(1)} collective-permute-done((bf16[256,512]{1,0:T(8,128)(2,1)S(1)}, bf16[256,512]{1,0:T(8,128)(2,1)S(1)}, u32[]{:S(2)}, u32[]{:S(2)}) %collective-permute-start.35) | collective-permute-done | bytes 262176 | tf_op jit(solution)/shard_map/ppermute | solution.py:60
  235.2 1.9 collective-permute-start.41
  237.0 3.6 %collective-permute-done.29 = bf16[256,512]{1,0:T(8,128)(2,1)S(1)} collective-permute-done((bf16[256,512]{1,0:T(8,128)(2,1)S(1)}, bf16[256,512]{1,0:T(8,128)(2,1)S(1)}, u32[]{:S(2)}, u32[]{:S(2)}) %collective-permute-start.29) | collective-permute-done | bytes 262176 | tf_op jit(solution)/shard_map/ppermute | solution.py:60
  240.7 4.6 %collective-permute-done.40 = bf16[256,512]{1,0:T(8,128)(2,1)S(1)} collective-permute-done((bf16[256,512]{1,0:T(8,128)(2,1)S(1)}, bf16[256,512]{1,0:T(8,128)(2,1)S(1)}, u32[]{:S(2)}, u32[]{:S(2)}) %collective-permute-start.40) | collective-permute-done | bytes 262176 | tf_op jit(solution)/shard_map/ppermute | solution.py:60
  246.7 26.5 %fusion.42 = bf16[256,2048]{1,0:T(8,128)(2,1)S(1)} fusion(bf16[256,512]{1,0:T(8,128)(2,1)} %copy-done.13, bf16[256,512]{1,0:T(8,128)(2,1)} %copy-done.12, bf16[512,512]{1,0:T(8,128)(2,1)} %collective-permute-done.39, bf16[512,512]{1,0:T(8,128)(2,1)} %collective-permute-done.38, bf16[512,512]{1,0:T(8,128)(2,1)S(1)} %get-tuple-element.18, ...), kind=kOutput, calls=%fused_computation.46 | convolution fusion | flops 2317877248 | bytes 10485760 | tf_op jit(solution)/shard_map/dot_general | solution.py:249
  273.5 1.8 collective-permute-done.42
  276.8 1.3 copy.51
  (138 shorter events, 35.9 us)
Async XLA Ops:
  0.1 1.2 copy-start
  1.3 0.7 copy-start.1
  4.2 21.6 %collective-permute-start.8 = (bf16[64,4096]{1,0:T(8,128)(2,1)}, bf16[64,4096]{1,0:T(8,128)(2,1)}, u32[]{:S(2)}, u32[]{:S(2)}) collective-permute-start(bf16[64,4096]{1,0:T(8,128)(2,1)} %get-tuple-element.16), channel_id=1, source_target_pairs={{1,0},{2,1},{3,2},{5,4},{6,5},{7,6},{9,8},{10,9},{11,10},{13,12},{... | collective-permute-start | bytes 1572872 | tf_op jit(solution)/shard_map/ppermute | solution.py:37
  5.4 21.9 %collective-permute-start.9 = (bf16[64,4096]{1,0:T(8,128)(2,1)}, bf16[64,4096]{1,0:T(8,128)(2,1)}, u32[]{:S(2)}, u32[]{:S(2)}) collective-permute-start(bf16[64,4096]{1,0:T(8,128)(2,1)} %get-tuple-element.16), channel_id=1, source_target_pairs={{0,1},{1,2},{2,3},{4,5},{5,6},{6,7},{8,9},{9,10},{10,11},{12,13},{... | collective-permute-start | bytes 1572872 | tf_op jit(solution)/shard_map/ppermute | solution.py:36
  11.8 20.7 %collective-permute-start.10 = (bf16[64,4096]{1,0:T(8,128)(2,1)}, bf16[64,4096]{1,0:T(8,128)(2,1)}, u32[]{:S(2)}, u32[]{:S(2)}) collective-permute-start(bf16[64,4096]{1,0:T(8,128)(2,1)} %get-tuple-element.15), channel_id=1, source_target_pairs={{1,0},{2,1},{3,2},{5,4},{6,5},{7,6},{9,8},{10,9},{11,10},{13,12},{... | collective-permute-start | bytes 1572872 | tf_op jit(solution)/shard_map/ppermute | solution.py:37
  13.1 20.7 %collective-permute-start.11 = (bf16[64,4096]{1,0:T(8,128)(2,1)}, bf16[64,4096]{1,0:T(8,128)(2,1)}, u32[]{:S(2)}, u32[]{:S(2)}) collective-permute-start(bf16[64,4096]{1,0:T(8,128)(2,1)} %get-tuple-element.15), channel_id=1, source_target_pairs={{0,1},{1,2},{2,3},{4,5},{5,6},{6,7},{8,9},{9,10},{10,11},{12,13},{... | collective-permute-start | bytes 1572872 | tf_op jit(solution)/shard_map/ppermute | solution.py:36
  20.2 42.7 %collective-permute-start = (bf16[3,512,512]{1,2,0:T(8,128)(2,1)S(1)}, bf16[3,512,512]{1,2,0:T(8,128)(2,1)}, u32[]{:S(2)}, u32[]{:S(2)}) collective-permute-start(bf16[3,512,512]{1,2,0:T(8,128)(2,1)S(1)} %copy.40), channel_id=1, source_target_pairs={{0,8},{8,0},{16,24},{24,16},{1,9},{9,1},{17,25},{25,17},{2,10},{10... | collective-permute-start | bytes 4718600 | tf_op jit(solution)/shard_map/ppermute | solution.py:57
  25.8 34.8 %collective-permute-start.1 = (bf16[3,512,512]{1,2,0:T(8,128)(2,1)S(1)}, bf16[3,512,512]{1,2,0:T(8,128)(2,1)S(1)}, u32[]{:S(2)}, u32[]{:S(2)}) collective-permute-start(bf16[3,512,512]{1,2,0:T(8,128)(2,1)S(1)} %copy.40), channel_id=1, source_target_pairs={{0,16},{8,24},{16,0},{24,8},{1,17},{9,25},{17,1},{25,9},{2,18},{10... | collective-permute-start | bytes 4718600 | tf_op jit(solution)/shard_map/ppermute | solution.py:58
  27.4 61.9 %collective-permute-start.4 = (bf16[3,512,512]{1,2,0:T(8,128)(2,1)S(1)}, bf16[3,512,512]{1,2,0:T(8,128)(2,1)}, u32[]{:S(2)}, u32[]{:S(2)}) collective-permute-start(bf16[3,512,512]{1,2,0:T(8,128)(2,1)S(1)} %copy.40), channel_id=1, source_target_pairs={{0,4},{4,0},{1,5},{5,1},{2,6},{6,2},{3,7},{7,3},{8,12},{12,8},{9,1... | collective-permute-start | bytes 4718600 | tf_op jit(solution)/shard_map/ppermute | solution.py:73
  32.5 15.2 %collective-permute-start.12 = (bf16[64,4096]{1,0:T(8,128)(2,1)}, bf16[64,4096]{1,0:T(8,128)(2,1)S(1)}, u32[]{:S(2)}, u32[]{:S(2)}) collective-permute-start(bf16[64,4096]{1,0:T(8,128)(2,1)} %collective-permute-done.8), channel_id=1, source_target_pairs={{2,1},{1,0},{6,5},{5,4},{10,9},{9,8},{14,13},{13,12},{18,17},{17,1... | collective-permute-start | bytes 1572872 | tf_op jit(solution)/shard_map/ppermute | solution.py:39
  33.8 15.2 %collective-permute-start.13 = (bf16[64,4096]{1,0:T(8,128)(2,1)}, bf16[64,4096]{1,0:T(8,128)(2,1)S(1)}, u32[]{:S(2)}, u32[]{:S(2)}) collective-permute-start(bf16[64,4096]{1,0:T(8,128)(2,1)} %collective-permute-done.9), channel_id=1, source_target_pairs={{1,2},{2,3},{5,6},{6,7},{9,10},{10,11},{13,14},{14,15},{17,18},{18... | collective-permute-start | bytes 1572872 | tf_op jit(solution)/shard_map/ppermute | solution.py:38
  47.7 17.5 %collective-permute-start.14 = (bf16[64,4096]{1,0:T(8,128)(2,1)}, bf16[64,4096]{1,0:T(8,128)(2,1)S(1)}, u32[]{:S(2)}, u32[]{:S(2)}) collective-permute-start(bf16[64,4096]{1,0:T(8,128)(2,1)} %collective-permute-done.10), channel_id=1, source_target_pairs={{2,1},{1,0},{6,5},{5,4},{10,9},{9,8},{14,13},{13,12},{18,17},{17,1... | collective-permute-start | bytes 1572872 | tf_op jit(solution)/shard_map/ppermute | solution.py:39
  49.0 17.9 %collective-permute-start.15 = (bf16[64,4096]{1,0:T(8,128)(2,1)}, bf16[64,4096]{1,0:T(8,128)(2,1)S(1)}, u32[]{:S(2)}, u32[]{:S(2)}) collective-permute-start(bf16[64,4096]{1,0:T(8,128)(2,1)} %collective-permute-done.11), channel_id=1, source_target_pairs={{1,2},{2,3},{5,6},{6,7},{9,10},{10,11},{13,14},{14,15},{17,18},{18... | collective-permute-start | bytes 1572872 | tf_op jit(solution)/shard_map/ppermute | solution.py:38
  60.6 38.9 %collective-permute-start.25 = (bf16[512,512]{1,0:T(8,128)(2,1)}, bf16[512,512]{1,0:T(8,128)(2,1)}, u32[]{:S(2)}, u32[]{:S(2)}) collective-permute-start(bf16[512,512]{1,0:T(8,128)(2,1)} %param.9), channel_id=1, source_target_pairs={{1,0},{2,1},{3,2},{5,4},{6,5},{7,6},{9,8},{10,9},{11,10},{13,12},{... | collective-permute-start | bytes 1572872 | tf_op jit(solution)/shard_map/ppermute | solution.py:37
  62.8 17.3 %collective-permute-start.2 = (bf16[3,256,512]{1,2,0:T(8,128)(2,1)}, bf16[3,256,512]{1,2,0:T(8,128)(2,1)}, u32[]{:S(2)}, u32[]{:S(2)}) collective-permute-start(bf16[3,256,512]{1,2,0:T(8,128)(2,1)} %slice.88), channel_id=1, source_target_pairs={{0,8},{8,0},{16,24},{24,16},{1,9},{9,1},{17,25},{25,17},{2,10},{10... | collective-permute-start | bytes 2359304 | tf_op jit(solution)/shard_map/ppermute | solution.py:60
  65.3 17.3 %collective-permute-start.3 = (bf16[3,256,512]{1,2,0:T(8,128)(2,1)}, bf16[3,256,512]{1,2,0:T(8,128)(2,1)}, u32[]{:S(2)}, u32[]{:S(2)}) collective-permute-start(bf16[3,256,512]{1,2,0:T(8,128)(2,1)} %slice.89), channel_id=1, source_target_pairs={{0,16},{8,24},{16,0},{24,8},{1,17},{9,25},{17,1},{25,9},{2,18},{10... | collective-permute-start | bytes 2359304 | tf_op jit(solution)/shard_map/ppermute | solution.py:61
  67.9 1.6 copy-start.3
  69.6 15.8 %collective-permute-start.17 = (bf16[64,4096]{1,0:T(8,128)(2,1)}, bf16[64,4096]{1,0:T(8,128)(2,1)}, u32[]{:S(2)}, u32[]{:S(2)}) collective-permute-start(bf16[64,4096]{1,0:T(8,128)(2,1)} %get-tuple-element.8), channel_id=1, source_target_pairs={{2,3},{1,0},{6,7},{5,4},{10,11},{9,8},{14,15},{13,12},{18,19},{17,... | collective-permute-start | bytes 1572872 | tf_op jit(solution)/shard_map/ppermute | solution.py:41
  80.1 17.7 %collective-permute-start.5 = (bf16[3,512,512]{1,2,0:T(8,128)(2,1)}, bf16[3,512,512]{1,2,0:T(8,128)(2,1)S(1)}, u32[]{:S(2)}, u32[]{:S(2)}) collective-permute-start(bf16[3,512,512]{1,2,0:T(8,128)(2,1)} %collective-permute-done), channel_id=1, source_target_pairs={{0,4},{4,0},{1,5},{5,1},{2,6},{6,2},{3,7},{7,3},{8,12},{12,8},{9,1... | collective-permute-start | bytes 4718600 | tf_op jit(solution)/shard_map/ppermute | solution.py:73
  82.5 23.3 %collective-permute-start.6 = (bf16[3,512,512]{1,2,0:T(8,128)(2,1)S(1)}, bf16[3,512,512]{1,2,0:T(8,128)(2,1)S(1)}, u32[]{:S(2)}, u32[]{:S(2)}) collective-permute-start(bf16[3,512,512]{1,2,0:T(8,128)(2,1)S(1)} %collective-permute-done.1), channel_id=1, source_target_pairs={{0,4},{4,0},{1,5},{5,1},{2,6},{6,2},{3,7},{7,3},{8,12},{12,8},{9,1... | collective-permute-start | bytes 4718600 | tf_op jit(solution)/shard_map/ppermute | solution.py:73
  85.4 22.2 %collective-permute-start.7 = (bf16[3,512,512]{1,2,0:T(8,128)(2,1)S(1)}, bf16[3,512,512]{1,2,0:T(8,128)(2,1)S(1)}, u32[]{:S(2)}, u32[]{:S(2)}) collective-permute-start(bf16[3,512,512]{1,2,0:T(8,128)(2,1)S(1)} %pad_maximum_fusion), channel_id=1, source_target_pairs={{0,4},{4,0},{1,5},{5,1},{2,6},{6,2},{3,7},{7,3},{8,12},{12,8},{9,1... | collective-permute-start | bytes 4718600 | tf_op jit(solution)/shard_map/ppermute | solution.py:73
  89.2 24.4 %copy-start.4 = (bf16[384,4096]{1,0:T(8,128)(2,1)S(1)}, bf16[384,4096]{1,0:T(8,128)(2,1)}, u32[]{:S(2)}) copy-start(bf16[384,4096]{1,0:T(8,128)(2,1)} %copy-done.3) | copy-start | bytes 9437188
  89.3 15.3 %collective-permute-start.26 = (bf16[512,512]{1,0:T(8,128)(2,1)}, bf16[512,512]{1,0:T(8,128)(2,1)}, u32[]{:S(2)}, u32[]{:S(2)}) collective-permute-start(bf16[512,512]{1,0:T(8,128)(2,1)} %param.9), channel_id=1, source_target_pairs={{0,1},{1,2},{2,3},{4,5},{5,6},{6,7},{8,9},{9,10},{10,11},{12,13},{... | collective-permute-start | bytes 1572872 | tf_op jit(solution)/shard_map/ppermute | solution.py:36
  97.8 88.3 %collective-permute-start.22 = (bf16[512,512]{1,0:T(8,128)(2,1)}, bf16[512,512]{1,0:T(8,128)(2,1)}, u32[]{:S(2)}, u32[]{:S(2)}) collective-permute-start(bf16[512,512]{1,0:T(8,128)(2,1)} %param.9), channel_id=1, source_target_pairs={{0,16},{8,24},{16,0},{24,8},{1,17},{9,25},{17,1},{25,9},{2,18},{10... | collective-permute-start | bytes 1572872 | tf_op jit(solution)/shard_map/ppermute | solution.py:58
  99.5 87.1 %collective-permute-start.21 = (bf16[512,512]{1,0:T(8,128)(2,1)}, bf16[512,512]{1,0:T(8,128)(2,1)}, u32[]{:S(2)}, u32[]{:S(2)}) collective-permute-start(bf16[512,512]{1,0:T(8,128)(2,1)} %param.9), channel_id=1, source_target_pairs={{0,8},{8,0},{16,24},{24,16},{1,9},{9,1},{17,25},{25,17},{2,10},{10... | collective-permute-start | bytes 1572872 | tf_op jit(solution)/shard_map/ppermute | solution.py:57
  104.6 46.1 %collective-permute-start.31 = (bf16[512,512]{1,0:T(8,128)(2,1)}, bf16[512,512]{1,0:T(8,128)(2,1)}, u32[]{:S(2)}, u32[]{:S(2)}) collective-permute-start(bf16[512,512]{1,0:T(8,128)(2,1)} %collective-permute-done.25), channel_id=1, source_target_pairs={{2,1},{1,0},{6,5},{5,4},{10,9},{9,8},{14,13},{13,12},{18,17},{17,1... | collective-permute-start | bytes 1572872 | tf_op jit(solution)/shard_map/ppermute | solution.py:39
  105.9 44.8 %collective-permute-start.32 = (bf16[512,512]{1,0:T(8,128)(2,1)}, bf16[512,512]{1,0:T(8,128)(2,1)}, u32[]{:S(2)}, u32[]{:S(2)}) collective-permute-start(bf16[512,512]{1,0:T(8,128)(2,1)} %collective-permute-done.26), channel_id=1, source_target_pairs={{1,2},{2,3},{5,6},{6,7},{9,10},{10,11},{13,14},{14,15},{17,18},{18... | collective-permute-start | bytes 1572872 | tf_op jit(solution)/shard_map/ppermute | solution.py:38
  107.6 24.2 %collective-permute-start.16 = (bf16[64,4096]{1,0:T(8,128)(2,1)}, bf16[64,4096]{1,0:T(8,128)(2,1)}, u32[]{:S(2)}, u32[]{:S(2)}) collective-permute-start(bf16[64,4096]{1,0:T(8,128)(2,1)} %get-tuple-element.10), channel_id=1, source_target_pairs={{2,3},{1,0},{6,7},{5,4},{10,11},{9,8},{14,15},{13,12},{18,19},{17,... | collective-permute-start | bytes 1572872 | tf_op jit(solution)/shard_map/ppermute | solution.py:41
  109.1 4.6 %copy-start.5 = (bf16[3,4096,512]{1,2,0:T(8,128)(2,1)}, bf16[3,4096,512]{1,2,0:T(8,128)(2,1)S(1)}, u32[]{:S(2)}) copy-start(bf16[3,4096,512]{1,2,0:T(8,128)(2,1)S(1)} %constant_dynamic-update-slice_fusion) | copy-start | bytes 37748740
  120.6 12.4 %copy-start.2 = (bf16[64,4096]{1,0:T(8,128)(2,1)S(1)}, bf16[64,4096]{1,0:T(8,128)(2,1)}, u32[]{:S(2)}) copy-start(bf16[64,4096]{1,0:T(8,128)(2,1)} %select_select_fusion.1) | copy-start | bytes 1572868
  123.0 18.2 %all-to-all-start = ((bf16[4,3,3,128,128]{4,3,2,1,0:T(8,128)(2,1)}), bf16[4,3,3,128,128]{4,3,2,1,0:T(8,128)(2,1)S(1)}, u32[]{:S(2)}, u32[]{:S(2)}) async-start(bf16[4,3,3,128,128]{4,3,2,1,0:T(8,128)(2,1)} %bitcast.20), calls=%async_computation | async-start | bytes 2359296 | tf_op jit(solution)/shard_map/all_to_all | solution.py:214
  141.1 9.5 %all-to-all-start.1 = ((bf16[4,3,1,128,128]{4,3,2,1,0:T(8,128)(2,1)}), bf16[4,3,1,128,128]{4,3,2,1,0:T(8,128)(2,1)S(1)}, u32[]{:S(2)}, u32[]{:S(2)}) async-start(bf16[4,3,1,128,128]{4,3,2,1,0:T(8,128)(2,1)} %bitcast.25), calls=%async_computation.1 | async-start | bytes 786432 | tf_op jit(solution)/shard_map/all_to_all | solution.py:214
  144.7 11.1 %collective-permute-start.18 = (bf16[4,2,3,128,128]{4,3,2,1,0:T(8,128)(2,1)S(1)}, bf16[4,2,3,128,128]{4,3,2,1,0:T(8,128)(2,1)S(1)}, u32[]{:S(2)}, u32[]{:S(2)}) collective-permute-start(bf16[4,2,3,128,128]{4,3,2,1,0:T(8,128)(2,1)S(1)} %slice.94.refs_2_), channel_id=1, source_target_pairs={{0,4},{4,0},{1,5},{5,1},{2,6},{6,2},{3,7},{7,3},{8,12},{12,8},{9,1... | collective-permute-start | bytes 2359304 | tf_op jit(solution)/shard_map/ppermute | solution.py:73
  150.6 3.3 %collective-permute-start.19 = (bf16[4,2,1,128,128]{4,3,2,1,0:T(8,128)(2,1)S(1)}, bf16[4,2,1,128,128]{4,3,2,1,0:T(8,128)(2,1)S(1)}, u32[]{:S(2)}, u32[]{:S(2)}) collective-permute-start(bf16[4,2,1,128,128]{4,3,2,1,0:T(8,128)(2,1)S(1)} %slice.95.refs_4_), channel_id=1, source_target_pairs={{0,4},{4,0},{1,5},{5,1},{2,6},{6,2},{3,7},{7,3},{8,12},{12,8},{9,1... | collective-permute-start | bytes 786440 | tf_op jit(solution)/shard_map/ppermute | solution.py:73
  152.6 30.4 %collective-permute-start.37 = (bf16[512,512]{1,0:T(8,128)(2,1)}, bf16[512,512]{1,0:T(8,128)(2,1)}, u32[]{:S(2)}, u32[]{:S(2)}) collective-permute-start(bf16[512,512]{1,0:T(8,128)(2,1)} %broadcast_select_fusion), channel_id=1, source_target_pairs={{2,3},{1,0},{6,7},{5,4},{10,11},{9,8},{14,15},{13,12},{18,19},{17,... | collective-permute-start | bytes 1572872 | tf_op jit(solution)/shard_map/ppermute | solution.py:41
  153.9 32.8 %collective-permute-start.34 = (bf16[512,512]{1,0:T(8,128)(2,1)}, bf16[512,512]{1,0:T(8,128)(2,1)}, u32[]{:S(2)}, u32[]{:S(2)}) collective-permute-start(bf16[512,512]{1,0:T(8,128)(2,1)} %broadcast_select_fusion), channel_id=1, source_target_pairs={{0,16},{8,24},{16,0},{24,8},{1,17},{9,25},{17,1},{25,9},{2,18},{10... | collective-permute-start | bytes 1572872 | tf_op jit(solution)/shard_map/ppermute | solution.py:58
  170.6 31.5 %all-to-all-start.2 = ((bf16[16,128,128]{2,1,0:T(8,128)(2,1)}), bf16[16,128,128]{2,1,0:T(8,128)(2,1)S(1)}, u32[]{:S(2)}, u32[]{:S(2)}) async-start(bf16[16,128,128]{2,1,0:T(8,128)(2,1)} %attention.1), calls=%async_computation.2 | async-start | bytes 1048576 | tf_op jit(solution)/shard_map/all_to_all | solution.py:240
  181.1 20.2 %collective-permute-start.33 = (bf16[512,512]{1,0:T(8,128)(2,1)}, bf16[512,512]{1,0:T(8,128)(2,1)S(1)}, u32[]{:S(2)}, u32[]{:S(2)}) collective-permute-start(bf16[512,512]{1,0:T(8,128)(2,1)} %broadcast_select_fusion), channel_id=1, source_target_pairs={{0,8},{8,0},{16,24},{24,16},{1,9},{9,1},{17,25},{25,17},{2,10},{10... | collective-permute-start | bytes 1572872 | tf_op jit(solution)/shard_map/ppermute | solution.py:57
  184.5 18.6 %collective-permute-start.28 = (bf16[512,512]{1,0:T(8,128)(2,1)S(1)}, bf16[512,512]{1,0:T(8,128)(2,1)}, u32[]{:S(2)}, u32[]{:S(2)}) collective-permute-start(bf16[512,512]{1,0:T(8,128)(2,1)S(1)} %get-tuple-element.17), channel_id=1, source_target_pairs={{0,16},{8,24},{16,0},{24,8},{1,17},{9,25},{17,1},{25,9},{2,18},{10... | collective-permute-start | bytes 1572872 | tf_op jit(solution)/shard_map/ppermute | solution.py:58
  186.0 26.6 %collective-permute-start.27 = (bf16[512,512]{1,0:T(8,128)(2,1)S(1)}, bf16[512,512]{1,0:T(8,128)(2,1)}, u32[]{:S(2)}, u32[]{:S(2)}) collective-permute-start(bf16[512,512]{1,0:T(8,128)(2,1)S(1)} %get-tuple-element.17), channel_id=1, source_target_pairs={{0,8},{8,0},{16,24},{24,16},{1,9},{9,1},{17,25},{25,17},{2,10},{10... | collective-permute-start | bytes 1572872 | tf_op jit(solution)/shard_map/ppermute | solution.py:57
  186.6 26.5 %collective-permute-start.39 = (bf16[512,512]{1,0:T(8,128)(2,1)S(1)}, bf16[512,512]{1,0:T(8,128)(2,1)}, u32[]{:S(2)}, u32[]{:S(2)}) collective-permute-start(bf16[512,512]{1,0:T(8,128)(2,1)S(1)} %get-tuple-element.18), channel_id=1, source_target_pairs={{0,16},{8,24},{16,0},{24,8},{1,17},{9,25},{17,1},{25,9},{2,18},{10... | collective-permute-start | bytes 1572872 | tf_op jit(solution)/shard_map/ppermute | solution.py:58
  186.8 37.1 %collective-permute-start.38 = (bf16[512,512]{1,0:T(8,128)(2,1)S(1)}, bf16[512,512]{1,0:T(8,128)(2,1)}, u32[]{:S(2)}, u32[]{:S(2)}) collective-permute-start(bf16[512,512]{1,0:T(8,128)(2,1)S(1)} %get-tuple-element.18), channel_id=1, source_target_pairs={{0,8},{8,0},{16,24},{24,16},{1,9},{9,1},{17,25},{25,17},{2,10},{10... | collective-permute-start | bytes 1572872 | tf_op jit(solution)/shard_map/ppermute | solution.py:57
  201.4 0.8 copy-start.6
  201.4 28.1 %collective-permute-start.23 = (bf16[256,512]{1,0:T(8,128)(2,1)S(1)}, bf16[256,512]{1,0:T(8,128)(2,1)S(1)}, u32[]{:S(2)}, u32[]{:S(2)}) collective-permute-start(bf16[256,512]{1,0:T(8,128)(2,1)S(1)} %slice.96), channel_id=1, source_target_pairs={{0,8},{8,0},{16,24},{24,16},{1,9},{9,1},{17,25},{25,17},{2,10},{10... | collective-permute-start | bytes 786440 | tf_op jit(solution)/shard_map/ppermute | solution.py:60
  203.1 26.4 %collective-permute-start.24 = (bf16[256,512]{1,0:T(8,128)(2,1)S(1)}, bf16[256,512]{1,0:T(8,128)(2,1)S(1)}, u32[]{:S(2)}, u32[]{:S(2)}) collective-permute-start(bf16[256,512]{1,0:T(8,128)(2,1)S(1)} %slice.97), channel_id=1, source_target_pairs={{0,16},{8,24},{16,0},{24,8},{1,17},{9,25},{17,1},{25,9},{2,18},{10... | collective-permute-start | bytes 786440 | tf_op jit(solution)/shard_map/ppermute | solution.py:61
  212.7 22.4 %collective-permute-start.35 = (bf16[256,512]{1,0:T(8,128)(2,1)S(1)}, bf16[256,512]{1,0:T(8,128)(2,1)S(1)}, u32[]{:S(2)}, u32[]{:S(2)}) collective-permute-start(bf16[256,512]{1,0:T(8,128)(2,1)S(1)} %slice.100), channel_id=1, source_target_pairs={{0,8},{8,0},{16,24},{24,16},{1,9},{9,1},{17,25},{25,17},{2,10},{10... | collective-permute-start | bytes 786440 | tf_op jit(solution)/shard_map/ppermute | solution.py:60
  213.2 22.0 %collective-permute-start.36 = (bf16[256,512]{1,0:T(8,128)(2,1)S(1)}, bf16[256,512]{1,0:T(8,128)(2,1)S(1)}, u32[]{:S(2)}, u32[]{:S(2)}) collective-permute-start(bf16[256,512]{1,0:T(8,128)(2,1)S(1)} %slice.101), channel_id=1, source_target_pairs={{0,16},{8,24},{16,0},{24,8},{1,17},{9,25},{17,1},{25,9},{2,18},{10... | collective-permute-start | bytes 786440 | tf_op jit(solution)/shard_map/ppermute | solution.py:61
  223.9 22.7 %collective-permute-start.20 = (bf16[128,2048]{0,1:T(8,128)(2,1)S(1)}, bf16[128,2048]{0,1:T(8,128)(2,1)S(1)}, u32[]{:S(2)}, u32[]{:S(2)}) collective-permute-start(bf16[128,2048]{0,1:T(8,128)(2,1)S(1)} %bitcast.93), channel_id=1, source_target_pairs={{0,4},{4,0},{1,5},{5,1},{2,6},{6,2},{3,7},{7,3},{8,12},{12,8},{9,1... | collective-permute-start | bytes 1572872 | tf_op jit(solution)/shard_map/ppermute | solution.py:73
  229.4 11.2 %collective-permute-start.29 = (bf16[256,512]{1,0:T(8,128)(2,1)S(1)}, bf16[256,512]{1,0:T(8,128)(2,1)S(1)}, u32[]{:S(2)}, u32[]{:S(2)}) collective-permute-start(bf16[256,512]{1,0:T(8,128)(2,1)S(1)} %slice.98), channel_id=1, source_target_pairs={{0,8},{8,0},{16,24},{24,16},{1,9},{9,1},{17,25},{25,17},{2,10},{10... | collective-permute-start | bytes 786440 | tf_op jit(solution)/shard_map/ppermute | solution.py:60
  229.6 15.7 %copy-start.7 = (bf16[256,512]{1,0:T(8,128)(2,1)}, bf16[256,512]{1,0:T(8,128)(2,1)S(1)}, u32[]{:S(2)}) copy-start(bf16[256,512]{1,0:T(8,128)(2,1)S(1)} %collective-permute-done.24) | copy-start | bytes 786436
  229.6 11.1 %collective-permute-start.30 = (bf16[256,512]{1,0:T(8,128)(2,1)S(1)}, bf16[256,512]{1,0:T(8,128)(2,1)S(1)}, u32[]{:S(2)}, u32[]{:S(2)}) collective-permute-start(bf16[256,512]{1,0:T(8,128)(2,1)S(1)} %slice.99), channel_id=1, source_target_pairs={{0,16},{8,24},{16,0},{24,8},{1,17},{9,25},{17,1},{25,9},{2,18},{10... | collective-permute-start | bytes 786440 | tf_op jit(solution)/shard_map/ppermute | solution.py:61
  235.1 10.2 %copy-start.8 = (bf16[256,512]{1,0:T(8,128)(2,1)}, bf16[256,512]{1,0:T(8,128)(2,1)S(1)}, u32[]{:S(2)}) copy-start(bf16[256,512]{1,0:T(8,128)(2,1)S(1)} %collective-permute-done.35) | copy-start | bytes 786436
  235.1 10.2 %collective-permute-start.40 = (bf16[256,512]{1,0:T(8,128)(2,1)S(1)}, bf16[256,512]{1,0:T(8,128)(2,1)S(1)}, u32[]{:S(2)}, u32[]{:S(2)}) collective-permute-start(bf16[256,512]{1,0:T(8,128)(2,1)S(1)} %slice.102), channel_id=1, source_target_pairs={{0,8},{8,0},{16,24},{24,16},{1,9},{9,1},{17,25},{25,17},{2,10},{10... | collective-permute-start | bytes 786440 | tf_op jit(solution)/shard_map/ppermute | solution.py:60
  235.2 10.1 %copy-start.9 = (bf16[256,512]{1,0:T(8,128)(2,1)}, bf16[256,512]{1,0:T(8,128)(2,1)S(1)}, u32[]{:S(2)}) copy-start(bf16[256,512]{1,0:T(8,128)(2,1)S(1)} %collective-permute-done.36) | copy-start | bytes 786436
  235.2 10.1 %collective-permute-start.41 = (bf16[256,512]{1,0:T(8,128)(2,1)S(1)}, bf16[256,512]{1,0:T(8,128)(2,1)S(1)}, u32[]{:S(2)}, u32[]{:S(2)}) collective-permute-start(bf16[256,512]{1,0:T(8,128)(2,1)S(1)} %slice.103), channel_id=1, source_target_pairs={{0,16},{8,24},{16,0},{24,8},{1,17},{9,25},{17,1},{25,9},{2,18},{10... | collective-permute-start | bytes 786440 | tf_op jit(solution)/shard_map/ppermute | solution.py:61
  240.7 4.6 %copy-start.10 = (bf16[256,512]{1,0:T(8,128)(2,1)}, bf16[256,512]{1,0:T(8,128)(2,1)S(1)}, u32[]{:S(2)}) copy-start(bf16[256,512]{1,0:T(8,128)(2,1)S(1)} %collective-permute-done.29) | copy-start | bytes 786436
  240.7 4.6 %copy-start.11 = (bf16[256,512]{1,0:T(8,128)(2,1)}, bf16[256,512]{1,0:T(8,128)(2,1)S(1)}, u32[]{:S(2)}) copy-start(bf16[256,512]{1,0:T(8,128)(2,1)S(1)} %collective-permute-done.30) | copy-start | bytes 786436
  245.2 0.7 copy-start.12
  245.9 0.7 copy-start.13
  273.4 2.0 collective-permute-start.42

commit v2 on v1

v2 whole, which is shorter than its diff:
```python
import functools
import math

import jax
import jax.numpy as jnp
import numpy as np
from jax import lax
from jax.experimental import pallas as pl
from jax.experimental.pallas import tpu as pltpu
from jax.sharding import Mesh
from jax.sharding import PartitionSpec as P

HEAD_DIM = 128
BLK = 128
EPSILON = 1e-05
MASKED = -1e30
F32 = jnp.float32
BF16 = jnp.bfloat16


def xor_pairs(size, bit):
    return [(i, i ^ bit) for i in range(size)]


def tie(value, *others):
    return lax.optimization_barrier((value, *others))[0]


def line_order(size):
    if size != 4:
        return [list(range(size))] * size
    return [[0, 1, 2, 3], [1, 0, 2, 3], [2, 3, 1, 0], [3, 2, 1, 0]]


def plane_order(size, at):
    return [at ^ r if size == 4 else jnp.int32(r) for r in range(size)]


def gathered(part, axis, size):
    whole = lax.all_gather(part, axis, axis=0)
    return [whole[i] for i in range(size)]


def pair_gather(part, size):
    if size != 2:
        return gathered(part, "rep", size)
    return [part, lax.ppermute(part, "rep", xor_pairs(2, 1))]


def hop(part, bit):
    return lax.ppermute(part, "head", xor_pairs(4, bit))


def normalize_kernel(order, tokens, gain, out):
    features = tokens[...].astype(F32)
    mean_square = jnp.mean(features * features, axis=-1, keepdims=True)
    scale = lax.rsqrt(mean_square + EPSILON)
    count = order.shape[0]
    width = tokens.shape[1] // count
    for r in range(count):
        source = pl.ds(pl.multiple_of(order[r] * width, width), width)
        out[:, r * width : (r + 1) * width] = (
            tokens[:, source].astype(F32) * scale * gain[:, source]
        ).astype(BF16)


def normalize(tokens, norm_gain, order):
    vmem = pl.BlockSpec(memory_space=pltpu.VMEM)
    return pl.pallas_call(
        normalize_kernel,
        out_shape=jax.ShapeDtypeStruct(tokens.shape, BF16),
        in_specs=[pl.BlockSpec(memory_space=pltpu.SMEM), vmem, vmem],
        out_specs=vmem,
        compiler_params=pltpu.CompilerParams(vmem_limit_bytes=16 << 20),
        name="normalize",
    )(order, tokens, norm_gain.reshape(1, -1))


def attention_kernel(
    sizes, places, biases, copies, targets, *refs
):
    groups, reps, heads, spans, slots = sizes
    total = sum(groups)
    parts = refs[: len(groups) * reps]
    out, held, asked, scores, sems = refs[len(groups) * reps :]
    waits = []
    at = 0
    for g, size in enumerate(groups):
        for r in range(reps):
            ref = parts[g * reps + r]
            to = held.at[r, :, :, at : at + size]
            waits.append(pltpu.make_async_copy(ref.at[:, 1:], to, sems.at[len(waits)]))
        own = parts[g * reps]
        waits.append(pltpu.make_async_copy(own.at[:, 0], asked.at[:, at : at + size], sems.at[len(waits)]))
        at += size
    for copy in waits:
        copy.start()
    for copy in waits:
        copy.wait()
    flat = held.reshape(reps * heads * 2 * total, BLK, HEAD_DIM)
    wanted = asked.reshape(heads * total, BLK, HEAD_DIM)
    blocks = heads * total
    factor = HEAD_DIM ** (-0.5) * math.log2(math.e)
    rows = lax.broadcasted_iota(jnp.int32, (BLK, BLK), 0)
    columns = lax.broadcasted_iota(jnp.int32, (BLK, BLK), 1)

    def score(j, place):
        keys = jnp.concatenate([flat[places[j, n]] for n in range(slots)], axis=0)
        scores[place] = lax.dot_general(wanted[j], keys, (((1,), (1,)), ((), ())), preferred_element_type=F32)

    def blend(j, place):
        parts = []
        for n in range(slots):
            part = scores[place, :, n * BLK : (n + 1) * BLK] * factor
            parts.append(jnp.where(columns <= rows, part, MASKED) if n == 0 else part + biases[j, n])
        top = parts[0]
        for n in range(1, slots):
            top = jnp.maximum(top, parts[n])
        top = jnp.max(top, axis=1, keepdims=True)
        weights = [jnp.exp2(part - top) for part in parts]
        weights[0] = weights[0] * copies[j]
        below = weights[0]
        for n in range(1, slots):
            below = below + weights[n]
        below = jnp.sum(below, axis=1, keepdims=True)
        values = jnp.concatenate([flat[places[j, n] + total] for n in range(slots)], axis=0)
        blended = jnp.dot(
            jnp.concatenate([w.astype(BF16) for w in weights], axis=1), values, preferred_element_type=F32
        )
        out[targets[j]] = (blended / below).astype(BF16)

    score(0, 0)

    def two_blocks(t, carry):
        for place in range(2):
            j = 2 * t + place
            score(jnp.minimum(j + 1, blocks - 1), 1 - place)
            blend(j, place)
        return carry

    lax.fori_loop(0, blocks // 2, two_blocks, 0)


def attention(parts, places, biases, copies, targets, sizes):
    groups, reps, heads, spans, slots = sizes
    total = sum(groups)
    smem = pl.BlockSpec(memory_space=pltpu.SMEM)
    hbm = pl.BlockSpec(memory_space=pl.ANY)
    blocks = heads * total
    return pl.pallas_call(
        functools.partial(attention_kernel, sizes),
        out_shape=jax.ShapeDtypeStruct((blocks, BLK, HEAD_DIM), BF16),
        in_specs=[smem] * 4 + [hbm] * len(parts),
        out_specs=pl.BlockSpec(memory_space=pltpu.VMEM),
        scratch_shapes=[
            pltpu.VMEM((reps, heads, 2, total, BLK, HEAD_DIM), BF16),
            pltpu.VMEM((heads, total, BLK, HEAD_DIM), BF16),
            pltpu.VMEM((2, BLK, slots * BLK), F32),
            pltpu.SemaphoreType.DMA((len(groups) * (1 + reps),)),
        ],
        compiler_params=pltpu.CompilerParams(vmem_limit_bytes=40 << 20),
        cost_estimate=pl.CostEstimate(
            flops=4 * blocks * slots * BLK * BLK * HEAD_DIM,
            bytes_accessed=8 * blocks * BLK * HEAD_DIM * reps,
            transcendentals=blocks * slots * BLK * BLK,
        ),
        name="attention",
    )(places, biases, copies, targets, *parts)


def project_kernel(spots, heads, lines, reps, planes, order, *refs):
    landed, pieces = refs[:reps], refs[reps : reps + len(spots)]
    out, weights, rows, sems = refs[reps + len(spots) :]
    copies = [
        pltpu.make_async_copy(ref, weights.at[s, r, pl.ds(first, ref.shape[0])], sems.at[i])
        for i, ((s, r, first), ref) in enumerate(zip(spots, pieces))
    ]
    for copy in copies:
        copy.start()
    depth = heads * HEAD_DIM
    for k in range(reps):
        for s in range(lines):
            for h in range(heads):
                at = s * depth + h * HEAD_DIM
                rows[k * BLK : (k + 1) * BLK, at : at + HEAD_DIM] = landed[k][h * lines + order[s]]
    width = weights.shape[3]
    for r in range(heads):
        total = None
        for s in range(lines):
            for copy, spot in zip(copies, spots):
                if spot[:2] == (s, r):
                    copy.wait()
            term = jnp.dot(rows[:, s * depth : (s + 1) * depth], weights[s, r], preferred_element_type=F32)
            total = term if total is None else total + term
        place = pl.ds(pl.multiple_of(planes[r] * width, width), width)
        for k in range(reps):
            out[k, :, place] = total[k * BLK : (k + 1) * BLK].astype(BF16)


def project(planes, order, landed, pieces, heads, lines):
    reps = len(landed)
    spots = [piece[:3] for piece in pieces]
    arrays = [piece[3] for piece in pieces]
    width = arrays[0].shape[1]
    depth = heads * HEAD_DIM
    smem = pl.BlockSpec(memory_space=pltpu.SMEM)
    vmem = pl.BlockSpec(memory_space=pltpu.VMEM)
    hbm = pl.BlockSpec(memory_space=pl.ANY)
    return pl.pallas_call(
        functools.partial(project_kernel, spots, heads, lines, reps),
        out_shape=jax.ShapeDtypeStruct((reps, BLK, heads * width), BF16),
        in_specs=[smem] * 2 + [vmem] * reps + [hbm] * len(arrays),
        out_specs=vmem,
        scratch_shapes=[
            pltpu.VMEM((lines, heads, depth, width), BF16),
            pltpu.VMEM((reps * BLK, lines * depth), BF16),
            pltpu.SemaphoreType.DMA((len(arrays),)),
        ],
        compiler_params=pltpu.CompilerParams(vmem_limit_bytes=58 << 20),
        name="project",
    )(planes, order, *landed, *arrays)


def enter_kernel(heads, count, *refs):
    chunks = refs[:count]
    pieces = refs[count:-4]
    out, weights, rows, sems = refs[-4:]
    copies = []
    for c in range(3):
        at = 0
        for piece in pieces:
            target = weights.at[c, pl.ds(at, piece.shape[1])]
            copies.append(pltpu.make_async_copy(piece.at[c], target, sems.at[len(copies)]))
            at += piece.shape[1]
    for copy in copies:
        copy.start()
    for n, chunk in enumerate(chunks):
        rows[n * BLK : (n + 1) * BLK] = chunk[...]
    for c in range(3):
        for copy in copies[c * len(pieces) : (c + 1) * len(pieces)]:
            copy.wait()
        total = jnp.dot(rows[...], weights[c], preferred_element_type=F32).astype(BF16)
        for n in range(count):
            for h in range(heads):
                out[h, c, n] = total[n * BLK : (n + 1) * BLK, h * HEAD_DIM : (h + 1) * HEAD_DIM]


def enter(chunks, pieces, heads):
    features = chunks[0].shape[1]
    vmem = pl.BlockSpec(memory_space=pltpu.VMEM)
    return pl.pallas_call(
        functools.partial(enter_kernel, heads, len(chunks)),
        out_shape=jax.ShapeDtypeStruct((heads, 3, len(chunks), BLK, HEAD_DIM), BF16),
        in_specs=[vmem] * len(chunks) + [pl.BlockSpec(memory_space=pl.ANY)] * len(pieces),
        out_specs=vmem,
        scratch_shapes=[
            pltpu.VMEM((3, features, heads * HEAD_DIM), BF16),
            pltpu.VMEM((len(chunks) * BLK, features), BF16),
            pltpu.SemaphoreType.DMA((3 * len(pieces),)),
        ],
        compiler_params=pltpu.CompilerParams(vmem_limit_bytes=58 << 20),
        cost_estimate=pl.CostEstimate(flops=1, bytes_accessed=1, transcendentals=0),
        name="enter",
    )(*chunks, *pieces)


def leave_kernel(heads, lines, count, order, *refs):
    landed, pieces = refs[:2], refs[2 : 2 + count]
    outs = refs[2 + count : 4 + count]
    weights, rows, sems = refs[4 + count :]
    depth = heads * HEAD_DIM
    width = weights.shape[3]
    copies = []
    for side in range(2):
        for i, (core, first) in enumerate(((0, side), (1, side), (0, 2 + side), (1, 2 + side))):
            at = 0
            for piece in pieces[core::2]:
                source = piece.at[:, pl.ds(first * width, width)]
                target = weights.at[side, i, pl.ds(at, piece.shape[0])]
                copies.append(pltpu.make_async_copy(source, target, sems.at[len(copies)]))
                at += piece.shape[0]
    for copy in copies:
        copy.start()
    for side in range(2):
        for s in range(lines):
            for h in range(heads):
                at = s * depth + h * HEAD_DIM
                rows[side, :, at : at + HEAD_DIM] = landed[side][h * lines + order[s]]
    for side in range(2):
        for i in range(4):
            for copy in copies[(side * 4 + i) * (count // 2) : (side * 4 + i + 1) * (count // 2)]:
                copy.wait()
            outs[side][:, i * width : (i + 1) * width] = jnp.dot(
                rows[side], weights[side, i], preferred_element_type=F32
            ).astype(BF16)


def leave(order, landed_x, landed_y, shared, heads, lines):
    depth = sum(piece.shape[0] for piece in shared[::2])
    width = shared[0].shape[1] // 4
    smem = pl.BlockSpec(memory_space=pltpu.SMEM)
    vmem = pl.BlockSpec(memory_space=pltpu.VMEM)
    hbm = pl.BlockSpec(memory_space=pl.ANY)
    out = jax.ShapeDtypeStruct((BLK, 4 * width), BF16)
    return pl.pallas_call(
        functools.partial(leave_kernel, heads, lines, len(shared)),
        out_shape=(out, out),
        in_specs=[smem] + [vmem] * 2 + [hbm] * len(shared),
        out_specs=(vmem, vmem),
        scratch_shapes=[
            pltpu.VMEM((2, 4, depth, width), BF16),
            pltpu.VMEM((2, BLK, depth), BF16),
            pltpu.SemaphoreType.DMA((4 * len(shared),)),
        ],
        compiler_params=pltpu.CompilerParams(vmem_limit_bytes=58 << 20),
        cost_estimate=pl.CostEstimate(
            flops=16 * BLK * depth * width, bytes_accessed=16 * depth * width, transcendentals=0
        ),
        name="leave",
    )(order, landed_x, landed_y, *shared)


def place_kernel(shifts, own_x, own_y, from_x, from_y, out):
    width = own_x.shape[1] // 4
    for ref, chips, half in ((own_x, (0, 2), 0), (own_y, (0, 1), 1), (from_x, (1, 3), 0), (from_y, (2, 3), 1)):
        for i, chip in enumerate(chips):
            for core in range(2):
                spot = ((shifts[0] ^ chip) * 2 + (shifts[1] ^ core)) * 2 + half
                at = (2 * i + core) * width
                out[:, pl.ds(pl.multiple_of(spot * width, width), width)] = ref[:, at : at + width]


def place(shifts, *parts):
    smem = pl.BlockSpec(memory_space=pltpu.SMEM)
    vmem = pl.BlockSpec(memory_space=pltpu.VMEM)
    return pl.pallas_call(
        place_kernel,
        out_shape=jax.ShapeDtypeStruct((BLK, 4 * parts[0].shape[1]), BF16),
        in_specs=[smem] + [vmem] * 4,
        out_specs=vmem,
        compiler_params=pltpu.CompilerParams(vmem_limit_bytes=16 << 20),
        name="place",
    )(shifts, *parts)


def by_head(projected):
    return lax.all_to_all(projected, "head", 0, 0, tiled=True)


def tables(heads, reps, lines, rep_at, order, layout):
    blocks = heads * reps * lines
    names = jnp.arange(blocks, dtype=jnp.int32)
    slot_of = jnp.argmax(order[None, :] == jnp.arange(lines, dtype=jnp.int32)[:, None], axis=1).astype(jnp.int32)
    span_of = names // lines
    rep_of, head_of = span_of % reps, span_of // reps
    side_of = rep_of ^ rep_at if reps == 2 else rep_of
    place_of = ((side_of * heads + head_of) * 2) * lines + slot_of[names % lines]
    own = ((jnp.arange(heads, dtype=jnp.int32)[:, None] * reps + rep_at) * lines + order[None, :]).reshape(-1)
    others = jnp.concatenate([(own - 1)[:, None], layout[own]], axis=1)
    index = jnp.concatenate([own[:, None], others], axis=1)
    places = place_of[jnp.maximum(index, 0)]
    off = (others < 0) | (others == own[:, None])
    biases = jnp.concatenate([jnp.zeros((own.shape[0], 1), F32), jnp.where(off, MASKED, 0.0)], axis=1)
    copies = 1.0 + jnp.sum(others == own[:, None], axis=1).astype(F32)
    targets = (jnp.arange(heads, dtype=jnp.int32)[:, None] * lines + order[None, :]).reshape(-1)
    return places, biases, copies, targets


def shards(heads, reps, lines, tokens, norm_gain, qkv_weight, out_weight, layout):
    head_at, rep_at, line_at = (lax.axis_index(a) for a in ("head", "rep", "line"))
    assert tokens.shape[0] == BLK
    order = jnp.asarray(line_order(lines), jnp.int32)[line_at]
    planes = plane_order(heads, head_at)
    fast = (heads, reps, lines) == (4, 2, 4)
    feature_order = jnp.stack(
        [(head_at ^ h) * reps + (rep_at ^ r) if fast else jnp.int32(h * reps + r) for r in range(reps) for h in range(heads)]
    ).astype(jnp.int32)
    planes = jnp.stack(planes).astype(jnp.int32)
    if fast:
        w_one, w_two = hop(qkv_weight, 1), hop(qkv_weight, 2)
    normed = normalize(tokens, norm_gain, feature_order)
    table = tables(heads, reps, lines, rep_at, order, layout)
    slots = table[0].shape[1]

    def attend(parts, groups):
        attended = attention(parts, *table, (groups, reps, heads, heads * reps, slots))
        return lax.all_to_all(attended, ("head", "line"), 0, 0, tiled=True)

    if not fast:
        weight = lax.all_gather(qkv_weight, ("head", "rep"), axis=1, tiled=True)
        rows = gathered(normed, "line", lines)
        landed = attend(pair_gather(by_head(enter(rows, [weight], heads)), reps), (lines,))
        out_pieces = [
            (s, h, 0, piece)
            for s, part in enumerate(gathered(out_weight, "line", lines))
            for h, piece in enumerate(gathered(part, "head", heads))
        ]
        product = project(planes, order, pair_gather(landed, reps), out_pieces, heads, lines)
        columns = lax.all_to_all(product, "rep", 0, 0).reshape(reps, BLK, heads, -1)
        return columns.transpose(1, 2, 0, 3).reshape(BLK, -1)

    barrier = lax.optimization_barrier
    inside = (line_at == 1) | (line_at == 2)
    middle, outward, inward = [(1, 2), (2, 1)], [(1, 0), (2, 3)], [(0, 1), (3, 2)]

    def along(part, pairs):
        return lax.ppermute(part, "line", pairs)

    def pair(part):
        return lax.ppermute(part, "rep", xor_pairs(2, 1))

    def share(part):
        width = part.shape[1] // 2
        return hop(part[:, :width], 2), hop(part[:, width:], 1)

    def joined(part, halves):
        return jnp.concatenate([part, *halves], axis=1)

    near, across = along(normed, xor_pairs(4, 1)), along(normed, middle)
    w_pairs = [pair(qkv_weight)]
    near, across, w_pairs[0], *table = barrier((near, across, w_pairs[0], *table))
    crossed, second = along(near, middle), along(across, outward)
    o_in = along(tie(out_weight, near), inward)
    half = w_one.shape[1] // 2
    onward = (w_two[:, :half], w_one[:, half:])
    crossed, second, o_in, w_one, w_two, *onward = barrier((crossed, second, o_in, w_one, w_two, *onward))
    third = along(crossed, outward)
    w_first, w_other = hop(onward[0], 1), hop(onward[1], 2)
    w_pairs += [pair(w) for w in (w_one, w_two)]
    chunk = jnp.where(inside, across, second)
    w_first, w_other, w_pairs[1], w_pairs[2], chunk = barrier((w_first, w_other, w_pairs[1], w_pairs[2], chunk))
    w_pairs += [pair(w) for w in (w_first, w_other)]
    o_own = tie(out_weight, w_first)
    o_out = [along(o_own, outward)]
    o_across = along(o_own, middle)
    first_halves = share(o_own)
    weights = [qkv_weight, w_one, w_two, w_first, w_other, *w_pairs]
    early = enter([normed, near, chunk], weights, heads)
    early, third, o_across, *first_halves = barrier((early, third, o_across, *first_halves))
    o_crossed = along(o_in, middle)
    o_out.append(along(o_across, outward))
    early_heads = by_head(early)
    late = enter([jnp.where(inside, crossed, third)], weights, heads)
    early_heads, late, o_out[0], o_crossed = barrier((early_heads, late, o_out[0], o_crossed))
    near_slot = jnp.where(inside, o_in, o_out[0])
    near_halves = share(near_slot)
    o_out.append(along(o_crossed, outward))
    early_parts = pair_gather(early_heads, reps)
    late_parts = pair_gather(by_head(late), reps)
    early_parts[1], late_parts[1], o_out[1], *near_halves = barrier(
        (early_parts[1], late_parts[1], o_out[1], *near_halves)
    )
    shared = [joined(o_own, first_halves), joined(near_slot, near_halves)]
    attended = attention(early_parts + late_parts, *table, ((lines - 1, 1), reps, heads, heads * reps, slots))
    second_slot = jnp.where(inside, o_across, o_out[1])
    second_halves = share(second_slot)
    attended, o_out[2], *second_halves = barrier((attended, o_out[2], *second_halves))
    landed = lax.all_to_all(attended, ("head", "line"), 0, 0, tiled=True)
    shared.append(joined(second_slot, second_halves))
    third_slot = jnp.where(inside, o_crossed, o_out[2])
    others = [pair(batch) for batch in shared]
    landed, *others = barrier((landed, *others))
    landed_x, landed_y = hop(landed, 1), hop(landed, 2)
    third_halves = share(third_slot)
    shared.append(joined(third_slot, third_halves))
    others.append(pair(shared[3]))
    landed, landed_x, landed_y, others[3] = barrier((landed, landed_x, landed_y, others[3]))
    shared = [batch for both in zip(shared, others) for batch in both]
    shifts = jnp.stack([head_at, rep_at]).astype(jnp.int32)
    to_x, to_y = leave(order, landed_x, landed_y, shared, heads, lines)
    own_x, own_y = leave(order, landed, landed, shared, heads, lines)
    return place(shifts, own_x, own_y, hop(to_x, 1), hop(to_y, 2))


def solution(mesh):
    spans, lines = mesh.shape["ctx"], mesh.shape["fsdp"]

    def run(tokens, norm_gain, qkv_weight, out_weight, layout):
        heads = qkv_weight.shape[2] // lines // HEAD_DIM
        reps = spans // heads
        fine = Mesh(mesh.devices.reshape(heads, reps, lines), ("head", "rep", "line"))
        ctx = ("head", "rep")
        rows = P(("head", "rep", "line"), None)
        placed = (rows, P(), P(None, ctx, "line"), P("line", ctx), P())
        return jax.shard_map(
            functools.partial(shards, heads, reps, lines),
            mesh=fine,
            in_specs=placed,
            out_specs=rows,
            check_vma=False,
        )(tokens, norm_gain, qkv_weight, out_weight, layout)

    return run
```

time: 280 us -> 217 us (0.78)
  matrix products: 40 us -> 0 us
  Pallas kernels: 15.9 us -> 45.6 us
  local copies, waits for them, and re-layouts: 42.4 us -> 20.7 us
  starting transfers between devices: 72.1 us -> 56.9 us
  waiting for transfers between devices: 90 us -> 80.2 us
  other arithmetic: 17 us -> 12 us
    dot_general x3 -> x0, matrix products: 40 us -> none  [the longest x1 26.5 us: shards(): jnp.dot(everyone, projection, preferred_element_type=F32).astype(BF16)]
    pallas_call x0 -> x5, Pallas kernels: none -> 33.5 us  [the longest x2 18.2 us: enter(): pl.pallas_call(functools.partial(enter_kernel, heads, len(chunks)), out_s...]
    ppermute x43 -> x38, waiting for transfers between devices: 88.7 us -> 68.1 us  [the longest x16 38.8 us: hop(): return lax.ppermute(part, 'head', xor_pairs(4, bit))]
    unnamed x39 -> x53, local copies, waits for them, and re-layouts: 19.3 us -> 9.52 us
    ppermute x43 -> x38, starting transfers between devices: 54.5 us -> 45 us  [the longest x11 23.9 us: along(): return lax.ppermute(part, 'line', pairs)]
    all_to_all x2, waiting for transfers between devices: 1.34 us -> 9.19 us  [by_head(): return lax.all_to_all(projected, 'head', 0, 0, tiled=True)]
    slice x14 -> x6, local copies, waits for them, and re-layouts: 11 us -> 4.47 us  [the longest x2 3.3 us: shards(): onward = (w_two[:, :half], w_one[:, half:])]
    all_to_all x1, starting transfers between devices: 10.5 us -> 4.91 us  [shards(): landed = lax.all_to_all(attended, ('head', 'line'), 0, 0, tiled=True)]
  transfers between devices with their start and end apart: 46 -> 41, of which waited for: 19 -> 16; matrix products, arithmetic and copies ran while one was open for 21% -> 12% of each run, Pallas kernels for 5% -> 17%
where the time goes in v2:
time: 217 us; the launch traced here: 216 us
  waiting for transfers between devices  80.2 us (37%)
  starting transfers between devices  56.9 us (26%)
  Pallas kernels  45.6 us (21%)
  local copies, waits for them, and re-layouts  20.7 us (10%)
  other arithmetic  12 us (6%)
    ppermute x16, waiting for transfers between devices, hop(): return lax.ppermute(part, 'head', xor_pairs(4, bit))  38.8 us
    ppermute x11, waiting for transfers between devices, along(): return lax.ppermute(part, 'line', pairs)  29.2 us
    ppermute x11, starting transfers between devices, along(): return lax.ppermute(part, 'line', pairs)  23.9 us
    ppermute x16, starting transfers between devices, hop(): return lax.ppermute(part, 'head', xor_pairs(4, bit))  19.9 us
    pallas_call x2, Pallas kernels, enter(): pl.pallas_call(functools.partial(enter_kernel, heads, len(chunks)), out_s...  18.2 us
    pallas_call x2, Pallas kernels, leave(): pl.pallas_call(functools.partial(leave_kernel, heads, lines, len(shared))...  13.6 us
    pallas_call x1, Pallas kernels, attention(): pl.pallas_call(functools.partial(attention_kernel, sizes), out_shape=jax....  11 us
    unnamed x53, local copies, waits for them, and re-layouts  9.52 us
  transfers between devices with their start and end apart: 41, of which 16 were waited for; matrix products, arithmetic and copies ran while one was open for 12% of the time, Pallas kernels for 17%

profile of v2, /device:TPU:0, one launch (start us, length us, event | category | flops | bytes accessed | tf_op | source)
XLA Modules:
  0.0 216.0 jit_solution(3794295579444157072)
XLA Ops:
  0.1 1.2 copy-done.1
  2.0 1.1 normalize.1.refs_0_
  3.1 3.1 %collective-permute-start = (bf16[128,4096]{1,0:T(8,128)(2,1)S(1)}, bf16[128,4096]{1,0:T(8,128)(2,1)S(1)}, u32[]{:S(2)}, u32[]{:S(2)}) collective-permute-start(bf16[128,4096]{1,0:T(8,128)(2,1)S(1)} %normalize.1.refs_0_), channel_id=1, source_target_pairs={{0,1},{1,0},{2,3},{3,2},{4,5},{5,4},{6,7},{7,6},{8,9},{9,8},{10,11... | collective-permute-start | bytes 3145736 | tf_op jit(solution)/shard_map/ppermute | solution.py:407
  6.2 0.7 collective-permute-start.1
  7.0 1.6 collective-permute-start.7
  8.6 1.5 collective-permute-start.6
  13.4 2.5 %fusion.4 = s32[32]{0:T(128)S(1)} fusion(s32[]{:T(128)} %bitcast.12, s32[]{:T(128)} %bitcast.13, s32[]{:T(128)} %bitcast.15, s32[]{:T(128)} %bitcast.14, s32[]{:T(128)} %axis_index.36), kind=kLoop, calls=%fused_computation.44 | loop fusion | flops 1504 | bytes 148 | tf_op jit(solution)/shard_map/add | solution.py:357
  15.9 2.4 %gather_fusion.1 = s32[288]{0:T(512)S(1)} fusion(s32[32]{0:T(128)S(1)} %fusion.4, s32[1024]{0:T(1024)S(1)} %pad_clamp_fusion), kind=kCustom, calls=%fused_computation.1 | custom fusion | bytes 3456 | tf_op jit(solution)/shard_map/gather | solution.py:361
  18.8 10.6 %collective-permute-done.refs_1_ = bf16[128,4096]{1,0:T(8,128)(2,1)S(1)} collective-permute-done((bf16[128,4096]{1,0:T(8,128)(2,1)S(1)}, bf16[128,4096]{1,0:T(8,128)(2,1)S(1)}, u32[]{:S(2)}, u32[]{:S(2)}) %collective-permute-start) | collective-permute-done | bytes 1048608 | tf_op jit(solution)/shard_map/ppermute | solution.py:407
  29.4 0.7 collective-permute-start.3
  30.1 1.3 collective-permute-start.4
  31.4 10.4 %collective-permute-start.5 = (bf16[512,512]{1,0:T(8,128)(2,1)}, bf16[512,512]{1,0:T(8,128)(2,1)}, u32[]{:S(2)}, u32[]{:S(2)}) collective-permute-start(bf16[512,512]{1,0:T(8,128)(2,1)} %param.9), channel_id=1, source_target_pairs={{0,1},{3,2},{4,5},{7,6},{8,9},{11,10},{12,13},{15,14},{16,17},{19,... | collective-permute-start | bytes 1572872 | tf_op jit(solution)/shard_map/ppermute | solution.py:407
  41.8 2.3 %collective-permute-done.7.refs_5_.refs_3_ = bf16[3,512,512]{2,1,0:T(8,128)(2,1)} collective-permute-done((bf16[3,512,512]{2,1,0:T(8,128)(2,1)}, bf16[3,512,512]{2,1,0:T(8,128)(2,1)}, u32[]{:S(2)}, u32[]{:S(2)}) %collective-permute-start.7) | collective-permute-done | bytes 1572896 | tf_op jit(solution)/shard_map/ppermute | solution.py:51
  44.1 1.2 slice.49
  45.4 2.1 slice.50
  47.5 3.7 %collective-permute-done.5 = bf16[512,512]{1,0:T(8,128)(2,1)} collective-permute-done((bf16[512,512]{1,0:T(8,128)(2,1)}, bf16[512,512]{1,0:T(8,128)(2,1)}, u32[]{:S(2)}, u32[]{:S(2)}) %collective-permute-start.5) | collective-permute-done | bytes 524320 | tf_op jit(solution)/shard_map/ppermute | solution.py:407
  51.2 9.7 %collective-permute-done.4 = bf16[128,4096]{1,0:T(8,128)(2,1)S(1)} collective-permute-done((bf16[128,4096]{1,0:T(8,128)(2,1)S(1)}, bf16[128,4096]{1,0:T(8,128)(2,1)S(1)}, u32[]{:S(2)}, u32[]{:S(2)}) %collective-permute-start.4) | collective-permute-done | bytes 1048608 | tf_op jit(solution)/shard_map/ppermute | solution.py:407
  60.8 1.0 copy-done.16
  61.8 1.5 collective-permute-start.8
  63.3 1.5 collective-permute-start.9
  64.8 1.3 collective-permute-start.14
  66.1 2.3 %broadcast_select_fusion.1.refs_2_ = bf16[128,4096]{1,0:T(8,128)(2,1)} fusion(bf16[128,4096]{1,0:T(8,128)(2,1)S(1)} %collective-permute-done.1, bf16[128,4096]{1,0:T(8,128)(2,1)} %copy-done.16, pred[]{:T(512)S(6)} %or.10), kind=kLoop, calls=%fused_computation.6 | loop fusion | flops 524288 | bytes 3145729 | tf_op jit(solution)/shard_map/jit(_where)/select_n | solution.py:430
  68.5 13.3 %collective-permute-done.8.refs_6_.refs_4_ = bf16[3,256,512]{2,1,0:T(8,128)(2,1)S(1)} collective-permute-done((bf16[3,256,512]{2,1,0:T(8,128)(2,1)S(1)}, bf16[3,256,512]{2,1,0:T(8,128)(2,1)S(1)}, u32[]{:S(2)}, u32[]{:S(2)}) %collective-permute-start.8) | collective-permute-done | bytes 786464 | tf_op jit(solution)/shard_map/ppermute | solution.py:51
  81.8 1.4 collective-permute-done.9.refs_7_.refs_5_
  83.8 1.5 collective-permute-start.15
  85.3 1.1 fusion.10
  86.3 1.6 collective-permute-start.16
  89.4 10.7 %enter.2 = bf16[4,3,3,128,128]{4,3,2,1,0:T(8,128)(2,1)} custom-call(bf16[128,4096]{1,0:T(8,128)(2,1)} %copy-done, bf16[128,4096]{1,0:T(8,128)(2,1)} %copy-done.13, bf16[128,4096]{1,0:T(8,128)(2,1)} %broadcast_select_fusion.1.refs_2_, bf16[3,512,512]{2,1,0:T(8,128)(2,1)} %refs_1_.1, bf16[3,512,512]{2,1,0:T(8,128)(2,1)} %collective-permute-done.6.refs_4_.refs_2_, ...), custom_call_target="tpu_custom_call" | custom-call | flops 1 | bytes 1 | tf_op jit(solution)/shard_map/enter/pallas_call | solution.py:251
  100.1 1.4 collective-permute-start.18
  102.2 3.5 %all-to-all-start = ((bf16[4,3,3,128,128]{4,3,2,1,0:T(8,128)(2,1)}), bf16[4,3,3,128,128]{4,3,2,1,0:T(8,128)(2,1)S(1)}, u32[]{:S(2)}, u32[]{:S(2)}) async-start(bf16[4,3,3,128,128]{4,3,2,1,0:T(8,128)(2,1)} %enter.2), calls=%async_computation | async-start | bytes 2359296 | tf_op jit(solution)/shard_map/all_to_all | solution.py:347
  105.8 2.3 %broadcast_select_fusion.refs_0_ = bf16[128,4096]{1,0:T(8,128)(2,1)} fusion(bf16[128,4096]{1,0:T(8,128)(2,1)S(1)} %copy-done.15, bf16[128,4096]{1,0:T(8,128)(2,1)} %collective-permute-done.14, pred[]{:T(512)S(6)} %or.10), kind=kLoop, calls=%fused_computation.5 | loop fusion | flops 524288 | bytes 3145729 | tf_op jit(solution)/shard_map/jit(_where)/select_n | solution.py:443
  108.1 7.6 %enter.3 = bf16[4,3,1,128,128]{4,3,2,1,0:T(8,128)(2,1)} custom-call(bf16[128,4096]{1,0:T(8,128)(2,1)} %broadcast_select_fusion.refs_0_, bf16[3,512,512]{2,1,0:T(8,128)(2,1)} %refs_1_.1, bf16[3,512,512]{2,1,0:T(8,128)(2,1)} %collective-permute-done.6.refs_4_.refs_2_, bf16[3,512,512]{2,1,0:T(8,128)(2,1)} %collective-permute-done.7.refs_5_.refs_3_, ...), custom_call_target="tpu_custom_call" | custom-call | flops 1 | bytes 1 | tf_op jit(solution)/shard_map/enter/pallas_call | solution.py:251
  115.7 0.9 collective-permute-done.18
  116.7 4.1 %all-to-all-done.refs_0_ = bf16[4,3,3,128,128]{4,3,2,1,0:T(8,128)(2,1)S(1)} async-done(((bf16[4,3,3,128,128]{4,3,2,1,0:T(8,128)(2,1)}), bf16[4,3,3,128,128]{4,3,2,1,0:T(8,128)(2,1)S(1)}, u32[]{:S(2)}, u32[]{:S(2)}) %all-to-all-start) | async-done | bytes 1179680 | tf_op jit(solution)/shard_map/all_to_all | solution.py:347
  120.8 3.5 %all-to-all-start.1 = ((bf16[4,3,1,128,128]{4,3,2,1,0:T(8,128)(2,1)}), bf16[4,3,1,128,128]{4,3,2,1,0:T(8,128)(2,1)S(1)}, u32[]{:S(2)}, u32[]{:S(2)}) async-start(bf16[4,3,1,128,128]{4,3,2,1,0:T(8,128)(2,1)} %enter.3), calls=%async_computation.1 | async-start | bytes 786432 | tf_op jit(solution)/shard_map/all_to_all | solution.py:347
  124.2 1.3 collective-permute-start.22
  125.5 1.1 broadcast_select_fusion.4
  126.6 5.1 %all-to-all-done.1.refs_2_ = bf16[4,3,1,128,128]{4,3,2,1,0:T(8,128)(2,1)S(1)} async-done(((bf16[4,3,1,128,128]{4,3,2,1,0:T(8,128)(2,1)}), bf16[4,3,1,128,128]{4,3,2,1,0:T(8,128)(2,1)S(1)}, u32[]{:S(2)}, u32[]{:S(2)}) %all-to-all-start.1) | async-done | bytes 393248 | tf_op jit(solution)/shard_map/all_to_all | solution.py:347
  131.8 1.5 collective-permute-start.23
  133.8 1.9 constant_dynamic-update-slice_fusion.2
  135.7 0.7 constant_dynamic-update-slice_fusion.1
  136.4 1.7 constant_dynamic-update-slice_fusion.refs_2_
  138.1 4.3 %collective-permute-done.22 = bf16[512,512]{1,0:T(8,128)(2,1)} collective-permute-done((bf16[512,512]{1,0:T(8,128)(2,1)}, bf16[512,512]{1,0:T(8,128)(2,1)}, u32[]{:S(2)}, u32[]{:S(2)}) %collective-permute-start.22) | collective-permute-done | bytes 524320 | tf_op jit(solution)/shard_map/ppermute | solution.py:407
  142.5 1.5 collective-permute-start.25
  144.0 1.1 broadcast_select_fusion.3
  145.1 1.8 collective-permute-start.26
  146.9 1.5 collective-permute-start.27
  148.4 1.1 pad_maximum_fusion.refs_4_
  149.5 11.0 %attention.1 = bf16[16,128,128]{2,1,0:T(8,128)(2,1)} custom-call(s32[16,18]{1,0:T(8,128)S(1)} %reshape.184.places, f32[16,18]{1,0:T(8,128)S(1)} %concatenate.40.biases, f32[16]{0:T(128)S(1)} %convert_add_fusion.copies, s32[16]{0:T(128)S(1)} %add.189.targets, bf16[4,3,3,128,128]{4,3,2,1,0:T(8,128)(2,1)S(1)} %all-to-all-done.refs_0_, ...), custom_call_target="tpu_custom_call" | custom-call | flops 2415919104 | bytes 4194304 | tf_op jit(solution)/shard_map/attention/pallas_call | solution.py:150
  161.4 4.9 %all-to-all-start.2 = ((bf16[16,128,128]{2,1,0:T(8,128)(2,1)}), bf16[16,128,128]{2,1,0:T(8,128)(2,1)S(1)}, u32[]{:S(2)}, u32[]{:S(2)}) async-start(bf16[16,128,128]{2,1,0:T(8,128)(2,1)} %attention.1), calls=%async_computation.2 | async-start | bytes 1048576 | tf_op jit(solution)/shard_map/all_to_all | solution.py:458
  166.3 2.0 collective-permute-start.33
  168.3 1.5 collective-permute-start.34
  169.8 9.5 %collective-permute-done.33 = bf16[512,256]{1,0:T(8,128)(2,1)S(1)} collective-permute-done((bf16[512,256]{1,0:T(8,128)(2,1)S(1)}, bf16[512,256]{1,0:T(8,128)(2,1)S(1)}, u32[]{:S(2)}, u32[]{:S(2)}) %collective-permute-start.33) | collective-permute-done | bytes 262176 | tf_op jit(solution)/shard_map/ppermute | solution.py:51
  179.7 2.9 %all-to-all-done.2.refs_0_.refs_1_ = bf16[16,128,128]{2,1,0:T(8,128)(2,1)S(1)} async-done(((bf16[16,128,128]{2,1,0:T(8,128)(2,1)}), bf16[16,128,128]{2,1,0:T(8,128)(2,1)S(1)}, u32[]{:S(2)}, u32[]{:S(2)}) %all-to-all-start.2) | async-done | bytes 524320 | tf_op jit(solution)/shard_map/all_to_all | solution.py:458
  182.7 1.1 collective-permute-start.32
  183.8 11.5 %collective-permute-done.31.refs_0_ = bf16[16,128,128]{2,1,0:T(8,128)(2,1)S(1)} collective-permute-done((bf16[16,128,128]{2,1,0:T(8,128)(2,1)S(1)}, bf16[16,128,128]{2,1,0:T(8,128)(2,1)S(1)}, u32[]{:S(2)}, u32[]{:S(2)}) %collective-permute-start.31) | collective-permute-done | bytes 524320 | tf_op jit(solution)/shard_map/ppermute | solution.py:51
  196.1 0.8 copy-done.18
  196.9 6.8 %leave.3 = (bf16[128,1024]{1,0:T(8,128)(2,1)}, bf16[128,1024]{1,0:T(8,128)(2,1)}) custom-call(s32[4]{0:T(128)} %copy-done.24, bf16[16,128,128]{2,1,0:T(8,128)(2,1)} %copy-done.17, bf16[16,128,128]{2,1,0:T(8,128)(2,1)} %copy-done.18, bf16[512,1024]{1,0:T(8,128)(2,1)} %constant_dynamic-update-slice_fusion.refs_2_, ...), custom_call_target="tpu_custom_call" | custom-call | flops 1073741824 | bytes 8388608 | tf_op jit(solution)/shard_map/leave/pallas_call | solution.py:305
  203.7 1.0 collective-permute-start.36
  204.7 0.8 collective-permute-start.37
  205.6 6.8 %leave.2 = (bf16[128,1024]{1,0:T(8,128)(2,1)}, bf16[128,1024]{1,0:T(8,128)(2,1)}) custom-call(s32[4]{0:T(128)} %copy-done.24, bf16[16,128,128]{2,1,0:T(8,128)(2,1)} %copy-done.8, bf16[16,128,128]{2,1,0:T(8,128)(2,1)} %copy-done.8, bf16[512,1024]{1,0:T(8,128)(2,1)} %constant_dynamic-update-slice_fusion.refs_2_, ...), custom_call_target="tpu_custom_call" | custom-call | flops 1073741824 | bytes 8388608 | tf_op jit(solution)/shard_map/leave/pallas_call | solution.py:305
  212.5 0.9 copy-done.2
  213.5 0.9 copy-done.3
  214.4 1.6 place.1
  (119 shorter events, 10.2 us)
Async XLA Ops:
  0.0 11.2 %copy-start.23 = (s32[32,16]{0,1:T(8,128)S(1)}, s32[32,16]{0,1:T(8,128)}, u32[]{:S(2)}) copy-start(s32[32,16]{0,1:T(8,128)} %param.10) | copy-start | bytes 6148
  0.1 1.2 copy-start.1
  3.1 15.1 %copy-start = (bf16[128,4096]{1,0:T(8,128)(2,1)}, bf16[128,4096]{1,0:T(8,128)(2,1)S(1)}, u32[]{:S(2)}) copy-start(bf16[128,4096]{1,0:T(8,128)(2,1)S(1)} %normalize.1.refs_0_) | copy-start | bytes 3145732
  3.1 26.2 %collective-permute-start = (bf16[128,4096]{1,0:T(8,128)(2,1)S(1)}, bf16[128,4096]{1,0:T(8,128)(2,1)S(1)}, u32[]{:S(2)}, u32[]{:S(2)}) collective-permute-start(bf16[128,4096]{1,0:T(8,128)(2,1)S(1)} %normalize.1.refs_0_), channel_id=1, source_target_pairs={{0,1},{1,0},{2,3},{3,2},{4,5},{5,4},{6,7},{7,6},{8,9},{9,8},{10,11... | collective-permute-start | bytes 3145736 | tf_op jit(solution)/shard_map/ppermute | solution.py:407
  6.2 23.2 %collective-permute-start.1 = (bf16[128,4096]{1,0:T(8,128)(2,1)S(1)}, bf16[128,4096]{1,0:T(8,128)(2,1)S(1)}, u32[]{:S(2)}, u32[]{:S(2)}) collective-permute-start(bf16[128,4096]{1,0:T(8,128)(2,1)S(1)} %normalize.1.refs_0_), channel_id=1, source_target_pairs={{1,2},{2,1},{5,6},{6,5},{9,10},{10,9},{13,14},{14,13},{17,18},{18,... | collective-permute-start | bytes 3145736 | tf_op jit(solution)/shard_map/ppermute | solution.py:407
  6.9 22.4 %collective-permute-start.2 = (bf16[3,512,512]{2,1,0:T(8,128)(2,1)}, bf16[3,512,512]{2,1,0:T(8,128)(2,1)}, u32[]{:S(2)}, u32[]{:S(2)}) collective-permute-start(bf16[3,512,512]{2,1,0:T(8,128)(2,1)} %refs_1_.1), channel_id=1, source_target_pairs={{0,4},{4,0},{1,5},{5,1},{2,6},{6,2},{3,7},{7,3},{8,12},{12,8},{9,1... | collective-permute-start | bytes 4718600 | tf_op jit(solution)/shard_map/ppermute | solution.py:410
  7.0 37.1 %collective-permute-start.7 = (bf16[3,512,512]{2,1,0:T(8,128)(2,1)}, bf16[3,512,512]{2,1,0:T(8,128)(2,1)}, u32[]{:S(2)}, u32[]{:S(2)}) collective-permute-start(bf16[3,512,512]{2,1,0:T(8,128)(2,1)} %refs_1_.1), channel_id=1, source_target_pairs={{0,16},{8,24},{16,0},{24,8},{1,17},{9,25},{17,1},{25,9},{2,18},{10... | collective-permute-start | bytes 4718600 | tf_op jit(solution)/shard_map/ppermute | solution.py:51
  8.6 36.8 %collective-permute-start.6 = (bf16[3,512,512]{2,1,0:T(8,128)(2,1)}, bf16[3,512,512]{2,1,0:T(8,128)(2,1)}, u32[]{:S(2)}, u32[]{:S(2)}) collective-permute-start(bf16[3,512,512]{2,1,0:T(8,128)(2,1)} %refs_1_.1), channel_id=1, source_target_pairs={{0,8},{8,0},{16,24},{24,16},{1,9},{9,1},{17,25},{25,17},{2,10},{10... | collective-permute-start | bytes 4718600 | tf_op jit(solution)/shard_map/ppermute | solution.py:51
  10.8 7.5 %copy-start.24 = (s32[4]{0:T(128)}, s32[4]{0:T(128)S(1)}, u32[]{:S(2)}) copy-start(s32[4]{0:T(128)S(1)} %dynamic-slice_bitcast_fusion.order) | copy-start | bytes 52
  29.4 18.1 %copy-start.13 = (bf16[128,4096]{1,0:T(8,128)(2,1)}, bf16[128,4096]{1,0:T(8,128)(2,1)S(1)}, u32[]{:S(2)}) copy-start(bf16[128,4096]{1,0:T(8,128)(2,1)S(1)} %collective-permute-done.refs_1_) | copy-start | bytes 3145732
  29.4 21.8 %collective-permute-start.3 = (bf16[128,4096]{1,0:T(8,128)(2,1)S(1)}, bf16[128,4096]{1,0:T(8,128)(2,1)S(1)}, u32[]{:S(2)}, u32[]{:S(2)}) collective-permute-start(bf16[128,4096]{1,0:T(8,128)(2,1)S(1)} %collective-permute-done.refs_1_), channel_id=1, source_target_pairs={{1,2},{2,1},{5,6},{6,5},{9,10},{10,9},{13,14},{14,13},{17,18},{18,... | collective-permute-start | bytes 3145736 | tf_op jit(solution)/shard_map/ppermute | solution.py:407
  30.1 30.7 %collective-permute-start.4 = (bf16[128,4096]{1,0:T(8,128)(2,1)S(1)}, bf16[128,4096]{1,0:T(8,128)(2,1)S(1)}, u32[]{:S(2)}, u32[]{:S(2)}) collective-permute-start(bf16[128,4096]{1,0:T(8,128)(2,1)S(1)} %collective-permute-done.1), channel_id=1, source_target_pairs={{1,0},{2,3},{5,4},{6,7},{9,8},{10,11},{13,12},{14,15},{17,16},{18,... | collective-permute-start | bytes 3145736 | tf_op jit(solution)/shard_map/ppermute | solution.py:407
  31.4 19.7 %collective-permute-start.5 = (bf16[512,512]{1,0:T(8,128)(2,1)}, bf16[512,512]{1,0:T(8,128)(2,1)}, u32[]{:S(2)}, u32[]{:S(2)}) collective-permute-start(bf16[512,512]{1,0:T(8,128)(2,1)} %param.9), channel_id=1, source_target_pairs={{0,1},{3,2},{4,5},{7,6},{8,9},{11,10},{12,13},{15,14},{16,17},{19,... | collective-permute-start | bytes 1572872 | tf_op jit(solution)/shard_map/ppermute | solution.py:407
  51.2 9.7 %copy-start.14 = (bf16[128,4096]{1,0:T(8,128)(2,1)}, bf16[128,4096]{1,0:T(8,128)(2,1)S(1)}, u32[]{:S(2)}) copy-start(bf16[128,4096]{1,0:T(8,128)(2,1)S(1)} %collective-permute-done.3) | copy-start | bytes 3145732
  60.8 1.0 copy-start.16
  60.8 22.4 %collective-permute-start.10 = (bf16[3,512,512]{2,1,0:T(8,128)(2,1)}, bf16[3,512,512]{2,1,0:T(8,128)(2,1)S(1)}, u32[]{:S(2)}, u32[]{:S(2)}) collective-permute-start(bf16[3,512,512]{2,1,0:T(8,128)(2,1)} %collective-permute-done.6.refs_4_.refs_2_), channel_id=1, source_target_pairs={{0,4},{4,0},{1,5},{5,1},{2,6},{6,2},{3,7},{7,3},{8,12},{12,8},{9,1... | collective-permute-start | bytes 4718600 | tf_op jit(solution)/shard_map/ppermute | solution.py:410
  61.8 21.4 %collective-permute-start.11 = (bf16[3,512,512]{2,1,0:T(8,128)(2,1)}, bf16[3,512,512]{2,1,0:T(8,128)(2,1)}, u32[]{:S(2)}, u32[]{:S(2)}) collective-permute-start(bf16[3,512,512]{2,1,0:T(8,128)(2,1)} %collective-permute-done.7.refs_5_.refs_3_), channel_id=1, source_target_pairs={{0,4},{4,0},{1,5},{5,1},{2,6},{6,2},{3,7},{7,3},{8,12},{12,8},{9,1... | collective-permute-start | bytes 4718600 | tf_op jit(solution)/shard_map/ppermute | solution.py:410
  61.8 20.0 %collective-permute-start.8 = (bf16[3,256,512]{2,1,0:T(8,128)(2,1)S(1)}, bf16[3,256,512]{2,1,0:T(8,128)(2,1)S(1)}, u32[]{:S(2)}, u32[]{:S(2)}) collective-permute-start(bf16[3,256,512]{2,1,0:T(8,128)(2,1)S(1)} %slice.49), channel_id=1, source_target_pairs={{0,8},{8,0},{16,24},{24,16},{1,9},{9,1},{17,25},{25,17},{2,10},{10... | collective-permute-start | bytes 2359304 | tf_op jit(solution)/shard_map/ppermute | solution.py:51
  63.3 19.9 %collective-permute-start.9 = (bf16[3,256,512]{2,1,0:T(8,128)(2,1)}, bf16[3,256,512]{2,1,0:T(8,128)(2,1)S(1)}, u32[]{:S(2)}, u32[]{:S(2)}) collective-permute-start(bf16[3,256,512]{2,1,0:T(8,128)(2,1)} %slice.50), channel_id=1, source_target_pairs={{0,16},{8,24},{16,0},{24,8},{1,17},{9,25},{17,1},{25,9},{2,18},{10... | collective-permute-start | bytes 2359304 | tf_op jit(solution)/shard_map/ppermute | solution.py:51
  64.8 35.2 %collective-permute-start.14 = (bf16[128,4096]{1,0:T(8,128)(2,1)}, bf16[128,4096]{1,0:T(8,128)(2,1)}, u32[]{:S(2)}, u32[]{:S(2)}) collective-permute-start(bf16[128,4096]{1,0:T(8,128)(2,1)} %copy-done.14), channel_id=1, source_target_pairs={{1,0},{2,3},{5,4},{6,7},{9,8},{10,11},{13,12},{14,15},{17,16},{18,... | collective-permute-start | bytes 3145736 | tf_op jit(solution)/shard_map/ppermute | solution.py:407
  81.8 7.4 %copy-start.9 = (bf16[3,256,512]{2,1,0:T(8,128)(2,1)}, bf16[3,256,512]{2,1,0:T(8,128)(2,1)S(1)}, u32[]{:S(2)}) copy-start(bf16[3,256,512]{2,1,0:T(8,128)(2,1)S(1)} %collective-permute-done.8.refs_6_.refs_4_) | copy-start | bytes 2359300
  83.2 6.0 %copy-start.10 = (bf16[3,256,512]{2,1,0:T(8,128)(2,1)}, bf16[3,256,512]{2,1,0:T(8,128)(2,1)S(1)}, u32[]{:S(2)}) copy-start(bf16[3,256,512]{2,1,0:T(8,128)(2,1)S(1)} %collective-permute-done.9.refs_7_.refs_5_) | copy-start | bytes 2359300
  83.2 6.0 %copy-start.7 = (bf16[3,512,512]{2,1,0:T(8,128)(2,1)}, bf16[3,512,512]{2,1,0:T(8,128)(2,1)S(1)}, u32[]{:S(2)}) copy-start(bf16[3,512,512]{2,1,0:T(8,128)(2,1)S(1)} %collective-permute-done.10.refs_9_.refs_7_) | copy-start | bytes 4718596
  83.2 4.7 %collective-permute-start.12 = (bf16[3,256,512]{2,1,0:T(8,128)(2,1)S(1)}, bf16[3,256,512]{2,1,0:T(8,128)(2,1)S(1)}, u32[]{:S(2)}, u32[]{:S(2)}) collective-permute-start(bf16[3,256,512]{2,1,0:T(8,128)(2,1)S(1)} %collective-permute-done.8.refs_6_.refs_4_), channel_id=1, source_target_pairs={{0,4},{4,0},{1,5},{5,1},{2,6},{6,2},{3,7},{7,3},{8,12},{12,8},{9,1... | collective-permute-start | bytes 2359304 | tf_op jit(solution)/shard_map/ppermute | solution.py:410
  83.3 5.2 %collective-permute-start.13 = (bf16[3,256,512]{2,1,0:T(8,128)(2,1)S(1)}, bf16[3,256,512]{2,1,0:T(8,128)(2,1)S(1)}, u32[]{:S(2)}, u32[]{:S(2)}) collective-permute-start(bf16[3,256,512]{2,1,0:T(8,128)(2,1)S(1)} %collective-permute-done.9.refs_7_.refs_5_), channel_id=1, source_target_pairs={{0,4},{4,0},{1,5},{5,1},{2,6},{6,2},{3,7},{7,3},{8,12},{12,8},{9,1... | collective-permute-start | bytes 2359304 | tf_op jit(solution)/shard_map/ppermute | solution.py:410
  83.8 17.7 %collective-permute-start.15 = (bf16[512,512]{1,0:T(8,128)(2,1)}, bf16[512,512]{1,0:T(8,128)(2,1)}, u32[]{:S(2)}, u32[]{:S(2)}) collective-permute-start(bf16[512,512]{1,0:T(8,128)(2,1)} %param.9), channel_id=1, source_target_pairs={{1,2},{2,1},{5,6},{6,5},{9,10},{10,9},{13,14},{14,13},{17,18},{18,... | collective-permute-start | bytes 1572872 | tf_op jit(solution)/shard_map/ppermute | solution.py:407
  86.3 15.2 %collective-permute-start.16 = (bf16[512,256]{1,0:T(8,128)(2,1)S(1)}, bf16[512,256]{1,0:T(8,128)(2,1)S(1)}, u32[]{:S(2)}, u32[]{:S(2)}) collective-permute-start(bf16[512,256]{1,0:T(8,128)(2,1)S(1)} %get-tuple-element.116), channel_id=1, source_target_pairs={{0,16},{8,24},{16,0},{24,8},{1,17},{9,25},{17,1},{25,9},{2,18},{10... | collective-permute-start | bytes 786440 | tf_op jit(solution)/shard_map/ppermute | solution.py:51
  87.9 1.3 copy-start.11
  87.9 13.6 %collective-permute-start.17 = (bf16[512,256]{1,0:T(8,128)(2,1)S(1)}, bf16[512,256]{1,0:T(8,128)(2,1)}, u32[]{:S(2)}, u32[]{:S(2)}) collective-permute-start(bf16[512,256]{1,0:T(8,128)(2,1)S(1)} %get-tuple-element.115), channel_id=1, source_target_pairs={{0,8},{8,0},{16,24},{24,16},{1,9},{9,1},{17,25},{25,17},{2,10},{10... | collective-permute-start | bytes 786440 | tf_op jit(solution)/shard_map/ppermute | solution.py:51
  88.5 0.9 copy-start.12
  88.5 27.2 %collective-permute-start.19 = (bf16[512,512]{1,0:T(8,128)(2,1)}, bf16[512,512]{1,0:T(8,128)(2,1)S(1)}, u32[]{:S(2)}, u32[]{:S(2)}) collective-permute-start(bf16[512,512]{1,0:T(8,128)(2,1)} %collective-permute-done.5), channel_id=1, source_target_pairs={{1,2},{2,1},{5,6},{6,5},{9,10},{10,9},{13,14},{14,13},{17,18},{18,... | collective-permute-start | bytes 1572872 | tf_op jit(solution)/shard_map/ppermute | solution.py:407
  100.1 5.7 %copy-start.15 = (bf16[128,4096]{1,0:T(8,128)(2,1)S(1)}, bf16[128,4096]{1,0:T(8,128)(2,1)}, u32[]{:S(2)}) copy-start(bf16[128,4096]{1,0:T(8,128)(2,1)} %copy-done.14) | copy-start | bytes 3145732
  100.1 16.6 %collective-permute-start.18 = (bf16[512,512]{1,0:T(8,128)(2,1)}, bf16[512,512]{1,0:T(8,128)(2,1)}, u32[]{:S(2)}, u32[]{:S(2)}) collective-permute-start(bf16[512,512]{1,0:T(8,128)(2,1)} %param.9), channel_id=1, source_target_pairs={{1,0},{2,3},{5,4},{6,7},{9,8},{10,11},{13,12},{14,15},{17,16},{18,... | collective-permute-start | bytes 1572872 | tf_op jit(solution)/shard_map/ppermute | solution.py:407
  102.2 18.5 %all-to-all-start = ((bf16[4,3,3,128,128]{4,3,2,1,0:T(8,128)(2,1)}), bf16[4,3,3,128,128]{4,3,2,1,0:T(8,128)(2,1)S(1)}, u32[]{:S(2)}, u32[]{:S(2)}) async-start(bf16[4,3,3,128,128]{4,3,2,1,0:T(8,128)(2,1)} %enter.2), calls=%async_computation | async-start | bytes 2359296 | tf_op jit(solution)/shard_map/all_to_all | solution.py:347
  115.7 5.0 %copy-start.19 = (bf16[512,512]{1,0:T(8,128)(2,1)}, bf16[512,512]{1,0:T(8,128)(2,1)S(1)}, u32[]{:S(2)}) copy-start(bf16[512,512]{1,0:T(8,128)(2,1)S(1)} %collective-permute-done.19) | copy-start | bytes 1572868
  120.7 23.2 %collective-permute-start.20 = (bf16[4,3,3,128,128]{4,3,2,1,0:T(8,128)(2,1)S(1)}, bf16[4,3,3,128,128]{4,3,2,1,0:T(8,128)(2,1)S(1)}, u32[]{:S(2)}, u32[]{:S(2)}) collective-permute-start(bf16[4,3,3,128,128]{4,3,2,1,0:T(8,128)(2,1)S(1)} %all-to-all-done.refs_0_), channel_id=1, source_target_pairs={{0,4},{4,0},{1,5},{5,1},{2,6},{6,2},{3,7},{7,3},{8,12},{12,8},{9,1... | collective-permute-start | bytes 3538952 | tf_op jit(solution)/shard_map/ppermute | solution.py:47
  120.8 11.0 %all-to-all-start.1 = ((bf16[4,3,1,128,128]{4,3,2,1,0:T(8,128)(2,1)}), bf16[4,3,1,128,128]{4,3,2,1,0:T(8,128)(2,1)S(1)}, u32[]{:S(2)}, u32[]{:S(2)}) async-start(bf16[4,3,1,128,128]{4,3,2,1,0:T(8,128)(2,1)} %enter.3), calls=%async_computation.1 | async-start | bytes 786432 | tf_op jit(solution)/shard_map/all_to_all | solution.py:347
  124.2 18.2 %collective-permute-start.22 = (bf16[512,512]{1,0:T(8,128)(2,1)}, bf16[512,512]{1,0:T(8,128)(2,1)}, u32[]{:S(2)}, u32[]{:S(2)}) collective-permute-start(bf16[512,512]{1,0:T(8,128)(2,1)} %collective-permute-done.15), channel_id=1, source_target_pairs={{1,0},{2,3},{5,4},{6,7},{9,8},{10,11},{13,12},{14,15},{17,16},{18,... | collective-permute-start | bytes 1572872 | tf_op jit(solution)/shard_map/ppermute | solution.py:407
  131.7 4.0 %copy-start.22 = (bf16[512,256]{1,0:T(8,128)(2,1)S(1)}, bf16[512,256]{1,0:T(8,128)(2,1)}, u32[]{:S(2)}) copy-start(bf16[512,256]{1,0:T(8,128)(2,1)} %copy-done.21) | copy-start | bytes 786436
  131.8 10.7 %copy-start.20 = (bf16[512,512]{1,0:T(8,128)(2,1)S(1)}, bf16[512,512]{1,0:T(8,128)(2,1)}, u32[]{:S(2)}) copy-start(bf16[512,512]{1,0:T(8,128)(2,1)} %copy-done.19) | copy-start | bytes 1572868
  131.8 12.2 %collective-permute-start.21 = (bf16[4,3,1,128,128]{4,3,2,1,0:T(8,128)(2,1)S(1)}, bf16[4,3,1,128,128]{4,3,2,1,0:T(8,128)(2,1)S(1)}, u32[]{:S(2)}, u32[]{:S(2)}) collective-permute-start(bf16[4,3,1,128,128]{4,3,2,1,0:T(8,128)(2,1)S(1)} %all-to-all-done.1.refs_2_), channel_id=1, source_target_pairs={{0,4},{4,0},{1,5},{5,1},{2,6},{6,2},{3,7},{7,3},{8,12},{12,8},{9,1... | collective-permute-start | bytes 1179656 | tf_op jit(solution)/shard_map/ppermute | solution.py:47
  131.8 10.6 %collective-permute-start.23 = (bf16[512,256]{1,0:T(8,128)(2,1)S(1)}, bf16[512,256]{1,0:T(8,128)(2,1)S(1)}, u32[]{:S(2)}, u32[]{:S(2)}) collective-permute-start(bf16[512,256]{1,0:T(8,128)(2,1)S(1)} %get-tuple-element.114), channel_id=1, source_target_pairs={{0,16},{8,24},{16,0},{24,8},{1,17},{9,25},{17,1},{25,9},{2,18},{10... | collective-permute-start | bytes 786440 | tf_op jit(solution)/shard_map/ppermute | solution.py:51
  133.3 10.6 %collective-permute-start.24 = (bf16[512,256]{1,0:T(8,128)(2,1)S(1)}, bf16[512,256]{1,0:T(8,128)(2,1)S(1)}, u32[]{:S(2)}, u32[]{:S(2)}) collective-permute-start(bf16[512,256]{1,0:T(8,128)(2,1)S(1)} %get-tuple-element.113), channel_id=1, source_target_pairs={{0,8},{8,0},{16,24},{24,16},{1,9},{9,1},{17,25},{25,17},{2,10},{10... | collective-permute-start | bytes 786440 | tf_op jit(solution)/shard_map/ppermute | solution.py:51
  142.4 37.3 %collective-permute-start.28 = (bf16[512,1024]{1,0:T(8,128)(2,1)}, bf16[512,1024]{1,0:T(8,128)(2,1)}, u32[]{:S(2)}, u32[]{:S(2)}) collective-permute-start(bf16[512,1024]{1,0:T(8,128)(2,1)} %constant_dynamic-update-slice_fusion.refs_2_), channel_id=1, source_target_pairs={{0,4},{4,0},{1,5},{5,1},{2,6},{6,2},{3,7},{7,3},{8,12},{12,8},{9,1... | collective-permute-start | bytes 3145736 | tf_op jit(solution)/shard_map/ppermute | solution.py:410
  142.5 18.1 %collective-permute-start.25 = (bf16[512,512]{1,0:T(8,128)(2,1)S(1)}, bf16[512,512]{1,0:T(8,128)(2,1)S(1)}, u32[]{:S(2)}, u32[]{:S(2)}) collective-permute-start(bf16[512,512]{1,0:T(8,128)(2,1)S(1)} %copy-done.20), channel_id=1, source_target_pairs={{1,0},{2,3},{5,4},{6,7},{9,8},{10,11},{13,12},{14,15},{17,16},{18,... | collective-permute-start | bytes 1572872 | tf_op jit(solution)/shard_map/ppermute | solution.py:407
  145.1 15.4 %collective-permute-start.26 = (bf16[512,256]{1,0:T(8,128)(2,1)S(1)}, bf16[512,256]{1,0:T(8,128)(2,1)S(1)}, u32[]{:S(2)}, u32[]{:S(2)}) collective-permute-start(bf16[512,256]{1,0:T(8,128)(2,1)S(1)} %get-tuple-element.112), channel_id=1, source_target_pairs={{0,16},{8,24},{16,0},{24,8},{1,17},{9,25},{17,1},{25,9},{2,18},{10... | collective-permute-start | bytes 786440 | tf_op jit(solution)/shard_map/ppermute | solution.py:51
  146.9 13.7 %collective-permute-start.27 = (bf16[512,256]{1,0:T(8,128)(2,1)S(1)}, bf16[512,256]{1,0:T(8,128)(2,1)S(1)}, u32[]{:S(2)}, u32[]{:S(2)}) collective-permute-start(bf16[512,256]{1,0:T(8,128)(2,1)S(1)} %get-tuple-element.111), channel_id=1, source_target_pairs={{0,8},{8,0},{16,24},{24,16},{1,9},{9,1},{17,25},{25,17},{2,10},{10... | collective-permute-start | bytes 786440 | tf_op jit(solution)/shard_map/ppermute | solution.py:51
  149.5 30.2 %collective-permute-start.29 = (bf16[512,1024]{1,0:T(8,128)(2,1)}, bf16[512,1024]{1,0:T(8,128)(2,1)}, u32[]{:S(2)}, u32[]{:S(2)}) collective-permute-start(bf16[512,1024]{1,0:T(8,128)(2,1)} %pad_maximum_fusion.refs_4_), channel_id=1, source_target_pairs={{0,4},{4,0},{1,5},{5,1},{2,6},{6,2},{3,7},{7,3},{8,12},{12,8},{9,1... | collective-permute-start | bytes 3145736 | tf_op jit(solution)/shard_map/ppermute | solution.py:410
  160.8 18.8 %copy-start.5 = (bf16[512,1024]{1,0:T(8,128)(2,1)}, bf16[512,1024]{1,0:T(8,128)(2,1)S(1)}, u32[]{:S(2)}) copy-start(bf16[512,1024]{1,0:T(8,128)(2,1)S(1)} %pad_maximum_fusion.1.refs_6_) | copy-start | bytes 3145732
  160.8 21.9 %collective-permute-start.30 = (bf16[512,1024]{1,0:T(8,128)(2,1)S(1)}, bf16[512,1024]{1,0:T(8,128)(2,1)}, u32[]{:S(2)}, u32[]{:S(2)}) collective-permute-start(bf16[512,1024]{1,0:T(8,128)(2,1)S(1)} %pad_maximum_fusion.1.refs_6_), channel_id=1, source_target_pairs={{0,4},{4,0},{1,5},{5,1},{2,6},{6,2},{3,7},{7,3},{8,12},{12,8},{9,1... | collective-permute-start | bytes 3145736 | tf_op jit(solution)/shard_map/ppermute | solution.py:410
  161.4 21.3 %all-to-all-start.2 = ((bf16[16,128,128]{2,1,0:T(8,128)(2,1)}), bf16[16,128,128]{2,1,0:T(8,128)(2,1)S(1)}, u32[]{:S(2)}, u32[]{:S(2)}) async-start(bf16[16,128,128]{2,1,0:T(8,128)(2,1)} %attention.1), calls=%async_computation.2 | async-start | bytes 1048576 | tf_op jit(solution)/shard_map/all_to_all | solution.py:458
  166.3 12.9 %collective-permute-start.33 = (bf16[512,256]{1,0:T(8,128)(2,1)S(1)}, bf16[512,256]{1,0:T(8,128)(2,1)S(1)}, u32[]{:S(2)}, u32[]{:S(2)}) collective-permute-start(bf16[512,256]{1,0:T(8,128)(2,1)S(1)} %get-tuple-element.109), channel_id=1, source_target_pairs={{0,16},{8,24},{16,0},{24,8},{1,17},{9,25},{17,1},{25,9},{2,18},{10... | collective-permute-start | bytes 786440 | tf_op jit(solution)/shard_map/ppermute | solution.py:51
  168.3 11.1 %collective-permute-start.34 = (bf16[512,256]{1,0:T(8,128)(2,1)S(1)}, bf16[512,256]{1,0:T(8,128)(2,1)S(1)}, u32[]{:S(2)}, u32[]{:S(2)}) collective-permute-start(bf16[512,256]{1,0:T(8,128)(2,1)S(1)} %get-tuple-element.110), channel_id=1, source_target_pairs={{0,8},{8,0},{16,24},{24,16},{1,9},{9,1},{17,25},{25,17},{2,10},{10... | collective-permute-start | bytes 786440 | tf_op jit(solution)/shard_map/ppermute | solution.py:51
  179.6 16.2 %copy-start.6 = (bf16[512,1024]{1,0:T(8,128)(2,1)}, bf16[512,1024]{1,0:T(8,128)(2,1)S(1)}, u32[]{:S(2)}) copy-start(bf16[512,1024]{1,0:T(8,128)(2,1)S(1)} %pad_maximum_fusion.2.refs_8_) | copy-start | bytes 3145732
  179.6 4.2 %collective-permute-start.35 = (bf16[512,1024]{1,0:T(8,128)(2,1)S(1)}, bf16[512,1024]{1,0:T(8,128)(2,1)}, u32[]{:S(2)}, u32[]{:S(2)}) collective-permute-start(bf16[512,1024]{1,0:T(8,128)(2,1)S(1)} %pad_maximum_fusion.2.refs_8_), channel_id=1, source_target_pairs={{0,4},{4,0},{1,5},{5,1},{2,6},{6,2},{3,7},{7,3},{8,12},{12,8},{9,1... | collective-permute-start | bytes 3145736 | tf_op jit(solution)/shard_map/ppermute | solution.py:410
  182.7 21.1 %copy-start.8 = (bf16[16,128,128]{2,1,0:T(8,128)(2,1)}, bf16[16,128,128]{2,1,0:T(8,128)(2,1)S(1)}, u32[]{:S(2)}) copy-start(bf16[16,128,128]{2,1,0:T(8,128)(2,1)S(1)} %all-to-all-done.2.refs_0_.refs_1_) | copy-start | bytes 1572868
  182.7 12.6 %collective-permute-start.31 = (bf16[16,128,128]{2,1,0:T(8,128)(2,1)S(1)}, bf16[16,128,128]{2,1,0:T(8,128)(2,1)S(1)}, u32[]{:S(2)}, u32[]{:S(2)}) collective-permute-start(bf16[16,128,128]{2,1,0:T(8,128)(2,1)S(1)} %all-to-all-done.2.refs_0_.refs_1_), channel_id=1, source_target_pairs={{0,8},{8,0},{16,24},{24,16},{1,9},{9,1},{17,25},{25,17},{2,10},{10... | collective-permute-start | bytes 1572872 | tf_op jit(solution)/shard_map/ppermute | solution.py:51
  182.7 13.1 %collective-permute-start.32 = (bf16[16,128,128]{2,1,0:T(8,128)(2,1)S(1)}, bf16[16,128,128]{2,1,0:T(8,128)(2,1)S(1)}, u32[]{:S(2)}, u32[]{:S(2)}) collective-permute-start(bf16[16,128,128]{2,1,0:T(8,128)(2,1)S(1)} %all-to-all-done.2.refs_0_.refs_1_), channel_id=1, source_target_pairs={{0,16},{8,24},{16,0},{24,8},{1,17},{9,25},{17,1},{25,9},{2,18},{10... | collective-permute-start | bytes 1572872 | tf_op jit(solution)/shard_map/ppermute | solution.py:51
  195.3 0.8 copy-start.17
  196.1 0.8 copy-start.18
  203.7 8.7 %collective-permute-start.36 = (bf16[128,1024]{1,0:T(8,128)(2,1)}, bf16[128,1024]{1,0:T(8,128)(2,1)S(1)}, u32[]{:S(2)}, u32[]{:S(2)}) collective-permute-start(bf16[128,1024]{1,0:T(8,128)(2,1)} %get-tuple-element.107), channel_id=1, source_target_pairs={{0,8},{8,0},{16,24},{24,16},{1,9},{9,1},{17,25},{25,17},{2,10},{10... | collective-permute-start | bytes 786440 | tf_op jit(solution)/shard_map/ppermute | solution.py:51
  204.7 7.8 %collective-permute-start.37 = (bf16[128,1024]{1,0:T(8,128)(2,1)}, bf16[128,1024]{1,0:T(8,128)(2,1)S(1)}, u32[]{:S(2)}, u32[]{:S(2)}) collective-permute-start(bf16[128,1024]{1,0:T(8,128)(2,1)} %get-tuple-element.108), channel_id=1, source_target_pairs={{0,16},{8,24},{16,0},{24,8},{1,17},{9,25},{17,1},{25,9},{2,18},{10... | collective-permute-start | bytes 786440 | tf_op jit(solution)/shard_map/ppermute | solution.py:51
  212.5 1.0 copy-start.2
  213.5 0.9 copy-start.3
  (2 other events, 1.4 us)

commit v3 on v2

--- a/solution.py
+++ b/solution.py
@@ -221,64 +221,85 @@
     )(planes, order, *landed, *arrays)
 
 
-def enter_kernel(heads, count, *refs):
-    chunks = refs[:count]
-    pieces = refs[count:-4]
-    out, weights, rows, sems = refs[-4:]
+def enter_kernel(heads, chunks, plan, flag, *refs):
+    count = sum(chunks)
+    rows_in, arrays = refs[:count], refs[count:-5]
+    out, weights, rows, row_sems, sems = refs[-5:]
+    at = 0
+    for n, choices in enumerate(chunks):
+        target = rows.at[pl.ds(n * BLK, BLK)]
+        if choices == 1:
+            pltpu.make_async_copy(rows_in[at], target, row_sems.at[n]).start()
+        else:
+            for choice in range(2):
+
+                @pl.when(flag[0] == choice)
+                def _(choice=choice):
+                    pltpu.make_async_copy(rows_in[at + choice], target, row_sems.at[n]).start()
+
+        at += choices
     copies = []
     for c in range(3):
         at = 0
-        for piece in pieces:
-            target = weights.at[c, pl.ds(at, piece.shape[1])]
-            copies.append(pltpu.make_async_copy(piece.at[c], target, sems.at[len(copies)]))
-            at += piece.shape[1]
-    for copy in copies:
+        for i, place in plan[c]:
+            size = arrays[i].shape[1]
+            target = weights.at[c, pl.ds(at, size)]
+            copies.append((c, pltpu.make_async_copy(arrays[i].at[place], target, sems.at[len(copies)])))
+            at += size
+    for _, copy in copies:
         copy.start()
-    for n, chunk in enumerate(chunks):
-        rows[n * BLK : (n + 1) * BLK] = chunk[...]
+    at = 0
+    for n, choices in enumerate(chunks):
+        pltpu.make_async_copy(rows_in[at], rows.at[pl.ds(n * BLK, BLK)], row_sems.at[n]).wait()
+        at += choices
     for c in range(3):
-        for copy in copies[c * len(pieces) : (c + 1) * len(pieces)]:
-            copy.wait()
+        for which, copy in copies:
+            if which == c:
+                copy.wait()
         total = jnp.dot(rows[...], weights[c], preferred_element_type=F32).astype(BF16)
-        for n in range(count):
+        for n in range(len(chunks)):
             for h in range(heads):
                 out[h, c, n] = total[n * BLK : (n + 1) * BLK, h * HEAD_DIM : (h + 1) * HEAD_DIM]
 
 
-def enter(chunks, pieces, heads):
-    features = chunks[0].shape[1]
-    vmem = pl.BlockSpec(memory_space=pltpu.VMEM)
+def enter(flag, chunks, arrays, plan, heads):
+    chunks = [chunk if isinstance(chunk, tuple) else (chunk,) for chunk in chunks]
+    features = chunks[0][0].shape[1]
+    hbm = pl.BlockSpec(memory_space=pl.ANY)
+    rows_in = [array for chunk in chunks for array in chunk]
     return pl.pallas_call(
-        functools.partial(enter_kernel, heads, len(chunks)),
+        functools.partial(enter_kernel, heads, [len(chunk) for chunk in chunks], plan),
         out_shape=jax.ShapeDtypeStruct((heads, 3, len(chunks), BLK, HEAD_DIM), BF16),
-        in_specs=[vmem] * len(chunks) + [pl.BlockSpec(memory_space=pl.ANY)] * len(pieces),
-        out_specs=vmem,
+        in_specs=[pl.BlockSpec(memory_space=pltpu.SMEM)] + [hbm] * (len(rows_in) + len(arrays)),
+        out_specs=pl.BlockSpec(memory_space=pltpu.VMEM),
         scratch_shapes=[
             pltpu.VMEM((3, features, heads * HEAD_DIM), BF16),
             pltpu.VMEM((len(chunks) * BLK, features), BF16),
-            pltpu.SemaphoreType.DMA((3 * len(pieces),)),
+            pltpu.SemaphoreType.DMA((len(chunks),)),
+            pltpu.SemaphoreType.DMA((sum(len(parts) for parts in plan),)),
         ],
         compiler_params=pltpu.CompilerParams(vmem_limit_bytes=58 << 20),
         cost_estimate=pl.CostEstimate(flops=1, bytes_accessed=1, transcendentals=0),
         name="enter",
-    )(*chunks, *pieces)
+    )(flag, *rows_in, *arrays)
 
 
 def leave_kernel(heads, lines, count, order, *refs):
-    landed, pieces = refs[:2], refs[2 : 2 + count]
-    outs = refs[2 + count : 4 + count]
-    weights, rows, sems = refs[4 + count :]
+    landed, pieces = refs[:2], refs[2 : 2 + 6 * count]
+    outs = refs[2 + 6 * count : 4 + 6 * count]
+    weights, rows, sems = refs[4 + 6 * count :]
     depth = heads * HEAD_DIM
     width = weights.shape[3]
     copies = []
     for side in range(2):
-        for i, (core, first) in enumerate(((0, side), (1, side), (0, 2 + side), (1, 2 + side))):
+        for i in range(4):
             at = 0
-            for piece in pieces[core::2]:
-                source = piece.at[:, pl.ds(first * width, width)]
-                target = weights.at[side, i, pl.ds(at, piece.shape[0])]
+            for b in range(count):
+                batch = pieces[6 * b + 3 * (i % 2) : 6 * b + 3 * (i % 2) + 3]
+                source = batch[0].at[:, pl.ds(side * width, width)] if i < 2 else batch[1 + side]
+                target = weights.at[side, i, pl.ds(at, source.shape[0])]
                 copies.append(pltpu.make_async_copy(source, target, sems.at[len(copies)]))
-                at += piece.shape[0]
+                at += source.shape[0]
     for copy in copies:
         copy.start()
     for side in range(2):
@@ -288,7 +309,7 @@
                 rows[side, :, at : at + HEAD_DIM] = landed[side][h * lines + order[s]]
     for side in range(2):
         for i in range(4):
-            for copy in copies[(side * 4 + i) * (count // 2) : (side * 4 + i + 1) * (count // 2)]:
+            for copy in copies[(side * 4 + i) * count : (side * 4 + i + 1) * count]:
                 copy.wait()
             outs[side][:, i * width : (i + 1) * width] = jnp.dot(
                 rows[side], weights[side, i], preferred_element_type=F32
@@ -296,8 +317,9 @@
 
 
 def leave(order, landed_x, landed_y, shared, heads, lines):
-    depth = sum(piece.shape[0] for piece in shared[::2])
-    width = shared[0].shape[1] // 4
+    depth = sum(batch[0].shape[0] for batch in shared)
+    width = shared[0][0].shape[1] // 2
+    arrays = [array for batch in shared for array in batch]
     smem = pl.BlockSpec(memory_space=pltpu.SMEM)
     vmem = pl.BlockSpec(memory_space=pltpu.VMEM)
     hbm = pl.BlockSpec(memory_space=pl.ANY)
@@ -305,19 +327,19 @@
     return pl.pallas_call(
         functools.partial(leave_kernel, heads, lines, len(shared)),
         out_shape=(out, out),
-        in_specs=[smem] + [vmem] * 2 + [hbm] * len(shared),
+        in_specs=[smem] + [vmem] * 2 + [hbm] * len(arrays),
         out_specs=(vmem, vmem),
         scratch_shapes=[
             pltpu.VMEM((2, 4, depth, width), BF16),
             pltpu.VMEM((2, BLK, depth), BF16),
-            pltpu.SemaphoreType.DMA((4 * len(shared),)),
+            pltpu.SemaphoreType.DMA((8 * len(shared),)),
         ],
         compiler_params=pltpu.CompilerParams(vmem_limit_bytes=58 << 20),
         cost_estimate=pl.CostEstimate(
             flops=16 * BLK * depth * width, bytes_accessed=16 * depth * width, transcendentals=0
         ),
         name="leave",
-    )(order, landed_x, landed_y, *shared)
+    )(order, landed_x, landed_y, *arrays)
 
 
 def place_kernel(shifts, own_x, own_y, from_x, from_y, out):
@@ -379,6 +401,8 @@
     if fast:
         w_one, w_two = hop(qkv_weight, 1), hop(qkv_weight, 2)
     normed = normalize(tokens, norm_gain, feature_order)
+    inside = (line_at == 1) | (line_at == 2)
+    flag = jnp.where(inside, 0, 1).astype(jnp.int32).reshape(1)
     table = tables(heads, reps, lines, rep_at, order, layout)
     slots = table[0].shape[1]
 
@@ -389,7 +413,7 @@
     if not fast:
         weight = lax.all_gather(qkv_weight, ("head", "rep"), axis=1, tiled=True)
         rows = gathered(normed, "line", lines)
-        landed = attend(pair_gather(by_head(enter(rows, [weight], heads)), reps), (lines,))
+        landed = attend(pair_gather(by_head(enter(flag, rows, [weight], [[(0, c)] for c in range(3)], heads)), reps), (lines,))
         out_pieces = [
             (s, h, 0, piece)
             for s, part in enumerate(gathered(out_weight, "line", lines))
@@ -400,7 +424,6 @@
         return columns.transpose(1, 2, 0, 3).reshape(BLK, -1)
 
     barrier = lax.optimization_barrier
-    inside = (line_at == 1) | (line_at == 2)
     middle, outward, inward = [(1, 2), (2, 1)], [(1, 0), (2, 3)], [(0, 1), (3, 2)]
 
     def along(part, pairs):
@@ -413,62 +436,46 @@
         width = part.shape[1] // 2
         return hop(part[:, :width], 2), hop(part[:, width:], 1)
 
-    def joined(part, halves):
-        return jnp.concatenate([part, *halves], axis=1)
-
     near, across = along(normed, xor_pairs(4, 1)), along(normed, middle)
-    w_pairs = [pair(qkv_weight)]
-    near, across, w_pairs[0], *table = barrier((near, across, w_pairs[0], *table))
-    crossed, second = along(near, middle), along(across, outward)
-    o_in = along(tie(out_weight, near), inward)
-    half = w_one.shape[1] // 2
-    onward = (w_two[:, :half], w_one[:, half:])
-    crossed, second, o_in, w_one, w_two, *onward = barrier((crossed, second, o_in, w_one, w_two, *onward))
+    w_others = [pair(qkv_weight)]
+    near, across, w_others[0], *table = barrier((near, across, w_others[0], *table))
+    second, crossed = along(across, outward), along(near, middle)
+    half = qkv_weight.shape[1] // 2
+    w_halves = [w_two[:, :half], w_one[:, half:]]
+    o_halves = share(tie(out_weight, w_one, w_two))
+    second, crossed, w_one, w_two, *halves = barrier((second, crossed, w_one, w_two, *w_halves, *o_halves))
+    w_halves, o_halves = halves[:2], halves[2:]
     third = along(crossed, outward)
-    w_first, w_other = hop(onward[0], 1), hop(onward[1], 2)
-    w_pairs += [pair(w) for w in (w_one, w_two)]
-    chunk = jnp.where(inside, across, second)
-    w_first, w_other, w_pairs[1], w_pairs[2], chunk = barrier((w_first, w_other, w_pairs[1], w_pairs[2], chunk))
-    w_pairs += [pair(w) for w in (w_first, w_other)]
-    o_own = tie(out_weight, w_first)
-    o_out = [along(o_own, outward)]
-    o_across = along(o_own, middle)
-    first_halves = share(o_own)
-    weights = [qkv_weight, w_one, w_two, w_first, w_other, *w_pairs]
-    early = enter([normed, near, chunk], weights, heads)
-    early, third, o_across, *first_halves = barrier((early, third, o_across, *first_halves))
-    o_crossed = along(o_in, middle)
-    o_out.append(along(o_across, outward))
-    early_heads = by_head(early)
-    late = enter([jnp.where(inside, crossed, third)], weights, heads)
-    early_heads, late, o_out[0], o_crossed = barrier((early_heads, late, o_out[0], o_crossed))
-    near_slot = jnp.where(inside, o_in, o_out[0])
-    near_halves = share(near_slot)
-    o_out.append(along(o_crossed, outward))
-    early_parts = pair_gather(early_heads, reps)
-    late_parts = pair_gather(by_head(late), reps)
-    early_parts[1], late_parts[1], o_out[1], *near_halves = barrier(
-        (early_parts[1], late_parts[1], o_out[1], *near_halves)
-    )
-    shared = [joined(o_own, first_halves), joined(near_slot, near_halves)]
-    attended = attention(early_parts + late_parts, *table, ((lines - 1, 1), reps, heads, heads * reps, slots))
-    second_slot = jnp.where(inside, o_across, o_out[1])
-    second_halves = share(second_slot)
-    attended, o_out[2], *second_halves = barrier((attended, o_out[2], *second_halves))
+    w_first, w_other = hop(w_halves[0], 1), hop(w_halves[1], 2)
+    w_others += [pair(w) for w in (w_one, w_two)]
+    w_first, w_other, *w_others = barrier((w_first, w_other, *w_others))
+    w_others += [pair(w) for w in (w_first, w_other)]
+    third, *w_others = barrier((third, *w_others))
+    o_own = tie(out_weight, third)
+    o_near, o_across = along(o_own, xor_pairs(4, 1)), along(o_own, middle)
+    weights = [qkv_weight, w_one, w_two, w_first, w_other, *w_others]
+    plan = [[(i, c) for i in range(len(weights))] for c in range(3)]
+    chunks = [normed, near, (across, second), (crossed, third)]
+    projected, o_near, o_across = barrier((enter(flag, chunks, weights, plan, heads), o_near, o_across))
+    mine = by_head(projected)
+    o_crossed, o_second = along(o_near, middle), along(o_across, outward)
+    mine, o_crossed, o_second = barrier((mine, o_crossed, o_second))
+    o_third = along(o_crossed, outward)
+    parts = pair_gather(mine, reps)
+    batch = jnp.concatenate([o_near, jnp.where(inside, o_across, o_second)], axis=0)
+    shared = [[out_weight, *o_halves], [batch, *share(batch)]]
+    attended = attention(parts, *table, ((lines,), reps, heads, heads * reps, slots))
+    attended, o_third, *shared[1] = barrier((attended, o_third, *shared[1]))
     landed = lax.all_to_all(attended, ("head", "line"), 0, 0, tiled=True)
-    shared.append(joined(second_slot, second_halves))
-    third_slot = jnp.where(inside, o_crossed, o_out[2])
-    others = [pair(batch) for batch in shared]
-    landed, *others = barrier((landed, *others))
+    last = jnp.where(inside, o_crossed, o_third)
+    shared.append([last, *share(last)])
+    landed, *others = barrier((landed, *(pair(piece) for pieces in shared for piece in pieces)))
+    shared = [pieces + others[3 * i : 3 * i + 3] for i, pieces in enumerate(shared)]
     landed_x, landed_y = hop(landed, 1), hop(landed, 2)
-    third_halves = share(third_slot)
-    shared.append(joined(third_slot, third_halves))
-    others.append(pair(shared[3]))
-    landed, landed_x, landed_y, others[3] = barrier((landed, landed_x, landed_y, others[3]))
-    shared = [batch for both in zip(shared, others) for batch in both]
+    own_x, own_y = leave(order, landed, landed, shared, heads, lines)
+    own_x, own_y, landed_x, landed_y = barrier((own_x, own_y, landed_x, landed_y))
+    to_x, to_y = leave(order, landed_x, landed_y, shared, heads, lines)
     shifts = jnp.stack([head_at, rep_at]).astype(jnp.int32)
-    to_x, to_y = leave(order, landed_x, landed_y, shared, heads, lines)
-    own_x, own_y = leave(order, landed, landed, shared, heads, lines)
     return place(shifts, own_x, own_y, hop(to_x, 1), hop(to_y, 2))
 
 

time: 217 us -> 202 us (0.931)
  waiting for transfers between devices: 80.2 us -> 98.5 us
  starting transfers between devices: 56.9 us -> 42.5 us
  local copies, waits for them, and re-layouts: 20.7 us -> 11 us
  other arithmetic: 12 us -> 7.05 us
  Pallas kernels: 45.6 us -> 41.3 us
    ppermute x16 -> x14, waiting for transfers between devices: 38.8 us -> 59.5 us  [hop(): return lax.ppermute(part, 'head', xor_pairs(4, bit))]
    ppermute x11 -> x10, starting transfers between devices: 23.9 us -> 12.8 us  [along(): return lax.ppermute(part, 'line', pairs)]
    all_to_all x2 -> x1, waiting for transfers between devices: 9.19 us -> 0.78 us  [by_head(): return lax.all_to_all(projected, 'head', 0, 0, tiled=True)]
    ppermute x11 -> x10, waiting for transfers between devices: 29.2 us -> 37.2 us  [along(): return lax.ppermute(part, 'line', pairs)]
    unnamed x53 -> x63, local copies, waits for them, and re-layouts: 9.52 us -> 4.73 us
    select_n x5 -> x2, other arithmetic: 6.96 us -> 2.23 us  [the longest x1 1.12 us: shards(): jnp.where(inside, o_across, o_second)]
    pallas_call x2 -> x1, Pallas kernels: 18.2 us -> 14.2 us  [enter(): pl.pallas_call(functools.partial(enter_kernel, heads, [len(chunk) for chu...]
    all_to_all x2 -> x1, starting transfers between devices: 6.99 us -> 3.57 us  [by_head(): return lax.all_to_all(projected, 'head', 0, 0, tiled=True)]
  transfers between devices with their start and end apart: 41 -> 41, of which waited for: 16 -> 20; matrix products, arithmetic and copies ran while one was open for 12% -> 7% of each run, Pallas kernels for 17% -> 16%
where the time goes in v3:
time: 202 us; the launch traced here: 201 us
  waiting for transfers between devices  98.5 us (49%)
  starting transfers between devices  42.5 us (21%)
  Pallas kernels  41.3 us (20%)
  local copies, waits for them, and re-layouts  11 us (5%)
  other arithmetic  7.05 us (3%)
    ppermute x14, waiting for transfers between devices, hop(): return lax.ppermute(part, 'head', xor_pairs(4, bit))  59.5 us
    ppermute x10, waiting for transfers between devices, along(): return lax.ppermute(part, 'line', pairs)  37.2 us
    ppermute x14, starting transfers between devices, hop(): return lax.ppermute(part, 'head', xor_pairs(4, bit))  18 us
    pallas_call x1, Pallas kernels, enter(): pl.pallas_call(functools.partial(enter_kernel, heads, [len(chunk) for chu...  14.2 us
    pallas_call x2, Pallas kernels, leave(): pl.pallas_call(functools.partial(leave_kernel, heads, lines, len(shared))...  13.5 us
    ppermute x10, starting transfers between devices, along(): return lax.ppermute(part, 'line', pairs)  12.8 us
    pallas_call x1, Pallas kernels, attention(): pl.pallas_call(functools.partial(attention_kernel, sizes), out_shape=jax....  10.9 us
    all_to_all x1, starting transfers between devices, shards(): landed = lax.all_to_all(attended, ('head', 'line'), 0, 0, tiled=True)  5.22 us
  transfers between devices with their start and end apart: 41, of which 20 were waited for; matrix products, arithmetic and copies ran while one was open for 7% of the time, Pallas kernels for 16%

profile of v3, /device:TPU:0, one launch (start us, length us, event | category | flops | bytes accessed | tf_op | source)
XLA Modules:
  0.0 201.0 jit_solution(9943268302231990796)
XLA Ops:
  0.1 1.2 copy-done.1
  1.3 0.7 copy-done.4
  2.0 1.1 normalize.1.refs_0_
  3.1 3.1 %collective-permute-start = (bf16[128,4096]{1,0:T(8,128)(2,1)S(1)}, bf16[128,4096]{1,0:T(8,128)(2,1)}, u32[]{:S(2)}, u32[]{:S(2)}) collective-permute-start(bf16[128,4096]{1,0:T(8,128)(2,1)S(1)} %normalize.1.refs_0_), channel_id=1, source_target_pairs={{0,1},{1,0},{2,3},{3,2},{4,5},{5,4},{6,7},{7,6},{8,9},{9,8},{10,11... | collective-permute-start | bytes 3145736 | tf_op jit(solution)/shard_map/ppermute | solution.py:430
  6.2 1.6 collective-permute-start.1
  7.9 1.5 collective-permute-start.5
  9.3 1.5 collective-permute-start.6
  10.9 0.7 dynamic-slice_bitcast_fusion.order
  12.1 0.6 gather_fusion
  12.8 0.7 iota_reduce_fusion
  13.5 0.6 fusion.11
  14.1 2.5 %fusion.6 = s32[32]{0:T(128)S(1)} fusion(s32[]{:T(128)} %bitcast.12, s32[]{:T(128)} %bitcast.13, s32[]{:T(128)} %bitcast.15, s32[]{:T(128)} %bitcast.14, s32[]{:T(128)} %axis_index.36), kind=kLoop, calls=%fused_computation.42 | loop fusion | flops 1504 | bytes 148 | tf_op jit(solution)/shard_map/add | solution.py:379
  16.6 2.4 %gather_fusion.1 = s32[288]{0:T(512)S(1)} fusion(s32[32]{0:T(128)S(1)} %fusion.6, s32[1024]{0:T(1024)S(1)} %pad_clamp_fusion), kind=kCustom, calls=%fused_computation.1 | custom fusion | bytes 3456 | tf_op jit(solution)/shard_map/gather | solution.py:383
  19.5 10.0 %collective-permute-done.refs_1_ = bf16[128,4096]{1,0:T(8,128)(2,1)} collective-permute-done((bf16[128,4096]{1,0:T(8,128)(2,1)S(1)}, bf16[128,4096]{1,0:T(8,128)(2,1)}, u32[]{:S(2)}, u32[]{:S(2)}) %collective-permute-start) | collective-permute-done | bytes 1048608 | tf_op jit(solution)/shard_map/ppermute | solution.py:430
  29.5 1.3 collective-permute-start.3
  30.8 0.7 collective-permute-start.4
  31.5 13.4 %collective-permute-done.5.refs_7_ = bf16[3,512,512]{2,1,0:T(8,128)(2,1)S(1)} collective-permute-done((bf16[3,512,512]{2,1,0:T(8,128)(2,1)}, bf16[3,512,512]{2,1,0:T(8,128)(2,1)S(1)}, u32[]{:S(2)}, u32[]{:S(2)}) %collective-permute-start.5) | collective-permute-done | bytes 1572896 | tf_op jit(solution)/shard_map/ppermute | solution.py:51
  44.9 1.3 collective-permute-done.6.refs_8_
  46.2 1.6 collective-permute-start.7
  47.8 0.5 collective-permute-start.8
  48.4 1.2 slice.41
  49.6 4.3 %collective-permute-done.7.refs_3_ = bf16[512,256]{1,0:T(8,128)(2,1)S(1)} collective-permute-done((bf16[512,256]{1,0:T(8,128)(2,1)S(1)}, bf16[512,256]{1,0:T(8,128)(2,1)S(1)}, u32[]{:S(2)}, u32[]{:S(2)}) %collective-permute-start.7) | collective-permute-done | bytes 262176 | tf_op jit(solution)/shard_map/ppermute | solution.py:51
  53.9 1.3 collective-permute-done.8.refs_4_
  55.3 2.7 %collective-permute-done.3.refs_3_ = bf16[128,4096]{1,0:T(8,128)(2,1)S(1)} collective-permute-done((bf16[128,4096]{1,0:T(8,128)(2,1)}, bf16[128,4096]{1,0:T(8,128)(2,1)S(1)}, u32[]{:S(2)}, u32[]{:S(2)}) %collective-permute-start.3) | collective-permute-done | bytes 1048608 | tf_op jit(solution)/shard_map/ppermute | solution.py:430
  58.6 1.5 collective-permute-start.10
  60.1 1.5 collective-permute-start.11
  61.6 1.3 collective-permute-start.9
  62.9 15.2 %collective-permute-done.10.refs_9_ = bf16[3,256,512]{2,1,0:T(8,128)(2,1)S(1)} collective-permute-done((bf16[3,256,512]{2,1,0:T(8,128)(2,1)S(1)}, bf16[3,256,512]{2,1,0:T(8,128)(2,1)S(1)}, u32[]{:S(2)}, u32[]{:S(2)}) %collective-permute-start.10) | collective-permute-done | bytes 786464 | tf_op jit(solution)/shard_map/ppermute | solution.py:51
  78.1 1.2 collective-permute-done.11.refs_10_
  79.9 9.4 %collective-permute-done.9.refs_5_ = bf16[128,4096]{1,0:T(8,128)(2,1)S(1)} collective-permute-done((bf16[128,4096]{1,0:T(8,128)(2,1)S(1)}, bf16[128,4096]{1,0:T(8,128)(2,1)S(1)}, u32[]{:S(2)}, u32[]{:S(2)}) %collective-permute-start.9) | collective-permute-done | bytes 1048608 | tf_op jit(solution)/shard_map/ppermute | solution.py:430
  89.5 0.8 copy-done.18
  90.3 0.7 collective-permute-start.17
  91.1 14.2 %enter.1 = bf16[4,3,4,128,128]{4,3,2,1,0:T(8,128)(2,1)} custom-call(s32[1]{0:T(128)} %bitcast.20.flag, bf16[128,4096]{1,0:T(8,128)(2,1)} %copy-done, bf16[128,4096]{1,0:T(8,128)(2,1)} %collective-permute-done.refs_1_, bf16[128,4096]{1,0:T(8,128)(2,1)} %collective-permute-done.1.refs_2_, bf16[128,4096]{1,0:T(8,128)(2,1)} %copy-done.16, ...), custom_call_target="tpu_custom_call" | custom-call | flops 1 | bytes 1 | tf_op jit(solution)/shard_map/enter/pallas_call | solution.py:270
  105.3 3.6 %all-to-all-start = ((bf16[4,3,4,128,128]{4,3,2,1,0:T(8,128)(2,1)}), bf16[4,3,4,128,128]{4,3,2,1,0:T(8,128)(2,1)S(1)}, u32[]{:S(2)}, u32[]{:S(2)}) async-start(bf16[4,3,4,128,128]{4,3,2,1,0:T(8,128)(2,1)} %enter.1), calls=%async_computation | async-start | bytes 3145728 | tf_op jit(solution)/shard_map/all_to_all | solution.py:369
  108.9 1.5 collective-permute-start.18
  110.4 1.3 collective-permute-start.19
  111.7 15.0 %collective-permute-done.19 = bf16[512,512]{1,0:T(8,128)(2,1)} collective-permute-done((bf16[512,512]{1,0:T(8,128)(2,1)S(1)}, bf16[512,512]{1,0:T(8,128)(2,1)}, u32[]{:S(2)}, u32[]{:S(2)}) %collective-permute-start.19) | collective-permute-done | bytes 524320 | tf_op jit(solution)/shard_map/ppermute | solution.py:430
  126.7 0.8 all-to-all-done.refs_0_
  127.5 1.3 collective-permute-start.21
  128.8 1.1 broadcast_select_fusion.1
  130.0 1.5 collective-permute-start.22
  131.5 0.9 collective-permute-start.23
  132.5 1.1 pad_maximum_fusion.refs_8_
  133.6 0.6 collective-permute-start.25
  134.2 10.9 %attention.1 = bf16[16,128,128]{2,1,0:T(8,128)(2,1)} custom-call(s32[16,18]{1,0:T(8,128)S(1)} %reshape.188.places, f32[16,18]{1,0:T(8,128)S(1)} %concatenate.31.biases, f32[16]{0:T(128)S(1)} %convert_add_fusion.copies, s32[16]{0:T(128)S(1)} %add.189.targets, bf16[4,3,4,128,128]{4,3,2,1,0:T(8,128)(2,1)S(1)} %all-to-all-done.refs_0_, ...), custom_call_target="tpu_custom_call" | custom-call | flops 2415919104 | bytes 4194304 | tf_op jit(solution)/shard_map/attention/pallas_call | solution.py:150
  145.7 5.2 %all-to-all-start.1 = ((bf16[16,128,128]{2,1,0:T(8,128)(2,1)}), bf16[16,128,128]{2,1,0:T(8,128)(2,1)S(1)}, u32[]{:S(2)}, u32[]{:S(2)}) async-start(bf16[16,128,128]{2,1,0:T(8,128)(2,1)} %attention.1), calls=%async_computation.1 | async-start | bytes 1048576 | tf_op jit(solution)/shard_map/all_to_all | solution.py:469
  151.0 1.1 broadcast_select_fusion.refs_14_
  152.2 2.0 collective-permute-start.31
  154.7 1.5 collective-permute-start.33
  156.1 8.2 %collective-permute-done.31.refs_15_ = bf16[512,256]{1,0:T(8,128)(2,1)S(1)} collective-permute-done((bf16[512,256]{1,0:T(8,128)(2,1)S(1)}, bf16[512,256]{1,0:T(8,128)(2,1)S(1)}, u32[]{:S(2)}, u32[]{:S(2)}) %collective-permute-start.31) | collective-permute-done | bytes 262176 | tf_op jit(solution)/shard_map/ppermute | solution.py:51
  164.4 0.9 collective-permute-done.33.refs_16_
  166.3 0.6 collective-permute-done.32.refs_18_
  167.1 0.7 copy-done.22
  167.8 2.2 %collective-permute-start.35 = (bf16[16,128,128]{2,1,0:T(8,128)(2,1)S(1)}, bf16[16,128,128]{2,1,0:T(8,128)(2,1)S(1)}, u32[]{:S(2)}, u32[]{:S(2)}) collective-permute-start(bf16[16,128,128]{2,1,0:T(8,128)(2,1)S(1)} %all-to-all-done.1.refs_0_.refs_1_), channel_id=1, source_target_pairs={{0,8},{8,0},{16,24},{24,16},{1,9},{9,1},{17,25},{25,17},{2,10},{10... | collective-permute-start | bytes 1572872 | tf_op jit(solution)/shard_map/ppermute | solution.py:51
  170.1 0.6 collective-permute-start.36
  170.7 6.8 %leave.2 = (bf16[128,1024]{1,0:T(8,128)(2,1)}, bf16[128,1024]{1,0:T(8,128)(2,1)}) custom-call(s32[4]{0:T(128)} %copy-done.30, bf16[16,128,128]{2,1,0:T(8,128)(2,1)} %copy-done.8, bf16[16,128,128]{2,1,0:T(8,128)(2,1)} %copy-done.8, bf16[512,512]{1,0:T(8,128)(2,1)} %refs_2_.3, bf16[512,256]{1,0:T(8,128)(2,1)} %copy-done.19, ...), custom_call_target="tpu_custom_call" | custom-call | flops 1073741824 | bytes 8388608 | tf_op jit(solution)/shard_map/leave/pallas_call | solution.py:327
  177.4 4.8 %collective-permute-done.35.refs_0_ = bf16[16,128,128]{2,1,0:T(8,128)(2,1)S(1)} collective-permute-done((bf16[16,128,128]{2,1,0:T(8,128)(2,1)S(1)}, bf16[16,128,128]{2,1,0:T(8,128)(2,1)S(1)}, u32[]{:S(2)}, u32[]{:S(2)}) %collective-permute-start.35) | collective-permute-done | bytes 524320 | tf_op jit(solution)/shard_map/ppermute | solution.py:51
  182.3 1.5 collective-permute-done.36.refs_1_
  183.7 0.8 copy-done.28
  184.6 6.8 %leave.3 = (bf16[128,1024]{1,0:T(8,128)(2,1)}, bf16[128,1024]{1,0:T(8,128)(2,1)}) custom-call(s32[4]{0:T(128)} %copy-done.30, bf16[16,128,128]{2,1,0:T(8,128)(2,1)} %copy-done.27, bf16[16,128,128]{2,1,0:T(8,128)(2,1)} %copy-done.28, bf16[512,512]{1,0:T(8,128)(2,1)} %refs_2_.3, bf16[512,256]{1,0:T(8,128)(2,1)} %copy-done.19, ...), custom_call_target="tpu_custom_call" | custom-call | flops 1073741824 | bytes 8388608 | tf_op jit(solution)/shard_map/leave/pallas_call | solution.py:327
  191.3 0.5 collective-permute-start.37
  191.9 0.6 collective-permute-start.38
  192.6 6.3 %collective-permute-done.37.from_x = bf16[128,1024]{1,0:T(8,128)(2,1)S(1)} collective-permute-done((bf16[128,1024]{1,0:T(8,128)(2,1)}, bf16[128,1024]{1,0:T(8,128)(2,1)S(1)}, u32[]{:S(2)}, u32[]{:S(2)}) %collective-permute-start.37) | collective-permute-done | bytes 262176 | tf_op jit(solution)/shard_map/ppermute | solution.py:51
  199.3 1.6 place.1
  (121 shorter events, 5.8 us)
Async XLA Ops:
  0.0 12.0 %copy-start.29 = (s32[32,16]{0,1:T(8,128)S(1)}, s32[32,16]{0,1:T(8,128)}, u32[]{:S(2)}) copy-start(s32[32,16]{0,1:T(8,128)} %param.10) | copy-start | bytes 6148
  3.1 15.8 %copy-start = (bf16[128,4096]{1,0:T(8,128)(2,1)}, bf16[128,4096]{1,0:T(8,128)(2,1)S(1)}, u32[]{:S(2)}) copy-start(bf16[128,4096]{1,0:T(8,128)(2,1)S(1)} %normalize.1.refs_0_) | copy-start | bytes 3145732
  3.1 26.4 %collective-permute-start = (bf16[128,4096]{1,0:T(8,128)(2,1)S(1)}, bf16[128,4096]{1,0:T(8,128)(2,1)}, u32[]{:S(2)}, u32[]{:S(2)}) collective-permute-start(bf16[128,4096]{1,0:T(8,128)(2,1)S(1)} %normalize.1.refs_0_), channel_id=1, source_target_pairs={{0,1},{1,0},{2,3},{3,2},{4,5},{5,4},{6,7},{7,6},{8,9},{9,8},{10,11... | collective-permute-start | bytes 3145736 | tf_op jit(solution)/shard_map/ppermute | solution.py:430
  6.2 23.3 %collective-permute-start.1 = (bf16[128,4096]{1,0:T(8,128)(2,1)S(1)}, bf16[128,4096]{1,0:T(8,128)(2,1)}, u32[]{:S(2)}, u32[]{:S(2)}) collective-permute-start(bf16[128,4096]{1,0:T(8,128)(2,1)S(1)} %normalize.1.refs_0_), channel_id=1, source_target_pairs={{1,2},{2,1},{5,6},{6,5},{9,10},{10,9},{13,14},{14,13},{17,18},{18,... | collective-permute-start | bytes 3145736 | tf_op jit(solution)/shard_map/ppermute | solution.py:430
  7.9 21.6 %collective-permute-start.2 = (bf16[3,512,512]{2,1,0:T(8,128)(2,1)}, bf16[3,512,512]{2,1,0:T(8,128)(2,1)}, u32[]{:S(2)}, u32[]{:S(2)}) collective-permute-start(bf16[3,512,512]{2,1,0:T(8,128)(2,1)} %refs_6_.1), channel_id=1, source_target_pairs={{0,4},{4,0},{1,5},{5,1},{2,6},{6,2},{3,7},{7,3},{8,12},{12,8},{9,1... | collective-permute-start | bytes 4718600 | tf_op jit(solution)/shard_map/ppermute | solution.py:433
  7.9 37.0 %collective-permute-start.5 = (bf16[3,512,512]{2,1,0:T(8,128)(2,1)}, bf16[3,512,512]{2,1,0:T(8,128)(2,1)S(1)}, u32[]{:S(2)}, u32[]{:S(2)}) collective-permute-start(bf16[3,512,512]{2,1,0:T(8,128)(2,1)} %refs_6_.1), channel_id=1, source_target_pairs={{0,8},{8,0},{16,24},{24,16},{1,9},{9,1},{17,25},{25,17},{2,10},{10... | collective-permute-start | bytes 4718600 | tf_op jit(solution)/shard_map/ppermute | solution.py:51
  9.3 36.8 %collective-permute-start.6 = (bf16[3,512,512]{2,1,0:T(8,128)(2,1)}, bf16[3,512,512]{2,1,0:T(8,128)(2,1)}, u32[]{:S(2)}, u32[]{:S(2)}) collective-permute-start(bf16[3,512,512]{2,1,0:T(8,128)(2,1)} %refs_6_.1), channel_id=1, source_target_pairs={{0,16},{8,24},{16,0},{24,8},{1,17},{9,25},{17,1},{25,9},{2,18},{10... | collective-permute-start | bytes 4718600 | tf_op jit(solution)/shard_map/ppermute | solution.py:51
  11.6 7.4 %copy-start.30 = (s32[4]{0:T(128)}, s32[4]{0:T(128)S(1)}, u32[]{:S(2)}) copy-start(s32[4]{0:T(128)S(1)} %dynamic-slice_bitcast_fusion.order) | copy-start | bytes 52
  16.6 29.6 %copy-start.7 = (bf16[512,512]{1,0:T(8,128)(2,1)S(1)}, bf16[512,512]{1,0:T(8,128)(2,1)}, u32[]{:S(2)}) copy-start(bf16[512,512]{1,0:T(8,128)(2,1)} %refs_2_.3) | copy-start | bytes 1572868
  29.5 28.5 %collective-permute-start.3 = (bf16[128,4096]{1,0:T(8,128)(2,1)}, bf16[128,4096]{1,0:T(8,128)(2,1)S(1)}, u32[]{:S(2)}, u32[]{:S(2)}) collective-permute-start(bf16[128,4096]{1,0:T(8,128)(2,1)} %collective-permute-done.1.refs_2_), channel_id=1, source_target_pairs={{1,0},{2,3},{5,4},{6,7},{9,8},{10,11},{13,12},{14,15},{17,16},{18,... | collective-permute-start | bytes 3145736 | tf_op jit(solution)/shard_map/ppermute | solution.py:430
  30.8 27.2 %collective-permute-start.4 = (bf16[128,4096]{1,0:T(8,128)(2,1)}, bf16[128,4096]{1,0:T(8,128)(2,1)S(1)}, u32[]{:S(2)}, u32[]{:S(2)}) collective-permute-start(bf16[128,4096]{1,0:T(8,128)(2,1)} %collective-permute-done.refs_1_), channel_id=1, source_target_pairs={{1,2},{2,1},{5,6},{6,5},{9,10},{10,9},{13,14},{14,13},{17,18},{18,... | collective-permute-start | bytes 3145736 | tf_op jit(solution)/shard_map/ppermute | solution.py:430
  44.9 13.1 %copy-start.9 = (bf16[3,512,512]{2,1,0:T(8,128)(2,1)}, bf16[3,512,512]{2,1,0:T(8,128)(2,1)S(1)}, u32[]{:S(2)}) copy-start(bf16[3,512,512]{2,1,0:T(8,128)(2,1)S(1)} %collective-permute-done.5.refs_7_) | copy-start | bytes 4718596
  46.2 7.7 %collective-permute-start.7 = (bf16[512,256]{1,0:T(8,128)(2,1)S(1)}, bf16[512,256]{1,0:T(8,128)(2,1)S(1)}, u32[]{:S(2)}, u32[]{:S(2)}) collective-permute-start(bf16[512,256]{1,0:T(8,128)(2,1)S(1)} %get-tuple-element.126), channel_id=1, source_target_pairs={{0,16},{8,24},{16,0},{24,8},{1,17},{9,25},{17,1},{25,9},{2,18},{10... | collective-permute-start | bytes 786440 | tf_op jit(solution)/shard_map/ppermute | solution.py:51
  47.8 7.4 %collective-permute-start.8 = (bf16[512,256]{1,0:T(8,128)(2,1)S(1)}, bf16[512,256]{1,0:T(8,128)(2,1)}, u32[]{:S(2)}, u32[]{:S(2)}) collective-permute-start(bf16[512,256]{1,0:T(8,128)(2,1)S(1)} %get-tuple-element.125), channel_id=1, source_target_pairs={{0,8},{8,0},{16,24},{24,16},{1,9},{9,1},{17,25},{25,17},{2,10},{10... | collective-permute-start | bytes 786440 | tf_op jit(solution)/shard_map/ppermute | solution.py:51
  53.9 79.7 %copy-start.19 = (bf16[512,256]{1,0:T(8,128)(2,1)}, bf16[512,256]{1,0:T(8,128)(2,1)S(1)}, u32[]{:S(2)}) copy-start(bf16[512,256]{1,0:T(8,128)(2,1)S(1)} %collective-permute-done.7.refs_3_) | copy-start | bytes 786436
  58.0 31.3 %copy-start.16 = (bf16[128,4096]{1,0:T(8,128)(2,1)}, bf16[128,4096]{1,0:T(8,128)(2,1)S(1)}, u32[]{:S(2)}) copy-start(bf16[128,4096]{1,0:T(8,128)(2,1)S(1)} %collective-permute-done.3.refs_3_) | copy-start | bytes 3145732
  58.0 31.5 %copy-start.17 = (bf16[128,4096]{1,0:T(8,128)(2,1)}, bf16[128,4096]{1,0:T(8,128)(2,1)S(1)}, u32[]{:S(2)}) copy-start(bf16[128,4096]{1,0:T(8,128)(2,1)S(1)} %collective-permute-done.4.refs_4_) | copy-start | bytes 3145732
  58.0 21.3 %collective-permute-start.12 = (bf16[3,512,512]{2,1,0:T(8,128)(2,1)S(1)}, bf16[3,512,512]{2,1,0:T(8,128)(2,1)S(1)}, u32[]{:S(2)}, u32[]{:S(2)}) collective-permute-start(bf16[3,512,512]{2,1,0:T(8,128)(2,1)S(1)} %collective-permute-done.5.refs_7_), channel_id=1, source_target_pairs={{0,4},{4,0},{1,5},{5,1},{2,6},{6,2},{3,7},{7,3},{8,12},{12,8},{9,1... | collective-permute-start | bytes 4718600 | tf_op jit(solution)/shard_map/ppermute | solution.py:433
  58.1 21.2 %collective-permute-start.13 = (bf16[3,512,512]{2,1,0:T(8,128)(2,1)}, bf16[3,512,512]{2,1,0:T(8,128)(2,1)S(1)}, u32[]{:S(2)}, u32[]{:S(2)}) collective-permute-start(bf16[3,512,512]{2,1,0:T(8,128)(2,1)} %collective-permute-done.6.refs_8_), channel_id=1, source_target_pairs={{0,4},{4,0},{1,5},{5,1},{2,6},{6,2},{3,7},{7,3},{8,12},{12,8},{9,1... | collective-permute-start | bytes 4718600 | tf_op jit(solution)/shard_map/ppermute | solution.py:433
  58.6 19.5 %collective-permute-start.10 = (bf16[3,256,512]{2,1,0:T(8,128)(2,1)S(1)}, bf16[3,256,512]{2,1,0:T(8,128)(2,1)S(1)}, u32[]{:S(2)}, u32[]{:S(2)}) collective-permute-start(bf16[3,256,512]{2,1,0:T(8,128)(2,1)S(1)} %slice.41), channel_id=1, source_target_pairs={{0,8},{8,0},{16,24},{24,16},{1,9},{9,1},{17,25},{25,17},{2,10},{10... | collective-permute-start | bytes 2359304 | tf_op jit(solution)/shard_map/ppermute | solution.py:51
  60.1 19.2 %collective-permute-start.11 = (bf16[3,256,512]{2,1,0:T(8,128)(2,1)S(1)}, bf16[3,256,512]{2,1,0:T(8,128)(2,1)S(1)}, u32[]{:S(2)}, u32[]{:S(2)}) collective-permute-start(bf16[3,256,512]{2,1,0:T(8,128)(2,1)S(1)} %slice.42), channel_id=1, source_target_pairs={{0,16},{8,24},{16,0},{24,8},{1,17},{9,25},{17,1},{25,9},{2,18},{10... | collective-permute-start | bytes 2359304 | tf_op jit(solution)/shard_map/ppermute | solution.py:51
  61.6 27.7 %collective-permute-start.9 = (bf16[128,4096]{1,0:T(8,128)(2,1)S(1)}, bf16[128,4096]{1,0:T(8,128)(2,1)S(1)}, u32[]{:S(2)}, u32[]{:S(2)}) collective-permute-start(bf16[128,4096]{1,0:T(8,128)(2,1)S(1)} %collective-permute-done.4.refs_4_), channel_id=1, source_target_pairs={{1,0},{2,3},{5,4},{6,7},{9,8},{10,11},{13,12},{14,15},{17,16},{18,... | collective-permute-start | bytes 3145736 | tf_op jit(solution)/shard_map/ppermute | solution.py:430
  78.1 11.4 %copy-start.23 = (bf16[3,256,512]{2,1,0:T(8,128)(2,1)}, bf16[3,256,512]{2,1,0:T(8,128)(2,1)S(1)}, u32[]{:S(2)}) copy-start(bf16[3,256,512]{2,1,0:T(8,128)(2,1)S(1)} %collective-permute-done.10.refs_9_) | copy-start | bytes 2359300
  79.3 10.2 %copy-start.24 = (bf16[3,256,512]{2,1,0:T(8,128)(2,1)}, bf16[3,256,512]{2,1,0:T(8,128)(2,1)S(1)}, u32[]{:S(2)}) copy-start(bf16[3,256,512]{2,1,0:T(8,128)(2,1)S(1)} %collective-permute-done.11.refs_10_) | copy-start | bytes 2359300
  79.3 10.0 %copy-start.14 = (bf16[3,512,512]{2,1,0:T(8,128)(2,1)}, bf16[3,512,512]{2,1,0:T(8,128)(2,1)S(1)}, u32[]{:S(2)}) copy-start(bf16[3,512,512]{2,1,0:T(8,128)(2,1)S(1)} %collective-permute-done.12.refs_12_) | copy-start | bytes 4718596
  79.3 10.2 %copy-start.15 = (bf16[3,512,512]{2,1,0:T(8,128)(2,1)}, bf16[3,512,512]{2,1,0:T(8,128)(2,1)S(1)}, u32[]{:S(2)}) copy-start(bf16[3,512,512]{2,1,0:T(8,128)(2,1)S(1)} %collective-permute-done.13.refs_13_) | copy-start | bytes 4718596
  79.3 10.0 %collective-permute-start.14 = (bf16[3,256,512]{2,1,0:T(8,128)(2,1)S(1)}, bf16[3,256,512]{2,1,0:T(8,128)(2,1)S(1)}, u32[]{:S(2)}, u32[]{:S(2)}) collective-permute-start(bf16[3,256,512]{2,1,0:T(8,128)(2,1)S(1)} %collective-permute-done.10.refs_9_), channel_id=1, source_target_pairs={{0,4},{4,0},{1,5},{5,1},{2,6},{6,2},{3,7},{7,3},{8,12},{12,8},{9,1... | collective-permute-start | bytes 2359304 | tf_op jit(solution)/shard_map/ppermute | solution.py:433
  79.4 9.9 %collective-permute-start.15 = (bf16[3,256,512]{2,1,0:T(8,128)(2,1)S(1)}, bf16[3,256,512]{2,1,0:T(8,128)(2,1)S(1)}, u32[]{:S(2)}, u32[]{:S(2)}) collective-permute-start(bf16[3,256,512]{2,1,0:T(8,128)(2,1)S(1)} %collective-permute-done.11.refs_10_), channel_id=1, source_target_pairs={{0,4},{4,0},{1,5},{5,1},{2,6},{6,2},{3,7},{7,3},{8,12},{12,8},{9,1... | collective-permute-start | bytes 2359304 | tf_op jit(solution)/shard_map/ppermute | solution.py:433
  89.3 1.7 copy-start.25
  89.4 15.9 %collective-permute-start.16 = (bf16[512,512]{1,0:T(8,128)(2,1)S(1)}, bf16[512,512]{1,0:T(8,128)(2,1)S(1)}, u32[]{:S(2)}, u32[]{:S(2)}) collective-permute-start(bf16[512,512]{1,0:T(8,128)(2,1)S(1)} %copy-done.7), channel_id=1, source_target_pairs={{0,1},{1,0},{2,3},{3,2},{4,5},{5,4},{6,7},{7,6},{8,9},{9,8},{10,11... | collective-permute-start | bytes 1572872 | tf_op jit(solution)/shard_map/ppermute | solution.py:430
  90.3 15.0 %collective-permute-start.17 = (bf16[512,512]{1,0:T(8,128)(2,1)S(1)}, bf16[512,512]{1,0:T(8,128)(2,1)S(1)}, u32[]{:S(2)}, u32[]{:S(2)}) collective-permute-start(bf16[512,512]{1,0:T(8,128)(2,1)S(1)} %copy-done.7), channel_id=1, source_target_pairs={{1,2},{2,1},{5,6},{6,5},{9,10},{10,9},{13,14},{14,13},{17,18},{18,... | collective-permute-start | bytes 1572872 | tf_op jit(solution)/shard_map/ppermute | solution.py:430
  105.3 27.1 %copy-start.13 = (bf16[512,512]{1,0:T(8,128)(2,1)}, bf16[512,512]{1,0:T(8,128)(2,1)S(1)}, u32[]{:S(2)}) copy-start(bf16[512,512]{1,0:T(8,128)(2,1)S(1)} %collective-permute-done.16) | copy-start | bytes 1572868
  105.3 22.2 %all-to-all-start = ((bf16[4,3,4,128,128]{4,3,2,1,0:T(8,128)(2,1)}), bf16[4,3,4,128,128]{4,3,2,1,0:T(8,128)(2,1)S(1)}, u32[]{:S(2)}, u32[]{:S(2)}) async-start(bf16[4,3,4,128,128]{4,3,2,1,0:T(8,128)(2,1)} %enter.1), calls=%async_computation | async-start | bytes 3145728 | tf_op jit(solution)/shard_map/all_to_all | solution.py:369
  108.9 2.8 %collective-permute-start.18 = (bf16[512,512]{1,0:T(8,128)(2,1)S(1)}, bf16[512,512]{1,0:T(8,128)(2,1)}, u32[]{:S(2)}, u32[]{:S(2)}) collective-permute-start(bf16[512,512]{1,0:T(8,128)(2,1)S(1)} %collective-permute-done.16), channel_id=1, source_target_pairs={{1,2},{2,1},{5,6},{6,5},{9,10},{10,9},{13,14},{14,13},{17,18},{18,... | collective-permute-start | bytes 1572872 | tf_op jit(solution)/shard_map/ppermute | solution.py:430
  110.4 16.3 %collective-permute-start.19 = (bf16[512,512]{1,0:T(8,128)(2,1)S(1)}, bf16[512,512]{1,0:T(8,128)(2,1)}, u32[]{:S(2)}, u32[]{:S(2)}) collective-permute-start(bf16[512,512]{1,0:T(8,128)(2,1)S(1)} %collective-permute-done.17), channel_id=1, source_target_pairs={{1,0},{2,3},{5,4},{6,7},{9,8},{10,11},{13,12},{14,15},{17,16},{18,... | collective-permute-start | bytes 1572872 | tf_op jit(solution)/shard_map/ppermute | solution.py:430
  127.5 6.1 %collective-permute-start.20 = (bf16[4,3,4,128,128]{4,3,2,1,0:T(8,128)(2,1)S(1)}, bf16[4,3,4,128,128]{4,3,2,1,0:T(8,128)(2,1)S(1)}, u32[]{:S(2)}, u32[]{:S(2)}) collective-permute-start(bf16[4,3,4,128,128]{4,3,2,1,0:T(8,128)(2,1)S(1)} %all-to-all-done.refs_0_), channel_id=1, source_target_pairs={{0,4},{4,0},{1,5},{5,1},{2,6},{6,2},{3,7},{7,3},{8,12},{12,8},{9,1... | collective-permute-start | bytes 4718600 | tf_op jit(solution)/shard_map/ppermute | solution.py:47
  127.5 17.6 %collective-permute-start.21 = (bf16[512,512]{1,0:T(8,128)(2,1)}, bf16[512,512]{1,0:T(8,128)(2,1)}, u32[]{:S(2)}, u32[]{:S(2)}) collective-permute-start(bf16[512,512]{1,0:T(8,128)(2,1)} %collective-permute-done.18), channel_id=1, source_target_pairs={{1,0},{2,3},{5,4},{6,7},{9,8},{10,11},{13,12},{14,15},{17,16},{18,... | collective-permute-start | bytes 1572872 | tf_op jit(solution)/shard_map/ppermute | solution.py:430
  130.0 15.2 %collective-permute-start.22 = (bf16[1024,256]{1,0:T(8,128)(2,1)S(1)}, bf16[1024,256]{1,0:T(8,128)(2,1)}, u32[]{:S(2)}, u32[]{:S(2)}) collective-permute-start(bf16[1024,256]{1,0:T(8,128)(2,1)S(1)} %get-tuple-element.122), channel_id=1, source_target_pairs={{0,16},{8,24},{16,0},{24,8},{1,17},{9,25},{17,1},{25,9},{2,18},{10... | collective-permute-start | bytes 1572872 | tf_op jit(solution)/shard_map/ppermute | solution.py:51
  131.5 14.2 %collective-permute-start.23 = (bf16[1024,256]{1,0:T(8,128)(2,1)S(1)}, bf16[1024,256]{1,0:T(8,128)(2,1)}, u32[]{:S(2)}, u32[]{:S(2)}) collective-permute-start(bf16[1024,256]{1,0:T(8,128)(2,1)S(1)} %get-tuple-element.121), channel_id=1, source_target_pairs={{0,8},{8,0},{16,24},{24,16},{1,9},{9,1},{17,25},{25,17},{2,10},{10... | collective-permute-start | bytes 1572872 | tf_op jit(solution)/shard_map/ppermute | solution.py:51
  132.4 21.7 %collective-permute-start.24 = (bf16[512,512]{1,0:T(8,128)(2,1)S(1)}, bf16[512,512]{1,0:T(8,128)(2,1)}, u32[]{:S(2)}, u32[]{:S(2)}) collective-permute-start(bf16[512,512]{1,0:T(8,128)(2,1)S(1)} %copy-done.7), channel_id=1, source_target_pairs={{0,4},{4,0},{1,5},{5,1},{2,6},{6,2},{3,7},{7,3},{8,12},{12,8},{9,1... | collective-permute-start | bytes 1572872 | tf_op jit(solution)/shard_map/ppermute | solution.py:433
  133.6 17.3 %copy-start.5 = (bf16[1024,512]{1,0:T(8,128)(2,1)}, bf16[1024,512]{1,0:T(8,128)(2,1)S(1)}, u32[]{:S(2)}) copy-start(bf16[1024,512]{1,0:T(8,128)(2,1)S(1)} %pad_maximum_fusion.refs_8_) | copy-start | bytes 3145732
  133.6 20.8 %collective-permute-start.25 = (bf16[512,256]{1,0:T(8,128)(2,1)S(1)}, bf16[512,256]{1,0:T(8,128)(2,1)}, u32[]{:S(2)}, u32[]{:S(2)}) collective-permute-start(bf16[512,256]{1,0:T(8,128)(2,1)S(1)} %collective-permute-done.7.refs_3_), channel_id=1, source_target_pairs={{0,4},{4,0},{1,5},{5,1},{2,6},{6,2},{3,7},{7,3},{8,12},{12,8},{9,1... | collective-permute-start | bytes 786440 | tf_op jit(solution)/shard_map/ppermute | solution.py:433
  145.1 9.6 %collective-permute-start.26 = (bf16[512,256]{1,0:T(8,128)(2,1)}, bf16[512,256]{1,0:T(8,128)(2,1)}, u32[]{:S(2)}, u32[]{:S(2)}) collective-permute-start(bf16[512,256]{1,0:T(8,128)(2,1)} %collective-permute-done.8.refs_4_), channel_id=1, source_target_pairs={{0,4},{4,0},{1,5},{5,1},{2,6},{6,2},{3,7},{7,3},{8,12},{12,8},{9,1... | collective-permute-start | bytes 786440 | tf_op jit(solution)/shard_map/ppermute | solution.py:433
  145.7 22.1 %all-to-all-start.1 = ((bf16[16,128,128]{2,1,0:T(8,128)(2,1)}), bf16[16,128,128]{2,1,0:T(8,128)(2,1)S(1)}, u32[]{:S(2)}, u32[]{:S(2)}) async-start(bf16[16,128,128]{2,1,0:T(8,128)(2,1)} %attention.1), calls=%async_computation.1 | async-start | bytes 1048576 | tf_op jit(solution)/shard_map/all_to_all | solution.py:469
  150.9 16.9 %collective-permute-start.27 = (bf16[1024,512]{1,0:T(8,128)(2,1)S(1)}, bf16[1024,512]{1,0:T(8,128)(2,1)}, u32[]{:S(2)}, u32[]{:S(2)}) collective-permute-start(bf16[1024,512]{1,0:T(8,128)(2,1)S(1)} %pad_maximum_fusion.refs_8_), channel_id=1, source_target_pairs={{0,4},{4,0},{1,5},{5,1},{2,6},{6,2},{3,7},{7,3},{8,12},{12,8},{9,1... | collective-permute-start | bytes 3145736 | tf_op jit(solution)/shard_map/ppermute | solution.py:433
  152.1 18.5 %copy-start.6 = (bf16[512,512]{1,0:T(8,128)(2,1)}, bf16[512,512]{1,0:T(8,128)(2,1)S(1)}, u32[]{:S(2)}) copy-start(bf16[512,512]{1,0:T(8,128)(2,1)S(1)} %broadcast_select_fusion.refs_14_) | copy-start | bytes 1572868
  152.2 12.2 %collective-permute-start.31 = (bf16[512,256]{1,0:T(8,128)(2,1)S(1)}, bf16[512,256]{1,0:T(8,128)(2,1)S(1)}, u32[]{:S(2)}, u32[]{:S(2)}) collective-permute-start(bf16[512,256]{1,0:T(8,128)(2,1)S(1)} %get-tuple-element.124), channel_id=1, source_target_pairs={{0,16},{8,24},{16,0},{24,8},{1,17},{9,25},{17,1},{25,9},{2,18},{10... | collective-permute-start | bytes 786440 | tf_op jit(solution)/shard_map/ppermute | solution.py:51
  154.2 11.1 %collective-permute-start.28 = (bf16[1024,256]{1,0:T(8,128)(2,1)}, bf16[1024,256]{1,0:T(8,128)(2,1)S(1)}, u32[]{:S(2)}, u32[]{:S(2)}) collective-permute-start(bf16[1024,256]{1,0:T(8,128)(2,1)} %collective-permute-done.22.refs_9_), channel_id=1, source_target_pairs={{0,4},{4,0},{1,5},{5,1},{2,6},{6,2},{3,7},{7,3},{8,12},{12,8},{9,1... | collective-permute-start | bytes 1572872 | tf_op jit(solution)/shard_map/ppermute | solution.py:433
  154.4 11.5 %collective-permute-start.29 = (bf16[1024,256]{1,0:T(8,128)(2,1)}, bf16[1024,256]{1,0:T(8,128)(2,1)S(1)}, u32[]{:S(2)}, u32[]{:S(2)}) collective-permute-start(bf16[1024,256]{1,0:T(8,128)(2,1)} %collective-permute-done.23.refs_10_), channel_id=1, source_target_pairs={{0,4},{4,0},{1,5},{5,1},{2,6},{6,2},{3,7},{7,3},{8,12},{12,8},{9,1... | collective-permute-start | bytes 1572872 | tf_op jit(solution)/shard_map/ppermute | solution.py:433
  154.7 10.6 %collective-permute-start.33 = (bf16[512,256]{1,0:T(8,128)(2,1)S(1)}, bf16[512,256]{1,0:T(8,128)(2,1)S(1)}, u32[]{:S(2)}, u32[]{:S(2)}) collective-permute-start(bf16[512,256]{1,0:T(8,128)(2,1)S(1)} %get-tuple-element.123), channel_id=1, source_target_pairs={{0,8},{8,0},{16,24},{24,16},{1,9},{9,1},{17,25},{25,17},{2,10},{10... | collective-permute-start | bytes 786440 | tf_op jit(solution)/shard_map/ppermute | solution.py:51
  164.4 2.5 %copy-start.20 = (bf16[512,256]{1,0:T(8,128)(2,1)}, bf16[512,256]{1,0:T(8,128)(2,1)S(1)}, u32[]{:S(2)}) copy-start(bf16[512,256]{1,0:T(8,128)(2,1)S(1)} %collective-permute-done.31.refs_15_) | copy-start | bytes 786436
  164.4 1.9 collective-permute-start.30
  165.3 5.4 %copy-start.21 = (bf16[512,256]{1,0:T(8,128)(2,1)}, bf16[512,256]{1,0:T(8,128)(2,1)S(1)}, u32[]{:S(2)}) copy-start(bf16[512,256]{1,0:T(8,128)(2,1)S(1)} %collective-permute-done.33.refs_16_) | copy-start | bytes 786436
  165.3 1.5 collective-permute-start.32
  165.3 5.4 %copy-start.10 = (bf16[1024,256]{1,0:T(8,128)(2,1)}, bf16[1024,256]{1,0:T(8,128)(2,1)S(1)}, u32[]{:S(2)}) copy-start(bf16[1024,256]{1,0:T(8,128)(2,1)S(1)} %collective-permute-done.28.refs_12_) | copy-start | bytes 1572868
  165.3 2.5 %collective-permute-start.34 = (bf16[512,256]{1,0:T(8,128)(2,1)S(1)}, bf16[512,256]{1,0:T(8,128)(2,1)}, u32[]{:S(2)}, u32[]{:S(2)}) collective-permute-start(bf16[512,256]{1,0:T(8,128)(2,1)S(1)} %collective-permute-done.33.refs_16_), channel_id=1, source_target_pairs={{0,4},{4,0},{1,5},{5,1},{2,6},{6,2},{3,7},{7,3},{8,12},{12,8},{9,1... | collective-permute-start | bytes 786440 | tf_op jit(solution)/shard_map/ppermute | solution.py:433
  165.8 4.9 %copy-start.11 = (bf16[1024,256]{1,0:T(8,128)(2,1)}, bf16[1024,256]{1,0:T(8,128)(2,1)S(1)}, u32[]{:S(2)}) copy-start(bf16[1024,256]{1,0:T(8,128)(2,1)S(1)} %collective-permute-done.29.refs_13_) | copy-start | bytes 1572868
  167.8 2.9 %copy-start.8 = (bf16[16,128,128]{2,1,0:T(8,128)(2,1)}, bf16[16,128,128]{2,1,0:T(8,128)(2,1)S(1)}, u32[]{:S(2)}) copy-start(bf16[16,128,128]{2,1,0:T(8,128)(2,1)S(1)} %all-to-all-done.1.refs_0_.refs_1_) | copy-start | bytes 1572868
  167.8 14.5 %collective-permute-start.35 = (bf16[16,128,128]{2,1,0:T(8,128)(2,1)S(1)}, bf16[16,128,128]{2,1,0:T(8,128)(2,1)S(1)}, u32[]{:S(2)}, u32[]{:S(2)}) collective-permute-start(bf16[16,128,128]{2,1,0:T(8,128)(2,1)S(1)} %all-to-all-done.1.refs_0_.refs_1_), channel_id=1, source_target_pairs={{0,8},{8,0},{16,24},{24,16},{1,9},{9,1},{17,25},{25,17},{2,10},{10... | collective-permute-start | bytes 1572872 | tf_op jit(solution)/shard_map/ppermute | solution.py:51
  170.1 13.7 %collective-permute-start.36 = (bf16[16,128,128]{2,1,0:T(8,128)(2,1)S(1)}, bf16[16,128,128]{2,1,0:T(8,128)(2,1)S(1)}, u32[]{:S(2)}, u32[]{:S(2)}) collective-permute-start(bf16[16,128,128]{2,1,0:T(8,128)(2,1)S(1)} %all-to-all-done.1.refs_0_.refs_1_), channel_id=1, source_target_pairs={{0,16},{8,24},{16,0},{24,8},{1,17},{9,25},{17,1},{25,9},{2,18},{10... | collective-permute-start | bytes 1572872 | tf_op jit(solution)/shard_map/ppermute | solution.py:51
  184.5 14.8 %copy-start.2 = (bf16[128,1024]{1,0:T(8,128)(2,1)S(1)}, bf16[128,1024]{1,0:T(8,128)(2,1)}, u32[]{:S(2)}) copy-start(bf16[128,1024]{1,0:T(8,128)(2,1)} %get-tuple-element.115.own_x) | copy-start | bytes 786436
  184.5 14.8 %copy-start.3 = (bf16[128,1024]{1,0:T(8,128)(2,1)S(1)}, bf16[128,1024]{1,0:T(8,128)(2,1)}, u32[]{:S(2)}) copy-start(bf16[128,1024]{1,0:T(8,128)(2,1)} %get-tuple-element.116.own_y) | copy-start | bytes 786436
  191.3 7.5 %collective-permute-start.37 = (bf16[128,1024]{1,0:T(8,128)(2,1)}, bf16[128,1024]{1,0:T(8,128)(2,1)S(1)}, u32[]{:S(2)}, u32[]{:S(2)}) collective-permute-start(bf16[128,1024]{1,0:T(8,128)(2,1)} %get-tuple-element.119), channel_id=1, source_target_pairs={{0,8},{8,0},{16,24},{24,16},{1,9},{9,1},{17,25},{25,17},{2,10},{10... | collective-permute-start | bytes 786440 | tf_op jit(solution)/shard_map/ppermute | solution.py:51
  191.9 7.5 %collective-permute-start.38 = (bf16[128,1024]{1,0:T(8,128)(2,1)}, bf16[128,1024]{1,0:T(8,128)(2,1)S(1)}, u32[]{:S(2)}, u32[]{:S(2)}) collective-permute-start(bf16[128,1024]{1,0:T(8,128)(2,1)} %get-tuple-element.120), channel_id=1, source_target_pairs={{0,16},{8,24},{16,0},{24,8},{1,17},{9,25},{17,1},{25,9},{2,18},{10... | collective-permute-start | bytes 786440 | tf_op jit(solution)/shard_map/ppermute | solution.py:51
  (8 other events, 8.4 us)

commit v4 on v3

--- a/solution.py
+++ b/solution.py
@@ -76,49 +76,38 @@
     )(order, tokens, norm_gain.reshape(1, -1))
 
 
-def attention_kernel(
-    sizes, places, biases, copies, targets, *refs
-):
-    groups, reps, heads, spans, slots = sizes
-    total = sum(groups)
-    parts = refs[: len(groups) * reps]
-    out, held, asked, scores, sems = refs[len(groups) * reps :]
-    waits = []
-    at = 0
-    for g, size in enumerate(groups):
-        for r in range(reps):
-            ref = parts[g * reps + r]
-            to = held.at[r, :, :, at : at + size]
-            waits.append(pltpu.make_async_copy(ref.at[:, 1:], to, sems.at[len(waits)]))
-        own = parts[g * reps]
-        waits.append(pltpu.make_async_copy(own.at[:, 0], asked.at[:, at : at + size], sems.at[len(waits)]))
-        at += size
+def attention_kernel(sizes, places, biases, turns, ends, targets, *refs):
+    total, reps, heads, buckets = sizes
+    parts = refs[:reps]
+    out, held, asked, scores, sems = refs[reps:]
+    waits = [pltpu.make_async_copy(parts[r].at[:, 1:], held.at[r], sems.at[r]) for r in range(reps)]
+    waits.append(pltpu.make_async_copy(parts[0].at[:, 0], asked, sems.at[reps]))
     for copy in waits:
         copy.start()
     for copy in waits:
         copy.wait()
     flat = held.reshape(reps * heads * 2 * total, BLK, HEAD_DIM)
     wanted = asked.reshape(heads * total, BLK, HEAD_DIM)
-    blocks = heads * total
     factor = HEAD_DIM ** (-0.5) * math.log2(math.e)
     rows = lax.broadcasted_iota(jnp.int32, (BLK, BLK), 0)
     columns = lax.broadcasted_iota(jnp.int32, (BLK, BLK), 1)
 
-    def score(j, place):
+    def score(turn, spot, slots):
+        j = turns[turn]
         keys = jnp.concatenate([flat[places[j, n]] for n in range(slots)], axis=0)
-        scores[place] = lax.dot_general(wanted[j], keys, (((1,), (1,)), ((), ())), preferred_element_type=F32)
-
-    def blend(j, place):
-        parts = []
-        for n in range(slots):
-            part = scores[place, :, n * BLK : (n + 1) * BLK] * factor
-            parts.append(jnp.where(columns <= rows, part, MASKED) if n == 0 else part + biases[j, n])
+        scores[spot, :, : slots * BLK] = lax.dot_general(
+            wanted[j], keys, (((1,), (1,)), ((), ())), preferred_element_type=F32
+        )
+
+    def blend(turn, spot, slots):
+        j = turns[turn]
+        parts = [scores[spot, :, n * BLK : (n + 1) * BLK] * factor + biases[j, n] for n in range(slots)]
+        parts[0] = jnp.where(columns <= rows, parts[0], MASKED)
         top = parts[0]
         for n in range(1, slots):
             top = jnp.maximum(top, parts[n])
         top = jnp.max(top, axis=1, keepdims=True)
         weights = [jnp.exp2(part - top) for part in parts]
-        weights[0] = weights[0] * copies[j]
         below = weights[0]
         for n in range(1, slots):
             below = below + weights[n]
@@ -129,34 +118,47 @@
         )
         out[targets[j]] = (blended / below).astype(BF16)
 
-    score(0, 0)
-
-    def two_blocks(t, carry):
-        for place in range(2):
-            j = 2 * t + place
-            score(jnp.minimum(j + 1, blocks - 1), 1 - place)
-            blend(j, place)
-        return carry
-
-    lax.fori_loop(0, blocks // 2, two_blocks, 0)
-
-
-def attention(parts, places, biases, copies, targets, sizes):
-    groups, reps, heads, spans, slots = sizes
-    total = sum(groups)
+    low = 0
+    for b, slots in enumerate(buckets):
+        high = ends[b]
+
+        @pl.when(high > low)
+        def _(low=low, high=high, slots=slots):
+            score(low, 0, slots)
+
+            def two_turns(t, carry):
+                turn = low + 2 * t
+                score(turn + 1, 1, slots)
+                blend(turn, 0, slots)
+                score(jnp.minimum(turn + 2, high - 1), 0, slots)
+                blend(turn + 1, 1, slots)
+                return carry
+
+            pairs = (high - low) // 2
+            lax.fori_loop(0, pairs, two_turns, 0)
+
+            @pl.when(low + 2 * pairs < high)
+            def _():
+                blend(high - 1, 0, slots)
+
+        low = high
+
+
+def attention(parts, places, biases, turns, ends, targets, buckets):
+    heads, _, total = parts[0].shape[:3]
+    reps = len(parts)
     smem = pl.BlockSpec(memory_space=pltpu.SMEM)
-    hbm = pl.BlockSpec(memory_space=pl.ANY)
-    blocks = heads * total
+    blocks, slots = places.shape
     return pl.pallas_call(
-        functools.partial(attention_kernel, sizes),
+        functools.partial(attention_kernel, (total, reps, heads, buckets)),
         out_shape=jax.ShapeDtypeStruct((blocks, BLK, HEAD_DIM), BF16),
-        in_specs=[smem] * 4 + [hbm] * len(parts),
+        in_specs=[smem] * 5 + [pl.BlockSpec(memory_space=pl.ANY)] * reps,
         out_specs=pl.BlockSpec(memory_space=pltpu.VMEM),
         scratch_shapes=[
             pltpu.VMEM((reps, heads, 2, total, BLK, HEAD_DIM), BF16),
             pltpu.VMEM((heads, total, BLK, HEAD_DIM), BF16),
             pltpu.VMEM((2, BLK, slots * BLK), F32),
-            pltpu.SemaphoreType.DMA((len(groups) * (1 + reps),)),
+            pltpu.SemaphoreType.DMA((reps + 1,)),
         ],
         compiler_params=pltpu.CompilerParams(vmem_limit_bytes=40 << 20),
         cost_estimate=pl.CostEstimate(
@@ -165,7 +167,7 @@
             transcendentals=blocks * slots * BLK * BLK,
         ),
         name="attention",
-    )(places, biases, copies, targets, *parts)
+    )(places, biases, turns, ends, targets, *parts)
 
 
 def project_kernel(spots, heads, lines, reps, planes, order, *refs):
@@ -221,67 +223,147 @@
     )(planes, order, *landed, *arrays)
 
 
-def enter_kernel(heads, chunks, plan, flag, *refs):
-    count = sum(chunks)
-    rows_in, arrays = refs[:count], refs[count:-5]
-    out, weights, rows, row_sems, sems = refs[-5:]
-    at = 0
-    for n, choices in enumerate(chunks):
-        target = rows.at[pl.ds(n * BLK, BLK)]
-        if choices == 1:
-            pltpu.make_async_copy(rows_in[at], target, row_sems.at[n]).start()
-        else:
-            for choice in range(2):
-
-                @pl.when(flag[0] == choice)
-                def _(choice=choice):
-                    pltpu.make_async_copy(rows_in[at + choice], target, row_sems.at[n]).start()
-
-        at += choices
+def fetch(flag, choices, columns, target, sem):
+    copies = [pltpu.make_async_copy(ref.at[:, columns], target, sem) for ref in choices]
+    if len(copies) == 1:
+        copies[0].start()
+    else:
+        for choice, copy in enumerate(copies):
+            pl.when(flag[0] == choice)(copy.start)
+    return copies[0]
+
+
+def split(refs, counts):
+    parts = []
+    for count in counts:
+        parts.append(refs[:count])
+        refs = refs[count:]
+    return parts
+
+
+def fetch_weights(arrays, places, weights, sems):
     copies = []
     for c in range(3):
+        row = []
+        for i, (ref, place) in enumerate(zip(arrays, places)):
+            target = weights.at[c, pl.ds(place, ref.shape[1])]
+            row.append(pltpu.make_async_copy(ref.at[c], target, sems.at[c, i]))
+            row[-1].start()
+        copies.append(row)
+    return copies
+
+
+def begin_kernel(counts, runs, places, flag, *refs):
+    chunks = split(refs, counts)
+    arrays = refs[sum(counts) : -5]
+    out, weights, rows, row_sems, sems = refs[-5:]
+    waits = [
+        fetch(flag, chunk, pl.ds(0, rows.shape[1]), rows.at[pl.ds(n * BLK, BLK)], row_sems.at[n])
+        for n, chunk in enumerate(chunks)
+    ]
+    copies = fetch_weights(arrays, places, weights, sems)
+    for wait in waits:
+        wait.wait()
+    for c in range(3):
+        for copy in copies[c]:
+            copy.wait()
+        total = None
         at = 0
-        for i, place in plan[c]:
-            size = arrays[i].shape[1]
-            target = weights.at[c, pl.ds(at, size)]
-            copies.append((c, pltpu.make_async_copy(arrays[i].at[place], target, sems.at[len(copies)])))
+        for first, size in runs:
+            term = jnp.dot(rows[:, first : first + size], weights[c, at : at + size], preferred_element_type=F32)
+            total = term if total is None else total + term
             at += size
-    for _, copy in copies:
-        copy.start()
-    at = 0
-    for n, choices in enumerate(chunks):
-        pltpu.make_async_copy(rows_in[at], rows.at[pl.ds(n * BLK, BLK)], row_sems.at[n]).wait()
-        at += choices
-    for c in range(3):
-        for which, copy in copies:
-            if which == c:
-                copy.wait()
-        total = jnp.dot(rows[...], weights[c], preferred_element_type=F32).astype(BF16)
-        for n in range(len(chunks)):
-            for h in range(heads):
-                out[h, c, n] = total[n * BLK : (n + 1) * BLK, h * HEAD_DIM : (h + 1) * HEAD_DIM]
-
-
-def enter(flag, chunks, arrays, plan, heads):
+        out[c] = total
+
+
+def begin(flag, chunks, arrays, runs):
     chunks = [chunk if isinstance(chunk, tuple) else (chunk,) for chunk in chunks]
-    features = chunks[0][0].shape[1]
+    counts = [len(chunk) for chunk in chunks]
+    features, width = chunks[0][0].shape[1], arrays[0].shape[2]
+    places, at = [], 0
+    for array in arrays:
+        places.append(at)
+        at += array.shape[1]
     hbm = pl.BlockSpec(memory_space=pl.ANY)
     rows_in = [array for chunk in chunks for array in chunk]
     return pl.pallas_call(
-        functools.partial(enter_kernel, heads, [len(chunk) for chunk in chunks], plan),
-        out_shape=jax.ShapeDtypeStruct((heads, 3, len(chunks), BLK, HEAD_DIM), BF16),
+        functools.partial(begin_kernel, counts, runs, places),
+        out_shape=jax.ShapeDtypeStruct((3, len(chunks) * BLK, width), F32),
         in_specs=[pl.BlockSpec(memory_space=pltpu.SMEM)] + [hbm] * (len(rows_in) + len(arrays)),
         out_specs=pl.BlockSpec(memory_space=pltpu.VMEM),
         scratch_shapes=[
-            pltpu.VMEM((3, features, heads * HEAD_DIM), BF16),
+            pltpu.VMEM((3, at, width), BF16),
             pltpu.VMEM((len(chunks) * BLK, features), BF16),
             pltpu.SemaphoreType.DMA((len(chunks),)),
-            pltpu.SemaphoreType.DMA((sum(len(parts) for parts in plan),)),
+            pltpu.SemaphoreType.DMA((3, len(arrays))),
+        ],
+        compiler_params=pltpu.CompilerParams(vmem_limit_bytes=58 << 20),
+        cost_estimate=pl.CostEstimate(flops=1, bytes_accessed=1, transcendentals=0),
+        name="begin",
+    )(flag, *rows_in, *arrays)
+
+
+def enter_kernel(heads, counts, runs, rest, places, flag, begun, *refs):
+    chunks = split(refs, counts)
+    arrays = refs[sum(counts) : -8]
+    out, weights, rows, last, so_far, row_sems, sems, begun_sem = refs[-8:]
+    waits = []
+    for n, chunk in enumerate(chunks):
+        at = 0
+        for first, size in runs:
+            target = rows.at[pl.ds(n * BLK, BLK), pl.ds(at, size)]
+            waits.append(fetch(flag, chunk, pl.ds(first, size), target, row_sems.at[len(waits)]))
+            at += size
+    common = at
+    at = 0
+    for first, size in rest:
+        waits.append(fetch(flag, chunks[-1], pl.ds(first, size), last.at[:, pl.ds(at, size)], row_sems.at[len(waits)]))
+        at += size
+    copies = fetch_weights(arrays, places, weights, sems)
+    begun_copy = pltpu.make_async_copy(begun, so_far, begun_sem)
+    begun_copy.start()
+    for wait in waits:
+        wait.wait()
+    early = so_far.shape[1]
+    for c in range(3):
+        for copy in copies[c]:
+            copy.wait()
+        if c == 0:
+            begun_copy.wait()
+        total = jnp.dot(rows[...], weights[c, :common], preferred_element_type=F32)
+        final = total[early:] + jnp.dot(last[...], weights[c, common:], preferred_element_type=F32)
+        parts = [(so_far[c] + total[:early]).astype(BF16), final.astype(BF16)]
+        for n in range(len(chunks)):
+            part, row = (parts[1], 0) if n * BLK == early else (parts[0], n * BLK)
+            for h in range(heads):
+                out[h, c, n] = part[row : row + BLK, h * HEAD_DIM : (h + 1) * HEAD_DIM]
+
+
+def enter(flag, begun, chunks, arrays, places, runs, rest, heads):
+    chunks = [chunk if isinstance(chunk, tuple) else (chunk,) for chunk in chunks]
+    counts = [len(chunk) for chunk in chunks]
+    features, width = chunks[0][0].shape[1], arrays[0].shape[2]
+    common = sum(size for _, size in runs)
+    hbm = pl.BlockSpec(memory_space=pl.ANY)
+    rows_in = [array for chunk in chunks for array in chunk]
+    return pl.pallas_call(
+        functools.partial(enter_kernel, heads, counts, runs, rest, places),
+        out_shape=jax.ShapeDtypeStruct((heads, 3, len(chunks), BLK, HEAD_DIM), BF16),
+        in_specs=[pl.BlockSpec(memory_space=pltpu.SMEM)] + [hbm] * (1 + len(rows_in) + len(arrays)),
+        out_specs=pl.BlockSpec(memory_space=pltpu.VMEM),
+        scratch_shapes=[
+            pltpu.VMEM((3, features, width), BF16),
+            pltpu.VMEM((len(chunks) * BLK, common), BF16),
+            pltpu.VMEM((BLK, features - common), BF16),
+            pltpu.VMEM(begun.shape, F32),
+            pltpu.SemaphoreType.DMA((len(chunks) * len(runs) + len(rest),)),
+            pltpu.SemaphoreType.DMA((3, len(arrays))),
+            pltpu.SemaphoreType.DMA,
         ],
         compiler_params=pltpu.CompilerParams(vmem_limit_bytes=58 << 20),
         cost_estimate=pl.CostEstimate(flops=1, bytes_accessed=1, transcendentals=0),
         name="enter",
-    )(flag, *rows_in, *arrays)
+    )(flag, begun, *rows_in, *arrays)
 
 
 def leave_kernel(heads, lines, count, order, *refs):
@@ -369,23 +451,43 @@
     return lax.all_to_all(projected, "head", 0, 0, tiled=True)
 
 
-def tables(heads, reps, lines, rep_at, order, layout):
-    blocks = heads * reps * lines
-    names = jnp.arange(blocks, dtype=jnp.int32)
-    slot_of = jnp.argmax(order[None, :] == jnp.arange(lines, dtype=jnp.int32)[:, None], axis=1).astype(jnp.int32)
-    span_of = names // lines
-    rep_of, head_of = span_of % reps, span_of // reps
-    side_of = rep_of ^ rep_at if reps == 2 else rep_of
-    place_of = ((side_of * heads + head_of) * 2) * lines + slot_of[names % lines]
-    own = ((jnp.arange(heads, dtype=jnp.int32)[:, None] * reps + rep_at) * lines + order[None, :]).reshape(-1)
-    others = jnp.concatenate([(own - 1)[:, None], layout[own]], axis=1)
-    index = jnp.concatenate([own[:, None], others], axis=1)
-    places = place_of[jnp.maximum(index, 0)]
-    off = (others < 0) | (others == own[:, None])
-    biases = jnp.concatenate([jnp.zeros((own.shape[0], 1), F32), jnp.where(off, MASKED, 0.0)], axis=1)
-    copies = 1.0 + jnp.sum(others == own[:, None], axis=1).astype(F32)
-    targets = (jnp.arange(heads, dtype=jnp.int32)[:, None] * lines + order[None, :]).reshape(-1)
-    return places, biases, copies, targets
+def tables(heads, reps, lines, rep_at, order, layout, buckets):
+    ints = jnp.int32
+
+    def place_of(block):
+        span = block // lines
+        side = (span % reps) ^ rep_at if reps == 2 else span % reps
+        slot = jnp.sum(jnp.where(block[..., None] % lines == order, jnp.arange(lines, dtype=ints), 0), axis=-1)
+        return ((side * heads + span // reps) * 2) * lines + slot
+
+    own = ((jnp.arange(heads, dtype=ints)[:, None] * reps + rep_at) * lines + order[None, :]).reshape(-1)
+    listed = jnp.sum(
+        jnp.where(own[:, None, None] == jnp.arange(layout.shape[0], dtype=ints)[None, :, None], layout[None], 0), axis=1
+    )
+    others = jnp.concatenate([(own - 1)[:, None], listed], axis=1)
+    count = others.shape[1]
+    at = jnp.arange(count, dtype=ints)
+    mine = others == own[:, None]
+    kept = (others >= 0) & ~mine
+    same = (others[:, :, None] == others[:, None, :]) & kept[:, None, :]
+    often = jnp.sum(same, axis=2)
+    first = kept & ~jnp.any(same & (at[None, :] < at[:, None])[None], axis=2)
+    rank = jnp.sum(first[:, None, :] & (at[None, :] < at[:, None])[None], axis=2)
+    chosen = first[:, None, :] & (rank[:, None, :] == at[None, :, None])
+    block = jnp.sum(jnp.where(chosen, others[:, None, :], 0), axis=2)
+    times = jnp.sum(jnp.where(chosen, often[:, None, :], 0), axis=2)
+    places = place_of(jnp.concatenate([own[:, None], jnp.where(times > 0, block, own[:, None])], axis=1))
+    times = jnp.concatenate([1 + jnp.sum(mine, axis=1, keepdims=True), times], axis=1)
+    biases = jnp.where(times > 0, jnp.log2(jnp.maximum(times, 1).astype(F32)), MASKED)
+    distinct = jnp.sum(times > 0, axis=1)
+    bucket = sum((distinct > size).astype(ints) for size in buckets[:-1])
+    here = jnp.arange(own.shape[0], dtype=ints)
+    ahead = (bucket[None, :] < bucket[:, None]) | ((bucket[None, :] == bucket[:, None]) & (here[None, :] < here[:, None]))
+    turn = jnp.sum(ahead, axis=1)
+    turns = jnp.sum(jnp.where(turn[None, :] == here[:, None], here[None, :], 0), axis=1)
+    ends = jnp.sum(bucket[None, :] <= jnp.arange(len(buckets), dtype=ints)[:, None], axis=1)
+    targets = (jnp.arange(heads, dtype=ints)[:, None] * lines + order[None, :]).reshape(-1)
+    return places.astype(ints), biases, turns.astype(ints), ends.astype(ints), targets
 
 
 def shards(heads, reps, lines, tokens, norm_gain, qkv_weight, out_weight, layout):
@@ -403,17 +505,17 @@
     normed = normalize(tokens, norm_gain, feature_order)
     inside = (line_at == 1) | (line_at == 2)
     flag = jnp.where(inside, 0, 1).astype(jnp.int32).reshape(1)
-    table = tables(heads, reps, lines, rep_at, order, layout)
-    slots = table[0].shape[1]
-
-    def attend(parts, groups):
-        attended = attention(parts, *table, (groups, reps, heads, heads * reps, slots))
-        return lax.all_to_all(attended, ("head", "line"), 0, 0, tiled=True)
+    slots = 2 + layout.shape[1]
+    buckets = sorted({min(8, slots), min(12, slots), slots})
+    table = tables(heads, reps, lines, rep_at, order, layout, buckets)
 
     if not fast:
         weight = lax.all_gather(qkv_weight, ("head", "rep"), axis=1, tiled=True)
         rows = gathered(normed, "line", lines)
-        landed = attend(pair_gather(by_head(enter(flag, rows, [weight], [[(0, c)] for c in range(3)], heads)), reps), (lines,))
+        whole = begin(flag, rows, [weight], [(0, weight.shape[1])]).astype(BF16)
+        projected = whole.reshape(3, lines, BLK, heads, HEAD_DIM).transpose(3, 0, 1, 2, 4)
+        attended = attention(pair_gather(by_head(projected), reps), *table, buckets)
+        landed = lax.all_to_all(attended, ("head", "line"), 0, 0, tiled=True)
         out_pieces = [
             (s, h, 0, piece)
             for s, part in enumerate(gathered(out_weight, "line", lines))
@@ -448,15 +550,20 @@
     third = along(crossed, outward)
     w_first, w_other = hop(w_halves[0], 1), hop(w_halves[1], 2)
     w_others += [pair(w) for w in (w_one, w_two)]
-    w_first, w_other, *w_others = barrier((w_first, w_other, *w_others))
-    w_others += [pair(w) for w in (w_first, w_other)]
-    third, *w_others = barrier((third, *w_others))
-    o_own = tie(out_weight, third)
+    size = qkv_weight.shape[1]
+    near_runs, far_runs = [(0, 3 * size), (4 * size, 3 * size)], [(3 * size, size), (7 * size, size)]
+    chunks = [normed, near, (across, second)]
+    near_weights = [qkv_weight, w_one, w_two, *w_others]
+    begun = begin(flag, chunks, near_weights, near_runs)
+    w_first, w_other, begun = barrier((w_first, w_other, begun))
+    w_others = [pair(w) for w in (w_first, w_other)]
+    third, o_own, *w_others = barrier((third, out_weight, *w_others))
+    chunks.append((crossed, third))
     o_near, o_across = along(o_own, xor_pairs(4, 1)), along(o_own, middle)
-    weights = [qkv_weight, w_one, w_two, w_first, w_other, *w_others]
-    plan = [[(i, c) for i in range(len(weights))] for c in range(3)]
-    chunks = [normed, near, (across, second), (crossed, third)]
-    projected, o_near, o_across = barrier((enter(flag, chunks, weights, plan, heads), o_near, o_across))
+    weights = [w_first, w_other, *w_others, *near_weights]
+    places = [0, half, 2 * half, 3 * half] + [2 * size + i * size for i in range(6)]
+    projected = enter(flag, begun, chunks, weights, places, far_runs, near_runs, heads)
+    projected, o_near, o_across = barrier((projected, o_near, o_across))
     mine = by_head(projected)
     o_crossed, o_second = along(o_near, middle), along(o_across, outward)
     mine, o_crossed, o_second = barrier((mine, o_crossed, o_second))
@@ -464,7 +571,7 @@
     parts = pair_gather(mine, reps)
     batch = jnp.concatenate([o_near, jnp.where(inside, o_across, o_second)], axis=0)
     shared = [[out_weight, *o_halves], [batch, *share(batch)]]
-    attended = attention(parts, *table, ((lines,), reps, heads, heads * reps, slots))
+    attended = attention(parts, *table, buckets)
     attended, o_third, *shared[1] = barrier((attended, o_third, *shared[1]))
     landed = lax.all_to_all(attended, ("head", "line"), 0, 0, tiled=True)
     last = jnp.where(inside, o_crossed, o_third)

time: 202 us -> 198 us (0.980)
  waiting for transfers between devices: 98.5 us -> 89.4 us
  Pallas kernels: 41.3 us -> 44.9 us
  starting transfers between devices: 42.5 us -> 44.6 us
    ppermute x14, waiting for transfers between devices: 59.5 us -> 45.3 us  [hop(): return lax.ppermute(part, 'head', xor_pairs(4, bit))]
    ppermute x10, waiting for transfers between devices: 37.2 us -> 42.3 us  [along(): return lax.ppermute(part, 'line', pairs)]
    gather x4 -> x0, local copies, waits for them, and re-layouts: 3.62 us -> none  [the longest x2 2.44 us: tables(): places = place_of[jnp.maximum(index, 0)]]
    pallas_call x2 -> x3, Pallas kernels: 25.1 us -> 28.7 us  [the longest x1 10.8 us: enter(): pl.pallas_call(functools.partial(enter_kernel, heads, counts, runs, rest,...]
    reduce_sum x1 -> x10, other arithmetic: 0.19 us -> 2.72 us  [the longest x1 0.65 us: tables(): times = jnp.sum(jnp.where(chosen, often[:, None, :], 0), axis=2)]
    add x3 -> x4, other arithmetic: 2.53 us -> 0.18 us  [the longest x1 0.1 us: place_of(): return (side * heads + span // reps) * 2 * lines + slot]
    unnamed x63 -> x52, local copies, waits for them, and re-layouts: 4.73 us -> 5.27 us
  transfers between devices with their start and end apart: 41 -> 41, of which waited for: 20 -> 22; matrix products, arithmetic and copies ran while one was open for 7% -> 7% of each run, Pallas kernels for 16% -> 18%
where the time goes in v4:
time: 198 us
  waiting for transfers between devices  89.4 us (45%)
  Pallas kernels  44.9 us (23%)
  starting transfers between devices  44.6 us (23%)
  local copies, waits for them, and re-layouts  11 us (6%)
  other arithmetic  7.37 us (4%)
    ppermute x14, waiting for transfers between devices, hop(): return lax.ppermute(part, 'head', xor_pairs(4, bit))  45.3 us
    ppermute x10, waiting for transfers between devices, along(): return lax.ppermute(part, 'line', pairs)  42.3 us
    ppermute x14, starting transfers between devices, hop(): return lax.ppermute(part, 'head', xor_pairs(4, bit))  19.3 us
    ppermute x10, starting transfers between devices, along(): return lax.ppermute(part, 'line', pairs)  13.7 us
    pallas_call x2, Pallas kernels, leave(): pl.pallas_call(functools.partial(leave_kernel, heads, lines, len(shared))...  13.5 us
    pallas_call x1, Pallas kernels, enter(): pl.pallas_call(functools.partial(enter_kernel, heads, counts, runs, rest,...  10.8 us
    pallas_call x1, Pallas kernels, begin(): pl.pallas_call(functools.partial(begin_kernel, counts, runs, places), out...  10.3 us
    pallas_call x1, Pallas kernels, attention(): pl.pallas_call(functools.partial(attention_kernel, (total, reps, heads, b...  7.69 us
  transfers between devices with their start and end apart: 41, of which 22 were waited for; matrix products, arithmetic and copies ran while one was open for 7% of the time, Pallas kernels for 18%

profile of v4, /device:TPU:0, one launch (start us, length us, event | category | flops | bytes accessed | tf_op | source)
XLA Modules:
  0.0 197.7 jit_solution(219887982495549033)
XLA Ops:
  0.1 1.2 copy-done.1
  1.3 0.7 copy-done.4
  2.0 1.1 normalize.1.refs_0_
  3.1 3.1 %collective-permute-start = (bf16[128,4096]{1,0:T(8,128)(2,1)S(1)}, bf16[128,4096]{1,0:T(8,128)(2,1)}, u32[]{:S(2)}, u32[]{:S(2)}) collective-permute-start(bf16[128,4096]{1,0:T(8,128)(2,1)S(1)} %normalize.1.refs_0_), channel_id=1, source_target_pairs={{0,1},{1,0},{2,3},{3,2},{4,5},{5,4},{6,7},{7,6},{8,9},{9,8},{10,11... | collective-permute-start | bytes 3145736 | tf_op jit(solution)/shard_map/ppermute | solution.py:532
  6.2 1.6 collective-permute-start.1
  7.8 1.5 collective-permute-start.5
  9.3 1.5 collective-permute-start.6
  10.9 0.7 dynamic-slice_bitcast_fusion.order
  14.3 0.7 select_reduce_fusion.1
  16.3 13.2 %collective-permute-done.refs_1_ = bf16[128,4096]{1,0:T(8,128)(2,1)} collective-permute-done((bf16[128,4096]{1,0:T(8,128)(2,1)S(1)}, bf16[128,4096]{1,0:T(8,128)(2,1)}, u32[]{:S(2)}, u32[]{:S(2)}) %collective-permute-start) | collective-permute-done | bytes 1048608 | tf_op jit(solution)/shard_map/ppermute | solution.py:532
  29.5 1.3 collective-permute-start.3
  30.8 1.6 collective-permute-start.4
  32.4 12.4 %collective-permute-done.5.refs_5_.refs_11_ = bf16[3,512,512]{2,1,0:T(8,128)(2,1)S(1)} collective-permute-done((bf16[3,512,512]{2,1,0:T(8,128)(2,1)}, bf16[3,512,512]{2,1,0:T(8,128)(2,1)S(1)}, u32[]{:S(2)}, u32[]{:S(2)}) %collective-permute-start.5) | collective-permute-done | bytes 1572896 | tf_op jit(solution)/shard_map/ppermute | solution.py:51
  44.9 1.3 collective-permute-done.6.refs_6_.refs_12_
  46.2 1.1 fusion.18
  47.2 1.6 collective-permute-start.7
  48.8 0.7 collective-permute-start.8
  49.6 2.1 %slice.32 = bf16[3,256,512]{2,1,0:T(8,128)(2,1)} slice(bf16[3,512,512]{2,1,0:T(8,128)(2,1)} %collective-permute-done.6.refs_6_.refs_12_), slice={[0:3], [0:256], [0:512]} | slice | bytes 1572864 | tf_op jit(solution)/shard_map/slice | solution.py:546
  51.7 0.9 slice.33
  52.6 2.4 %collective-permute-done.7.refs_3_ = bf16[512,256]{1,0:T(8,128)(2,1)S(1)} collective-permute-done((bf16[512,256]{1,0:T(8,128)(2,1)S(1)}, bf16[512,256]{1,0:T(8,128)(2,1)S(1)}, u32[]{:S(2)}, u32[]{:S(2)}) %collective-permute-start.7) | collective-permute-done | bytes 262176 | tf_op jit(solution)/shard_map/ppermute | solution.py:51
  54.9 1.3 collective-permute-done.8.refs_4_
  56.3 1.7 collective-permute-done.3.refs_3_
  58.1 0.9 copy-done.11
  59.0 1.5 collective-permute-start.9
  60.5 1.5 collective-permute-start.10
  62.0 1.3 collective-permute-start.13
  63.4 0.7 collective-permute-done.12.refs_9_.refs_15_
  64.6 10.3 %begin.1.begun = f32[3,384,512]{2,1,0:T(8,128)} custom-call(s32[1]{0:T(128)} %bitcast.13.flag, bf16[128,4096]{1,0:T(8,128)(2,1)} %copy-done, bf16[128,4096]{1,0:T(8,128)(2,1)} %collective-permute-done.refs_1_, bf16[128,4096]{1,0:T(8,128)(2,1)} %collective-permute-done.1.refs_2_, bf16[128,4096]{1,0:T(8,128)(2,1)} %copy-done.11, ...), custom_call_target="tpu_custom_call" | custom-call | flops 1 | bytes 1 | tf_op jit(solution)/shard_map/begin/pallas_call | solution.py:289
  74.8 4.5 %collective-permute-done.9.refs_6_ = bf16[3,256,512]{2,1,0:T(8,128)(2,1)} collective-permute-done((bf16[3,256,512]{2,1,0:T(8,128)(2,1)}, bf16[3,256,512]{2,1,0:T(8,128)(2,1)}, u32[]{:S(2)}, u32[]{:S(2)}) %collective-permute-start.9) | collective-permute-done | bytes 786464 | tf_op jit(solution)/shard_map/ppermute | solution.py:51
  79.3 1.2 collective-permute-done.10.refs_7_
  81.0 8.8 %collective-permute-done.13.refs_5_ = bf16[128,4096]{1,0:T(8,128)(2,1)} collective-permute-done((bf16[128,4096]{1,0:T(8,128)(2,1)}, bf16[128,4096]{1,0:T(8,128)(2,1)}, u32[]{:S(2)}, u32[]{:S(2)}) %collective-permute-start.13) | collective-permute-done | bytes 1048608 | tf_op jit(solution)/shard_map/ppermute | solution.py:532
  89.9 0.7 collective-permute-start.17
  90.9 10.8 %enter.1 = bf16[4,3,4,128,128]{4,3,2,1,0:T(8,128)(2,1)} custom-call(s32[1]{0:T(128)} %bitcast.13.flag, f32[3,384,512]{2,1,0:T(8,128)} %begin.1.begun, bf16[128,4096]{1,0:T(8,128)(2,1)} %copy-done, bf16[128,4096]{1,0:T(8,128)(2,1)} %collective-permute-done.refs_1_, bf16[128,4096]{1,0:T(8,128)(2,1)} %collective-permute-done.1.refs_2_, ...), custom_call_target="tpu_custom_call" | custom-call | flops 1 | bytes 1 | tf_op jit(solution)/shard_map/enter/pallas_call | solution.py:349
  101.7 0.9 collective-permute-done.16
  102.6 3.6 %all-to-all-start = ((bf16[4,3,4,128,128]{4,3,2,1,0:T(8,128)(2,1)}), bf16[4,3,4,128,128]{4,3,2,1,0:T(8,128)(2,1)S(1)}, u32[]{:S(2)}, u32[]{:S(2)}) async-start(bf16[4,3,4,128,128]{4,3,2,1,0:T(8,128)(2,1)} %enter.1), calls=%async_computation | async-start | bytes 3145728 | tf_op jit(solution)/shard_map/all_to_all | solution.py:451
  106.2 1.5 collective-permute-start.18
  107.7 1.3 collective-permute-start.19
  109.0 15.1 %collective-permute-done.19 = bf16[512,512]{1,0:T(8,128)(2,1)} collective-permute-done((bf16[512,512]{1,0:T(8,128)(2,1)S(1)}, bf16[512,512]{1,0:T(8,128)(2,1)}, u32[]{:S(2)}, u32[]{:S(2)}) %collective-permute-start.19) | collective-permute-done | bytes 524320 | tf_op jit(solution)/shard_map/ppermute | solution.py:532
  124.0 1.3 collective-permute-start.21
  125.3 1.1 broadcast_select_fusion.1
  126.5 1.8 collective-permute-start.22
  128.3 1.5 collective-permute-start.23
  129.8 1.1 pad_maximum_fusion.refs_8_
  131.5 7.7 %attention.1 = bf16[16,128,128]{2,1,0:T(8,128)(2,1)} custom-call(s32[16,18]{1,0:T(8,128)S(1)} %fusion.7.places, f32[16,18]{1,0:T(8,128)S(1)} %multiply_select_fusion.biases, s32[16]{0:T(128)S(1)} %select_reduce_fusion.4.turns, s32[3]{0:T(128)S(1)} %convert_reduce_fusion.5.ends, s32[16]{0:T(128)S(1)} %add.182.targets, ...), custom_call_target="tpu_custom_call" | custom-call | flops 2415919104 | bytes 4194304 | tf_op jit(solution)/shard_map/attention/pallas_call | solution.py:152
  139.2 2.6 %collective-permute-done.21 = bf16[512,512]{1,0:T(8,128)(2,1)} collective-permute-done((bf16[512,512]{1,0:T(8,128)(2,1)}, bf16[512,512]{1,0:T(8,128)(2,1)}, u32[]{:S(2)}, u32[]{:S(2)}) %collective-permute-start.21) | collective-permute-done | bytes 524320 | tf_op jit(solution)/shard_map/ppermute | solution.py:532
  141.8 0.6 collective-permute-done.23.refs_10_
  142.5 5.7 %all-to-all-start.1 = ((bf16[16,128,128]{2,1,0:T(8,128)(2,1)}), bf16[16,128,128]{2,1,0:T(8,128)(2,1)S(1)}, u32[]{:S(2)}, u32[]{:S(2)}) async-start(bf16[16,128,128]{2,1,0:T(8,128)(2,1)} %attention.1), calls=%async_computation.1 | async-start | bytes 1048576 | tf_op jit(solution)/shard_map/all_to_all | solution.py:576
  148.3 1.1 broadcast_select_fusion.refs_14_
  149.5 2.0 %collective-permute-start.31 = (bf16[512,256]{1,0:T(8,128)(2,1)S(1)}, bf16[512,256]{1,0:T(8,128)(2,1)S(1)}, u32[]{:S(2)}, u32[]{:S(2)}) collective-permute-start(bf16[512,256]{1,0:T(8,128)(2,1)S(1)} %get-tuple-element.118), channel_id=1, source_target_pairs={{0,16},{8,24},{16,0},{24,8},{1,17},{9,25},{17,1},{25,9},{2,18},{10... | collective-permute-start | bytes 786440 | tf_op jit(solution)/shard_map/ppermute | solution.py:51
  152.0 1.5 collective-permute-start.33
  153.4 7.9 %collective-permute-done.31.refs_15_ = bf16[512,256]{1,0:T(8,128)(2,1)S(1)} collective-permute-done((bf16[512,256]{1,0:T(8,128)(2,1)S(1)}, bf16[512,256]{1,0:T(8,128)(2,1)S(1)}, u32[]{:S(2)}, u32[]{:S(2)}) %collective-permute-start.31) | collective-permute-done | bytes 262176 | tf_op jit(solution)/shard_map/ppermute | solution.py:51
  161.3 1.1 collective-permute-done.33.refs_16_
  163.2 0.8 collective-permute-done.32.refs_18_
  164.0 0.7 copy-done.19
  164.7 2.0 %collective-permute-start.35 = (bf16[16,128,128]{2,1,0:T(8,128)(2,1)S(1)}, bf16[16,128,128]{2,1,0:T(8,128)(2,1)S(1)}, u32[]{:S(2)}, u32[]{:S(2)}) collective-permute-start(bf16[16,128,128]{2,1,0:T(8,128)(2,1)S(1)} %all-to-all-done.1.refs_0_.refs_1_), channel_id=1, source_target_pairs={{0,8},{8,0},{16,24},{24,16},{1,9},{9,1},{17,25},{25,17},{2,10},{10... | collective-permute-start | bytes 1572872 | tf_op jit(solution)/shard_map/ppermute | solution.py:51
  166.8 0.9 collective-permute-start.36
  167.7 6.7 %leave.2 = (bf16[128,1024]{1,0:T(8,128)(2,1)}, bf16[128,1024]{1,0:T(8,128)(2,1)}) custom-call(s32[4]{0:T(128)} %copy-done.24, bf16[16,128,128]{2,1,0:T(8,128)(2,1)} %copy-done.10, bf16[16,128,128]{2,1,0:T(8,128)(2,1)} %copy-done.10, bf16[512,512]{1,0:T(8,128)(2,1)} %refs_2_.3, bf16[512,256]{1,0:T(8,128)(2,1)} %copy-done.16, ...), custom_call_target="tpu_custom_call" | custom-call | flops 1073741824 | bytes 8388608 | tf_op jit(solution)/shard_map/leave/pallas_call | solution.py:409
  174.4 4.6 %collective-permute-done.35.refs_0_ = bf16[16,128,128]{2,1,0:T(8,128)(2,1)S(1)} collective-permute-done((bf16[16,128,128]{2,1,0:T(8,128)(2,1)S(1)}, bf16[16,128,128]{2,1,0:T(8,128)(2,1)S(1)}, u32[]{:S(2)}, u32[]{:S(2)}) %collective-permute-start.35) | collective-permute-done | bytes 524320 | tf_op jit(solution)/shard_map/ppermute | solution.py:51
  179.0 1.5 collective-permute-done.36.refs_1_
  180.5 0.8 copy-done.23
  181.3 6.8 %leave.3 = (bf16[128,1024]{1,0:T(8,128)(2,1)}, bf16[128,1024]{1,0:T(8,128)(2,1)}) custom-call(s32[4]{0:T(128)} %copy-done.24, bf16[16,128,128]{2,1,0:T(8,128)(2,1)} %copy-done.22, bf16[16,128,128]{2,1,0:T(8,128)(2,1)} %copy-done.23, bf16[512,512]{1,0:T(8,128)(2,1)} %refs_2_.3, bf16[512,256]{1,0:T(8,128)(2,1)} %copy-done.16, ...), custom_call_target="tpu_custom_call" | custom-call | flops 1073741824 | bytes 8388608 | tf_op jit(solution)/shard_map/leave/pallas_call | solution.py:409
  188.6 0.9 collective-permute-start.38
  189.5 6.0 %collective-permute-done.37.from_x = bf16[128,1024]{1,0:T(8,128)(2,1)S(1)} collective-permute-done((bf16[128,1024]{1,0:T(8,128)(2,1)}, bf16[128,1024]{1,0:T(8,128)(2,1)S(1)}, u32[]{:S(2)}, u32[]{:S(2)}) %collective-permute-start.37) | collective-permute-done | bytes 262176 | tf_op jit(solution)/shard_map/ppermute | solution.py:51
  196.0 1.6 place.1
  (122 shorter events, 8.9 us)
Async XLA Ops:
  0.0 11.9 %copy-start.25 = (s32[32,16]{0,1:T(8,128)S(1)}, s32[32,16]{0,1:T(8,128)}, u32[]{:S(2)}) copy-start(s32[32,16]{0,1:T(8,128)} %param.10) | copy-start | bytes 6148
  0.1 1.2 copy-start.1
  3.1 48.5 %copy-start = (bf16[128,4096]{1,0:T(8,128)(2,1)}, bf16[128,4096]{1,0:T(8,128)(2,1)S(1)}, u32[]{:S(2)}) copy-start(bf16[128,4096]{1,0:T(8,128)(2,1)S(1)} %normalize.1.refs_0_) | copy-start | bytes 3145732
  3.1 26.4 %collective-permute-start = (bf16[128,4096]{1,0:T(8,128)(2,1)S(1)}, bf16[128,4096]{1,0:T(8,128)(2,1)}, u32[]{:S(2)}, u32[]{:S(2)}) collective-permute-start(bf16[128,4096]{1,0:T(8,128)(2,1)S(1)} %normalize.1.refs_0_), channel_id=1, source_target_pairs={{0,1},{1,0},{2,3},{3,2},{4,5},{5,4},{6,7},{7,6},{8,9},{9,8},{10,11... | collective-permute-start | bytes 3145736 | tf_op jit(solution)/shard_map/ppermute | solution.py:532
  6.2 23.3 %collective-permute-start.1 = (bf16[128,4096]{1,0:T(8,128)(2,1)S(1)}, bf16[128,4096]{1,0:T(8,128)(2,1)}, u32[]{:S(2)}, u32[]{:S(2)}) collective-permute-start(bf16[128,4096]{1,0:T(8,128)(2,1)S(1)} %normalize.1.refs_0_), channel_id=1, source_target_pairs={{1,2},{2,1},{5,6},{6,5},{9,10},{10,9},{13,14},{14,13},{17,18},{18,... | collective-permute-start | bytes 3145736 | tf_op jit(solution)/shard_map/ppermute | solution.py:532
  7.8 21.6 %collective-permute-start.2 = (bf16[3,512,512]{2,1,0:T(8,128)(2,1)}, bf16[3,512,512]{2,1,0:T(8,128)(2,1)}, u32[]{:S(2)}, u32[]{:S(2)}) collective-permute-start(bf16[3,512,512]{2,1,0:T(8,128)(2,1)} %refs_10_.1), channel_id=1, source_target_pairs={{0,4},{4,0},{1,5},{5,1},{2,6},{6,2},{3,7},{7,3},{8,12},{12,8},{9,1... | collective-permute-start | bytes 4718600 | tf_op jit(solution)/shard_map/ppermute | solution.py:535
  7.8 37.0 %collective-permute-start.5 = (bf16[3,512,512]{2,1,0:T(8,128)(2,1)}, bf16[3,512,512]{2,1,0:T(8,128)(2,1)S(1)}, u32[]{:S(2)}, u32[]{:S(2)}) collective-permute-start(bf16[3,512,512]{2,1,0:T(8,128)(2,1)} %refs_10_.1), channel_id=1, source_target_pairs={{0,8},{8,0},{16,24},{24,16},{1,9},{9,1},{17,25},{25,17},{2,10},{10... | collective-permute-start | bytes 4718600 | tf_op jit(solution)/shard_map/ppermute | solution.py:51
  9.3 36.8 %collective-permute-start.6 = (bf16[3,512,512]{2,1,0:T(8,128)(2,1)}, bf16[3,512,512]{2,1,0:T(8,128)(2,1)}, u32[]{:S(2)}, u32[]{:S(2)}) collective-permute-start(bf16[3,512,512]{2,1,0:T(8,128)(2,1)} %refs_10_.1), channel_id=1, source_target_pairs={{0,16},{8,24},{16,0},{24,8},{1,17},{9,25},{17,1},{25,9},{2,18},{10... | collective-permute-start | bytes 4718600 | tf_op jit(solution)/shard_map/ppermute | solution.py:51
  11.6 40.1 %copy-start.24 = (s32[4]{0:T(128)}, s32[4]{0:T(128)S(1)}, u32[]{:S(2)}) copy-start(s32[4]{0:T(128)S(1)} %dynamic-slice_bitcast_fusion.order) | copy-start | bytes 52
  29.5 28.5 %collective-permute-start.3 = (bf16[128,4096]{1,0:T(8,128)(2,1)}, bf16[128,4096]{1,0:T(8,128)(2,1)S(1)}, u32[]{:S(2)}, u32[]{:S(2)}) collective-permute-start(bf16[128,4096]{1,0:T(8,128)(2,1)} %collective-permute-done.1.refs_2_), channel_id=1, source_target_pairs={{1,0},{2,3},{5,4},{6,7},{9,8},{10,11},{13,12},{14,15},{17,16},{18,... | collective-permute-start | bytes 3145736 | tf_op jit(solution)/shard_map/ppermute | solution.py:532
  30.8 27.2 %collective-permute-start.4 = (bf16[128,4096]{1,0:T(8,128)(2,1)}, bf16[128,4096]{1,0:T(8,128)(2,1)}, u32[]{:S(2)}, u32[]{:S(2)}) collective-permute-start(bf16[128,4096]{1,0:T(8,128)(2,1)} %collective-permute-done.refs_1_), channel_id=1, source_target_pairs={{1,2},{2,1},{5,6},{6,5},{9,10},{10,9},{13,14},{14,13},{17,18},{18,... | collective-permute-start | bytes 3145736 | tf_op jit(solution)/shard_map/ppermute | solution.py:532
  44.9 13.1 %copy-start.5 = (bf16[3,512,512]{2,1,0:T(8,128)(2,1)}, bf16[3,512,512]{2,1,0:T(8,128)(2,1)S(1)}, u32[]{:S(2)}) copy-start(bf16[3,512,512]{2,1,0:T(8,128)(2,1)S(1)} %collective-permute-done.5.refs_5_.refs_11_) | copy-start | bytes 4718596
  47.2 7.7 %collective-permute-start.7 = (bf16[512,256]{1,0:T(8,128)(2,1)S(1)}, bf16[512,256]{1,0:T(8,128)(2,1)S(1)}, u32[]{:S(2)}, u32[]{:S(2)}) collective-permute-start(bf16[512,256]{1,0:T(8,128)(2,1)S(1)} %get-tuple-element.120), channel_id=1, source_target_pairs={{0,16},{8,24},{16,0},{24,8},{1,17},{9,25},{17,1},{25,9},{2,18},{10... | collective-permute-start | bytes 786440 | tf_op jit(solution)/shard_map/ppermute | solution.py:51
  48.8 7.4 %collective-permute-start.8 = (bf16[512,256]{1,0:T(8,128)(2,1)S(1)}, bf16[512,256]{1,0:T(8,128)(2,1)}, u32[]{:S(2)}, u32[]{:S(2)}) collective-permute-start(bf16[512,256]{1,0:T(8,128)(2,1)S(1)} %get-tuple-element.119), channel_id=1, source_target_pairs={{0,8},{8,0},{16,24},{24,16},{1,9},{9,1},{17,25},{25,17},{2,10},{10... | collective-permute-start | bytes 786440 | tf_op jit(solution)/shard_map/ppermute | solution.py:51
  54.9 76.0 %copy-start.16 = (bf16[512,256]{1,0:T(8,128)(2,1)}, bf16[512,256]{1,0:T(8,128)(2,1)S(1)}, u32[]{:S(2)}) copy-start(bf16[512,256]{1,0:T(8,128)(2,1)S(1)} %collective-permute-done.7.refs_3_) | copy-start | bytes 786436
  58.0 1.0 copy-start.11
  58.0 5.3 %collective-permute-start.11 = (bf16[3,512,512]{2,1,0:T(8,128)(2,1)S(1)}, bf16[3,512,512]{2,1,0:T(8,128)(2,1)S(1)}, u32[]{:S(2)}, u32[]{:S(2)}) collective-permute-start(bf16[3,512,512]{2,1,0:T(8,128)(2,1)S(1)} %collective-permute-done.5.refs_5_.refs_11_), channel_id=1, source_target_pairs={{0,4},{4,0},{1,5},{5,1},{2,6},{6,2},{3,7},{7,3},{8,12},{12,8},{9,1... | collective-permute-start | bytes 4718600 | tf_op jit(solution)/shard_map/ppermute | solution.py:535
  59.0 5.1 %collective-permute-start.12 = (bf16[3,512,512]{2,1,0:T(8,128)(2,1)}, bf16[3,512,512]{2,1,0:T(8,128)(2,1)}, u32[]{:S(2)}, u32[]{:S(2)}) collective-permute-start(bf16[3,512,512]{2,1,0:T(8,128)(2,1)} %collective-permute-done.6.refs_6_.refs_12_), channel_id=1, source_target_pairs={{0,4},{4,0},{1,5},{5,1},{2,6},{6,2},{3,7},{7,3},{8,12},{12,8},{9,1... | collective-permute-start | bytes 4718600 | tf_op jit(solution)/shard_map/ppermute | solution.py:535
  59.0 20.3 %collective-permute-start.9 = (bf16[3,256,512]{2,1,0:T(8,128)(2,1)}, bf16[3,256,512]{2,1,0:T(8,128)(2,1)}, u32[]{:S(2)}, u32[]{:S(2)}) collective-permute-start(bf16[3,256,512]{2,1,0:T(8,128)(2,1)} %slice.32), channel_id=1, source_target_pairs={{0,8},{8,0},{16,24},{24,16},{1,9},{9,1},{17,25},{25,17},{2,10},{10... | collective-permute-start | bytes 2359304 | tf_op jit(solution)/shard_map/ppermute | solution.py:51
  60.5 20.0 %collective-permute-start.10 = (bf16[3,256,512]{2,1,0:T(8,128)(2,1)}, bf16[3,256,512]{2,1,0:T(8,128)(2,1)}, u32[]{:S(2)}, u32[]{:S(2)}) collective-permute-start(bf16[3,256,512]{2,1,0:T(8,128)(2,1)} %slice.33), channel_id=1, source_target_pairs={{0,16},{8,24},{16,0},{24,8},{1,17},{9,25},{17,1},{25,9},{2,18},{10... | collective-permute-start | bytes 2359304 | tf_op jit(solution)/shard_map/ppermute | solution.py:51
  62.0 27.7 %collective-permute-start.13 = (bf16[128,4096]{1,0:T(8,128)(2,1)}, bf16[128,4096]{1,0:T(8,128)(2,1)}, u32[]{:S(2)}, u32[]{:S(2)}) collective-permute-start(bf16[128,4096]{1,0:T(8,128)(2,1)} %collective-permute-done.4.refs_4_), channel_id=1, source_target_pairs={{1,0},{2,3},{5,4},{6,7},{9,8},{10,11},{13,12},{14,15},{17,16},{18,... | collective-permute-start | bytes 3145736 | tf_op jit(solution)/shard_map/ppermute | solution.py:532
  63.3 1.2 copy-start.8
  64.5 25.2 %copy-start.9 = (bf16[512,512]{1,0:T(8,128)(2,1)S(1)}, bf16[512,512]{1,0:T(8,128)(2,1)}, u32[]{:S(2)}) copy-start(bf16[512,512]{1,0:T(8,128)(2,1)} %refs_2_.3) | copy-start | bytes 1572868
  80.5 9.3 %collective-permute-start.14 = (bf16[3,256,512]{2,1,0:T(8,128)(2,1)}, bf16[3,256,512]{2,1,0:T(8,128)(2,1)S(1)}, u32[]{:S(2)}, u32[]{:S(2)}) collective-permute-start(bf16[3,256,512]{2,1,0:T(8,128)(2,1)} %collective-permute-done.9.refs_6_), channel_id=1, source_target_pairs={{0,4},{4,0},{1,5},{5,1},{2,6},{6,2},{3,7},{7,3},{8,12},{12,8},{9,1... | collective-permute-start | bytes 2359304 | tf_op jit(solution)/shard_map/ppermute | solution.py:535
  80.5 9.3 %collective-permute-start.15 = (bf16[3,256,512]{2,1,0:T(8,128)(2,1)}, bf16[3,256,512]{2,1,0:T(8,128)(2,1)S(1)}, u32[]{:S(2)}, u32[]{:S(2)}) collective-permute-start(bf16[3,256,512]{2,1,0:T(8,128)(2,1)} %collective-permute-done.10.refs_7_), channel_id=1, source_target_pairs={{0,4},{4,0},{1,5},{5,1},{2,6},{6,2},{3,7},{7,3},{8,12},{12,8},{9,1... | collective-permute-start | bytes 2359304 | tf_op jit(solution)/shard_map/ppermute | solution.py:535
  89.8 0.9 copy-start.20
  89.8 1.1 copy-start.21
  89.8 12.8 %collective-permute-start.16 = (bf16[512,512]{1,0:T(8,128)(2,1)S(1)}, bf16[512,512]{1,0:T(8,128)(2,1)S(1)}, u32[]{:S(2)}, u32[]{:S(2)}) collective-permute-start(bf16[512,512]{1,0:T(8,128)(2,1)S(1)} %copy-done.9), channel_id=1, source_target_pairs={{0,1},{1,0},{2,3},{3,2},{4,5},{5,4},{6,7},{7,6},{8,9},{9,8},{10,11... | collective-permute-start | bytes 1572872 | tf_op jit(solution)/shard_map/ppermute | solution.py:532
  89.9 12.7 %collective-permute-start.17 = (bf16[512,512]{1,0:T(8,128)(2,1)S(1)}, bf16[512,512]{1,0:T(8,128)(2,1)S(1)}, u32[]{:S(2)}, u32[]{:S(2)}) collective-permute-start(bf16[512,512]{1,0:T(8,128)(2,1)S(1)} %copy-done.9), channel_id=1, source_target_pairs={{1,2},{2,1},{5,6},{6,5},{9,10},{10,9},{13,14},{14,13},{17,18},{18,... | collective-permute-start | bytes 1572872 | tf_op jit(solution)/shard_map/ppermute | solution.py:532
  102.6 27.2 %copy-start.15 = (bf16[512,512]{1,0:T(8,128)(2,1)}, bf16[512,512]{1,0:T(8,128)(2,1)S(1)}, u32[]{:S(2)}) copy-start(bf16[512,512]{1,0:T(8,128)(2,1)S(1)} %collective-permute-done.16) | copy-start | bytes 1572868
  102.6 21.4 %all-to-all-start = ((bf16[4,3,4,128,128]{4,3,2,1,0:T(8,128)(2,1)}), bf16[4,3,4,128,128]{4,3,2,1,0:T(8,128)(2,1)S(1)}, u32[]{:S(2)}, u32[]{:S(2)}) async-start(bf16[4,3,4,128,128]{4,3,2,1,0:T(8,128)(2,1)} %enter.1), calls=%async_computation | async-start | bytes 3145728 | tf_op jit(solution)/shard_map/all_to_all | solution.py:451
  106.2 2.8 %collective-permute-start.18 = (bf16[512,512]{1,0:T(8,128)(2,1)S(1)}, bf16[512,512]{1,0:T(8,128)(2,1)}, u32[]{:S(2)}, u32[]{:S(2)}) collective-permute-start(bf16[512,512]{1,0:T(8,128)(2,1)S(1)} %collective-permute-done.16), channel_id=1, source_target_pairs={{1,2},{2,1},{5,6},{6,5},{9,10},{10,9},{13,14},{14,13},{17,18},{18,... | collective-permute-start | bytes 1572872 | tf_op jit(solution)/shard_map/ppermute | solution.py:532
  107.7 16.4 %collective-permute-start.19 = (bf16[512,512]{1,0:T(8,128)(2,1)S(1)}, bf16[512,512]{1,0:T(8,128)(2,1)}, u32[]{:S(2)}, u32[]{:S(2)}) collective-permute-start(bf16[512,512]{1,0:T(8,128)(2,1)S(1)} %collective-permute-done.17), channel_id=1, source_target_pairs={{1,0},{2,3},{5,4},{6,7},{9,8},{10,11},{13,12},{14,15},{17,16},{18,... | collective-permute-start | bytes 1572872 | tf_op jit(solution)/shard_map/ppermute | solution.py:532
  124.0 6.9 %collective-permute-start.20 = (bf16[4,3,4,128,128]{4,3,2,1,0:T(8,128)(2,1)S(1)}, bf16[4,3,4,128,128]{4,3,2,1,0:T(8,128)(2,1)S(1)}, u32[]{:S(2)}, u32[]{:S(2)}) collective-permute-start(bf16[4,3,4,128,128]{4,3,2,1,0:T(8,128)(2,1)S(1)} %all-to-all-done.refs_0_), channel_id=1, source_target_pairs={{0,4},{4,0},{1,5},{5,1},{2,6},{6,2},{3,7},{7,3},{8,12},{12,8},{9,1... | collective-permute-start | bytes 4718600 | tf_op jit(solution)/shard_map/ppermute | solution.py:47
  124.0 17.8 %collective-permute-start.21 = (bf16[512,512]{1,0:T(8,128)(2,1)}, bf16[512,512]{1,0:T(8,128)(2,1)}, u32[]{:S(2)}, u32[]{:S(2)}) collective-permute-start(bf16[512,512]{1,0:T(8,128)(2,1)} %collective-permute-done.18), channel_id=1, source_target_pairs={{1,0},{2,3},{5,4},{6,7},{9,8},{10,11},{13,12},{14,15},{17,16},{18,... | collective-permute-start | bytes 1572872 | tf_op jit(solution)/shard_map/ppermute | solution.py:532
  126.5 15.3 %collective-permute-start.22 = (bf16[1024,256]{1,0:T(8,128)(2,1)S(1)}, bf16[1024,256]{1,0:T(8,128)(2,1)}, u32[]{:S(2)}, u32[]{:S(2)}) collective-permute-start(bf16[1024,256]{1,0:T(8,128)(2,1)S(1)} %get-tuple-element.116), channel_id=1, source_target_pairs={{0,16},{8,24},{16,0},{24,8},{1,17},{9,25},{17,1},{25,9},{2,18},{10... | collective-permute-start | bytes 1572872 | tf_op jit(solution)/shard_map/ppermute | solution.py:51
  128.3 14.2 %collective-permute-start.23 = (bf16[1024,256]{1,0:T(8,128)(2,1)S(1)}, bf16[1024,256]{1,0:T(8,128)(2,1)}, u32[]{:S(2)}, u32[]{:S(2)}) collective-permute-start(bf16[1024,256]{1,0:T(8,128)(2,1)S(1)} %get-tuple-element.115), channel_id=1, source_target_pairs={{0,8},{8,0},{16,24},{24,16},{1,9},{9,1},{17,25},{25,17},{2,10},{10... | collective-permute-start | bytes 1572872 | tf_op jit(solution)/shard_map/ppermute | solution.py:51
  129.8 21.7 %collective-permute-start.24 = (bf16[512,512]{1,0:T(8,128)(2,1)S(1)}, bf16[512,512]{1,0:T(8,128)(2,1)}, u32[]{:S(2)}, u32[]{:S(2)}) collective-permute-start(bf16[512,512]{1,0:T(8,128)(2,1)S(1)} %copy-done.9), channel_id=1, source_target_pairs={{0,4},{4,0},{1,5},{5,1},{2,6},{6,2},{3,7},{7,3},{8,12},{12,8},{9,1... | collective-permute-start | bytes 1572872 | tf_op jit(solution)/shard_map/ppermute | solution.py:535
  130.9 17.3 %copy-start.6 = (bf16[1024,512]{1,0:T(8,128)(2,1)}, bf16[1024,512]{1,0:T(8,128)(2,1)S(1)}, u32[]{:S(2)}) copy-start(bf16[1024,512]{1,0:T(8,128)(2,1)S(1)} %pad_maximum_fusion.refs_8_) | copy-start | bytes 3145732
  130.9 20.7 %collective-permute-start.25 = (bf16[512,256]{1,0:T(8,128)(2,1)S(1)}, bf16[512,256]{1,0:T(8,128)(2,1)}, u32[]{:S(2)}, u32[]{:S(2)}) collective-permute-start(bf16[512,256]{1,0:T(8,128)(2,1)S(1)} %collective-permute-done.7.refs_3_), channel_id=1, source_target_pairs={{0,4},{4,0},{1,5},{5,1},{2,6},{6,2},{3,7},{7,3},{8,12},{12,8},{9,1... | collective-permute-start | bytes 786440 | tf_op jit(solution)/shard_map/ppermute | solution.py:535
  141.8 10.2 %collective-permute-start.26 = (bf16[512,256]{1,0:T(8,128)(2,1)}, bf16[512,256]{1,0:T(8,128)(2,1)}, u32[]{:S(2)}, u32[]{:S(2)}) collective-permute-start(bf16[512,256]{1,0:T(8,128)(2,1)} %collective-permute-done.8.refs_4_), channel_id=1, source_target_pairs={{0,4},{4,0},{1,5},{5,1},{2,6},{6,2},{3,7},{7,3},{8,12},{12,8},{9,1... | collective-permute-start | bytes 786440 | tf_op jit(solution)/shard_map/ppermute | solution.py:535
  142.5 22.3 %all-to-all-start.1 = ((bf16[16,128,128]{2,1,0:T(8,128)(2,1)}), bf16[16,128,128]{2,1,0:T(8,128)(2,1)S(1)}, u32[]{:S(2)}, u32[]{:S(2)}) async-start(bf16[16,128,128]{2,1,0:T(8,128)(2,1)} %attention.1), calls=%async_computation.1 | async-start | bytes 1048576 | tf_op jit(solution)/shard_map/all_to_all | solution.py:576
  148.2 16.5 %collective-permute-start.27 = (bf16[1024,512]{1,0:T(8,128)(2,1)S(1)}, bf16[1024,512]{1,0:T(8,128)(2,1)}, u32[]{:S(2)}, u32[]{:S(2)}) collective-permute-start(bf16[1024,512]{1,0:T(8,128)(2,1)S(1)} %pad_maximum_fusion.refs_8_), channel_id=1, source_target_pairs={{0,4},{4,0},{1,5},{5,1},{2,6},{6,2},{3,7},{7,3},{8,12},{12,8},{9,1... | collective-permute-start | bytes 3145736 | tf_op jit(solution)/shard_map/ppermute | solution.py:535
  149.4 18.2 %copy-start.7 = (bf16[512,512]{1,0:T(8,128)(2,1)}, bf16[512,512]{1,0:T(8,128)(2,1)S(1)}, u32[]{:S(2)}) copy-start(bf16[512,512]{1,0:T(8,128)(2,1)S(1)} %broadcast_select_fusion.refs_14_) | copy-start | bytes 1572868
  149.5 11.8 %collective-permute-start.31 = (bf16[512,256]{1,0:T(8,128)(2,1)S(1)}, bf16[512,256]{1,0:T(8,128)(2,1)S(1)}, u32[]{:S(2)}, u32[]{:S(2)}) collective-permute-start(bf16[512,256]{1,0:T(8,128)(2,1)S(1)} %get-tuple-element.118), channel_id=1, source_target_pairs={{0,16},{8,24},{16,0},{24,8},{1,17},{9,25},{17,1},{25,9},{2,18},{10... | collective-permute-start | bytes 786440 | tf_op jit(solution)/shard_map/ppermute | solution.py:51
  151.4 11.0 %collective-permute-start.28 = (bf16[1024,256]{1,0:T(8,128)(2,1)}, bf16[1024,256]{1,0:T(8,128)(2,1)S(1)}, u32[]{:S(2)}, u32[]{:S(2)}) collective-permute-start(bf16[1024,256]{1,0:T(8,128)(2,1)} %collective-permute-done.22.refs_9_), channel_id=1, source_target_pairs={{0,4},{4,0},{1,5},{5,1},{2,6},{6,2},{3,7},{7,3},{8,12},{12,8},{9,1... | collective-permute-start | bytes 1572872 | tf_op jit(solution)/shard_map/ppermute | solution.py:535
  151.7 11.3 %collective-permute-start.29 = (bf16[1024,256]{1,0:T(8,128)(2,1)}, bf16[1024,256]{1,0:T(8,128)(2,1)S(1)}, u32[]{:S(2)}, u32[]{:S(2)}) collective-permute-start(bf16[1024,256]{1,0:T(8,128)(2,1)} %collective-permute-done.23.refs_10_), channel_id=1, source_target_pairs={{0,4},{4,0},{1,5},{5,1},{2,6},{6,2},{3,7},{7,3},{8,12},{12,8},{9,1... | collective-permute-start | bytes 1572872 | tf_op jit(solution)/shard_map/ppermute | solution.py:535
  152.0 10.5 %collective-permute-start.33 = (bf16[512,256]{1,0:T(8,128)(2,1)S(1)}, bf16[512,256]{1,0:T(8,128)(2,1)S(1)}, u32[]{:S(2)}, u32[]{:S(2)}) collective-permute-start(bf16[512,256]{1,0:T(8,128)(2,1)S(1)} %get-tuple-element.117), channel_id=1, source_target_pairs={{0,8},{8,0},{16,24},{24,16},{1,9},{9,1},{17,25},{25,17},{2,10},{10... | collective-permute-start | bytes 786440 | tf_op jit(solution)/shard_map/ppermute | solution.py:51
  161.3 2.7 %copy-start.17 = (bf16[512,256]{1,0:T(8,128)(2,1)}, bf16[512,256]{1,0:T(8,128)(2,1)S(1)}, u32[]{:S(2)}) copy-start(bf16[512,256]{1,0:T(8,128)(2,1)S(1)} %collective-permute-done.31.refs_15_) | copy-start | bytes 786436
  161.3 1.9 collective-permute-start.30
  162.4 5.2 %copy-start.18 = (bf16[512,256]{1,0:T(8,128)(2,1)}, bf16[512,256]{1,0:T(8,128)(2,1)S(1)}, u32[]{:S(2)}) copy-start(bf16[512,256]{1,0:T(8,128)(2,1)S(1)} %collective-permute-done.33.refs_16_) | copy-start | bytes 786436
  162.4 1.5 collective-permute-start.32
  162.5 5.2 %copy-start.12 = (bf16[1024,256]{1,0:T(8,128)(2,1)}, bf16[1024,256]{1,0:T(8,128)(2,1)S(1)}, u32[]{:S(2)}) copy-start(bf16[1024,256]{1,0:T(8,128)(2,1)S(1)} %collective-permute-done.28.refs_12_) | copy-start | bytes 1572868
  162.5 2.2 %collective-permute-start.34 = (bf16[512,256]{1,0:T(8,128)(2,1)S(1)}, bf16[512,256]{1,0:T(8,128)(2,1)}, u32[]{:S(2)}, u32[]{:S(2)}) collective-permute-start(bf16[512,256]{1,0:T(8,128)(2,1)S(1)} %collective-permute-done.33.refs_16_), channel_id=1, source_target_pairs={{0,4},{4,0},{1,5},{5,1},{2,6},{6,2},{3,7},{7,3},{8,12},{12,8},{9,1... | collective-permute-start | bytes 786440 | tf_op jit(solution)/shard_map/ppermute | solution.py:535
  163.0 4.7 %copy-start.13 = (bf16[1024,256]{1,0:T(8,128)(2,1)}, bf16[1024,256]{1,0:T(8,128)(2,1)S(1)}, u32[]{:S(2)}) copy-start(bf16[1024,256]{1,0:T(8,128)(2,1)S(1)} %collective-permute-done.29.refs_13_) | copy-start | bytes 1572868
  164.7 2.9 %copy-start.10 = (bf16[16,128,128]{2,1,0:T(8,128)(2,1)}, bf16[16,128,128]{2,1,0:T(8,128)(2,1)S(1)}, u32[]{:S(2)}) copy-start(bf16[16,128,128]{2,1,0:T(8,128)(2,1)S(1)} %all-to-all-done.1.refs_0_.refs_1_) | copy-start | bytes 1572868
  164.7 14.3 %collective-permute-start.35 = (bf16[16,128,128]{2,1,0:T(8,128)(2,1)S(1)}, bf16[16,128,128]{2,1,0:T(8,128)(2,1)S(1)}, u32[]{:S(2)}, u32[]{:S(2)}) collective-permute-start(bf16[16,128,128]{2,1,0:T(8,128)(2,1)S(1)} %all-to-all-done.1.refs_0_.refs_1_), channel_id=1, source_target_pairs={{0,8},{8,0},{16,24},{24,16},{1,9},{9,1},{17,25},{25,17},{2,10},{10... | collective-permute-start | bytes 1572872 | tf_op jit(solution)/shard_map/ppermute | solution.py:51
  166.8 13.7 %collective-permute-start.36 = (bf16[16,128,128]{2,1,0:T(8,128)(2,1)S(1)}, bf16[16,128,128]{2,1,0:T(8,128)(2,1)S(1)}, u32[]{:S(2)}, u32[]{:S(2)}) collective-permute-start(bf16[16,128,128]{2,1,0:T(8,128)(2,1)S(1)} %all-to-all-done.1.refs_0_.refs_1_), channel_id=1, source_target_pairs={{0,16},{8,24},{16,0},{24,8},{1,17},{9,25},{17,1},{25,9},{2,18},{10... | collective-permute-start | bytes 1572872 | tf_op jit(solution)/shard_map/ppermute | solution.py:51
  179.0 1.5 copy-start.22
  180.5 0.8 copy-start.23
  181.2 14.8 %copy-start.2 = (bf16[128,1024]{1,0:T(8,128)(2,1)S(1)}, bf16[128,1024]{1,0:T(8,128)(2,1)}, u32[]{:S(2)}) copy-start(bf16[128,1024]{1,0:T(8,128)(2,1)} %get-tuple-element.105.own_x) | copy-start | bytes 786436
  181.3 14.8 %copy-start.3 = (bf16[128,1024]{1,0:T(8,128)(2,1)S(1)}, bf16[128,1024]{1,0:T(8,128)(2,1)}, u32[]{:S(2)}) copy-start(bf16[128,1024]{1,0:T(8,128)(2,1)} %get-tuple-element.106.own_y) | copy-start | bytes 786436
  188.0 7.5 %collective-permute-start.37 = (bf16[128,1024]{1,0:T(8,128)(2,1)}, bf16[128,1024]{1,0:T(8,128)(2,1)S(1)}, u32[]{:S(2)}, u32[]{:S(2)}) collective-permute-start(bf16[128,1024]{1,0:T(8,128)(2,1)} %get-tuple-element.109), channel_id=1, source_target_pairs={{0,8},{8,0},{16,24},{24,16},{1,9},{9,1},{17,25},{25,17},{2,10},{10... | collective-permute-start | bytes 786440 | tf_op jit(solution)/shard_map/ppermute | solution.py:51
  188.6 7.5 %collective-permute-start.38 = (bf16[128,1024]{1,0:T(8,128)(2,1)}, bf16[128,1024]{1,0:T(8,128)(2,1)S(1)}, u32[]{:S(2)}, u32[]{:S(2)}) collective-permute-start(bf16[128,1024]{1,0:T(8,128)(2,1)} %get-tuple-element.110), channel_id=1, source_target_pairs={{0,16},{8,24},{16,0},{24,8},{1,17},{9,25},{17,1},{25,9},{2,18},{10... | collective-permute-start | bytes 786440 | tf_op jit(solution)/shard_map/ppermute | solution.py:51
  (3 other events, 2.2 us)

commit v5 on v4

--- a/solution.py
+++ b/solution.py
@@ -51,17 +51,23 @@
     return lax.ppermute(part, "head", xor_pairs(4, bit))
 
 
+def normalize_rows(rows, order, gain):
+    width = rows.shape[1] // order.shape[0]
+    parts = [slice(r * width, (r + 1) * width) for r in range(order.shape[0])]
+    total = None
+    for part in parts:
+        features = rows[:, part].astype(F32)
+        squares = jnp.sum(features * features, axis=-1, keepdims=True)
+        total = squares if total is None else total + squares
+    scale = lax.rsqrt(total * (1.0 / rows.shape[1]) + EPSILON)
+    for r, part in enumerate(parts):
+        place = pl.ds(pl.multiple_of(order[r] * width, width), width)
+        rows[:, part] = (rows[:, part].astype(F32) * scale * gain[:, place]).astype(BF16)
+
+
 def normalize_kernel(order, tokens, gain, out):
-    features = tokens[...].astype(F32)
-    mean_square = jnp.mean(features * features, axis=-1, keepdims=True)
-    scale = lax.rsqrt(mean_square + EPSILON)
-    count = order.shape[0]
-    width = tokens.shape[1] // count
-    for r in range(count):
-        source = pl.ds(pl.multiple_of(order[r] * width, width), width)
-        out[:, r * width : (r + 1) * width] = (
-            tokens[:, source].astype(F32) * scale * gain[:, source]
-        ).astype(BF16)
+    out[...] = tokens[...]
+    normalize_rows(out, order, gain)
 
 
 def normalize(tokens, norm_gain, order):
@@ -73,7 +79,7 @@
         out_specs=vmem,
         compiler_params=pltpu.CompilerParams(vmem_limit_bytes=16 << 20),
         name="normalize",
-    )(order, tokens, norm_gain.reshape(1, -1))
+    )(order, tokens, norm_gain)
 
 
 def attention_kernel(sizes, places, biases, turns, ends, targets, *refs):
@@ -223,14 +229,21 @@
     )(planes, order, *landed, *arrays)
 
 
-def fetch(flag, choices, columns, target, sem):
-    copies = [pltpu.make_async_copy(ref.at[:, columns], target, sem) for ref in choices]
-    if len(copies) == 1:
-        copies[0].start()
+def fetch(flag, order, choices, target, sem):
+    count = order.shape[0]
+    width = target.shape[1] // count
+
+    def start(ref):
+        for r in range(count):
+            source = ref.at[:, pl.ds(pl.multiple_of(order[r] * width, width), width)]
+            pltpu.make_async_copy(source, target.at[:, pl.ds(r * width, width)], sem).start()
+
+    if len(choices) == 1:
+        start(choices[0])
     else:
-        for choice, copy in enumerate(copies):
-            pl.when(flag[0] == choice)(copy.start)
-    return copies[0]
+        for choice, ref in enumerate(choices):
+            pl.when(flag[0] == choice)(functools.partial(start, ref))
+    return pltpu.make_async_copy(choices[0], target, sem)
 
 
 def split(refs, counts):
@@ -253,17 +266,27 @@
     return copies
 
 
-def begin_kernel(counts, runs, places, flag, *refs):
+def begin_kernel(counts, runs, rest, places, raw, flag, order, gain, *refs):
     chunks = split(refs, counts)
-    arrays = refs[sum(counts) : -5]
-    out, weights, rows, row_sems, sems = refs[-5:]
-    waits = [
-        fetch(flag, chunk, pl.ds(0, rows.shape[1]), rows.at[pl.ds(n * BLK, BLK)], row_sems.at[n])
-        for n, chunk in enumerate(chunks)
-    ]
+    arrays = refs[sum(counts) : -6]
+    out, left, weights, rows, row_sems, sems = refs[-6:]
+    waits = []
+    for n, chunk in enumerate(chunks):
+        target = rows.at[pl.ds(n * BLK, BLK)]
+        if raw:
+            waits.append(fetch(flag, order, chunk, target, row_sems.at[n]))
+        else:
+            waits.append(pltpu.make_async_copy(chunk[0], target, row_sems.at[n]))
+            waits[-1].start()
     copies = fetch_weights(arrays, places, weights, sems)
     for wait in waits:
         wait.wait()
+    if raw:
+        normalize_rows(rows, order, gain)
+    at = 0
+    for first, size in rest:
+        left[:, at : at + size] = rows[:, first : first + size]
+        at += size
     for c in range(3):
         for copy in copies[c]:
             copy.wait()
@@ -276,126 +299,135 @@
         out[c] = total
 
 
-def begin(flag, chunks, arrays, runs):
+def begin(flag, order, gain, chunks, arrays, runs, rest, raw):
     chunks = [chunk if isinstance(chunk, tuple) else (chunk,) for chunk in chunks]
     counts = [len(chunk) for chunk in chunks]
     features, width = chunks[0][0].shape[1], arrays[0].shape[2]
+    rows = len(chunks) * BLK
     places, at = [], 0
     for array in arrays:
         places.append(at)
         at += array.shape[1]
+    smem = pl.BlockSpec(memory_space=pltpu.SMEM)
+    vmem = pl.BlockSpec(memory_space=pltpu.VMEM)
     hbm = pl.BlockSpec(memory_space=pl.ANY)
     rows_in = [array for chunk in chunks for array in chunk]
     return pl.pallas_call(
-        functools.partial(begin_kernel, counts, runs, places),
-        out_shape=jax.ShapeDtypeStruct((3, len(chunks) * BLK, width), F32),
-        in_specs=[pl.BlockSpec(memory_space=pltpu.SMEM)] + [hbm] * (len(rows_in) + len(arrays)),
-        out_specs=pl.BlockSpec(memory_space=pltpu.VMEM),
+        functools.partial(begin_kernel, counts, runs, rest, places, raw),
+        out_shape=(
+            jax.ShapeDtypeStruct((3, rows, width), F32),
+            jax.ShapeDtypeStruct((rows, max(HEAD_DIM, sum(size for _, size in rest))), BF16),
+        ),
+        in_specs=[smem, smem, vmem] + [hbm] * (len(rows_in) + len(arrays)),
+        out_specs=(vmem, vmem),
         scratch_shapes=[
             pltpu.VMEM((3, at, width), BF16),
-            pltpu.VMEM((len(chunks) * BLK, features), BF16),
+            pltpu.VMEM((rows, features), BF16),
             pltpu.SemaphoreType.DMA((len(chunks),)),
             pltpu.SemaphoreType.DMA((3, len(arrays))),
         ],
         compiler_params=pltpu.CompilerParams(vmem_limit_bytes=58 << 20),
         cost_estimate=pl.CostEstimate(flops=1, bytes_accessed=1, transcendentals=0),
         name="begin",
-    )(flag, *rows_in, *arrays)
-
-
-def enter_kernel(heads, counts, runs, rest, places, flag, begun, *refs):
-    chunks = split(refs, counts)
-    arrays = refs[sum(counts) : -8]
-    out, weights, rows, last, so_far, row_sems, sems, begun_sem = refs[-8:]
-    waits = []
-    for n, chunk in enumerate(chunks):
-        at = 0
-        for first, size in runs:
-            target = rows.at[pl.ds(n * BLK, BLK), pl.ds(at, size)]
-            waits.append(fetch(flag, chunk, pl.ds(first, size), target, row_sems.at[len(waits)]))
-            at += size
+    )(flag, order, gain, *rows_in, *arrays)
+
+
+def enter_kernel(heads, runs, rest, places, flag, order, gain, begun, left, *refs):
+    chunk, arrays = refs[:2], refs[2:-7]
+    out, weights, rows, last, so_far, other_sems, sems = refs[-7:]
+    early = so_far.shape[1]
+    last_copy = fetch(flag, order, chunk, last, other_sems.at[0])
+    left_copy = pltpu.make_async_copy(left, rows.at[pl.ds(0, early)], other_sems.at[1])
+    begun_copy = pltpu.make_async_copy(begun, so_far, other_sems.at[2])
+    left_copy.start()
+    copies = fetch_weights(arrays, places, weights, sems)
+    begun_copy.start()
+    last_copy.wait()
+    normalize_rows(last, order, gain)
+    at = 0
+    for first, size in runs:
+        rows[early:, at : at + size] = last[:, first : first + size]
+        at += size
     common = at
-    at = 0
-    for first, size in rest:
-        waits.append(fetch(flag, chunks[-1], pl.ds(first, size), last.at[:, pl.ds(at, size)], row_sems.at[len(waits)]))
-        at += size
-    copies = fetch_weights(arrays, places, weights, sems)
-    begun_copy = pltpu.make_async_copy(begun, so_far, begun_sem)
-    begun_copy.start()
-    for wait in waits:
-        wait.wait()
-    early = so_far.shape[1]
+    left_copy.wait()
     for c in range(3):
         for copy in copies[c]:
             copy.wait()
         if c == 0:
             begun_copy.wait()
         total = jnp.dot(rows[...], weights[c, :common], preferred_element_type=F32)
-        final = total[early:] + jnp.dot(last[...], weights[c, common:], preferred_element_type=F32)
+        final = total[early:]
+        at = common
+        for first, size in rest:
+            final = final + jnp.dot(
+                last[:, first : first + size], weights[c, at : at + size], preferred_element_type=F32
+            )
+            at += size
         parts = [(so_far[c] + total[:early]).astype(BF16), final.astype(BF16)]
-        for n in range(len(chunks)):
+        for n in range(early // BLK + 1):
             part, row = (parts[1], 0) if n * BLK == early else (parts[0], n * BLK)
             for h in range(heads):
                 out[h, c, n] = part[row : row + BLK, h * HEAD_DIM : (h + 1) * HEAD_DIM]
 
 
-def enter(flag, begun, chunks, arrays, places, runs, rest, heads):
-    chunks = [chunk if isinstance(chunk, tuple) else (chunk,) for chunk in chunks]
-    counts = [len(chunk) for chunk in chunks]
-    features, width = chunks[0][0].shape[1], arrays[0].shape[2]
-    common = sum(size for _, size in runs)
+def enter(flag, order, gain, begun, left, chunk, arrays, places, runs, rest, heads):
+    features, width = chunk[0].shape[1], arrays[0].shape[2]
+    early, common = left.shape
+    smem = pl.BlockSpec(memory_space=pltpu.SMEM)
+    vmem = pl.BlockSpec(memory_space=pltpu.VMEM)
     hbm = pl.BlockSpec(memory_space=pl.ANY)
-    rows_in = [array for chunk in chunks for array in chunk]
     return pl.pallas_call(
-        functools.partial(enter_kernel, heads, counts, runs, rest, places),
-        out_shape=jax.ShapeDtypeStruct((heads, 3, len(chunks), BLK, HEAD_DIM), BF16),
-        in_specs=[pl.BlockSpec(memory_space=pltpu.SMEM)] + [hbm] * (1 + len(rows_in) + len(arrays)),
-        out_specs=pl.BlockSpec(memory_space=pltpu.VMEM),
+        functools.partial(enter_kernel, heads, runs, rest, places),
+        out_shape=jax.ShapeDtypeStruct((heads, 3, early // BLK + 1, BLK, HEAD_DIM), BF16),
+        in_specs=[smem, smem, vmem] + [hbm] * (4 + len(arrays)),
+        out_specs=vmem,
         scratch_shapes=[
             pltpu.VMEM((3, features, width), BF16),
-            pltpu.VMEM((len(chunks) * BLK, common), BF16),
-            pltpu.VMEM((BLK, features - common), BF16),
+            pltpu.VMEM((early + BLK, common), BF16),
+            pltpu.VMEM((BLK, features), BF16),
             pltpu.VMEM(begun.shape, F32),
-            pltpu.SemaphoreType.DMA((len(chunks) * len(runs) + len(rest),)),
+            pltpu.SemaphoreType.DMA((3,)),
             pltpu.SemaphoreType.DMA((3, len(arrays))),
-            pltpu.SemaphoreType.DMA,
         ],
         compiler_params=pltpu.CompilerParams(vmem_limit_bytes=58 << 20),
         cost_estimate=pl.CostEstimate(flops=1, bytes_accessed=1, transcendentals=0),
         name="enter",
-    )(flag, begun, *rows_in, *arrays)
+    )(flag, order, gain, begun, left, *chunk, *arrays)
 
 
 def leave_kernel(heads, lines, count, order, *refs):
     landed, pieces = refs[:2], refs[2 : 2 + 6 * count]
     outs = refs[2 + 6 * count : 4 + 6 * count]
-    weights, rows, sems = refs[4 + 6 * count :]
+    both, beside, rows, sems = refs[4 + 6 * count :]
     depth = heads * HEAD_DIM
-    width = weights.shape[3]
+    width = beside.shape[3]
     copies = []
-    for side in range(2):
-        for i in range(4):
+    for kind in range(3):
+        for core in range(2):
             at = 0
             for b in range(count):
-                batch = pieces[6 * b + 3 * (i % 2) : 6 * b + 3 * (i % 2) + 3]
-                source = batch[0].at[:, pl.ds(side * width, width)] if i < 2 else batch[1 + side]
-                target = weights.at[side, i, pl.ds(at, source.shape[0])]
-                copies.append(pltpu.make_async_copy(source, target, sems.at[len(copies)]))
+                source = pieces[6 * b + 3 * core + kind]
+                target = beside.at[kind - 1, core] if kind else both.at[core]
+                copies.append(
+                    pltpu.make_async_copy(source, target.at[pl.ds(at, source.shape[0])], sems.at[len(copies)])
+                )
+                copies[-1].start()
                 at += source.shape[0]
-    for copy in copies:
-        copy.start()
     for side in range(2):
         for s in range(lines):
             for h in range(heads):
                 at = s * depth + h * HEAD_DIM
                 rows[side, :, at : at + HEAD_DIM] = landed[side][h * lines + order[s]]
-    for side in range(2):
-        for i in range(4):
-            for copy in copies[(side * 4 + i) * count : (side * 4 + i + 1) * count]:
+    for kind in range(3):
+        for core in range(2):
+            for copy in copies[(kind * 2 + core) * count : (kind * 2 + core + 1) * count]:
                 copy.wait()
-            outs[side][:, i * width : (i + 1) * width] = jnp.dot(
-                rows[side], weights[side, i], preferred_element_type=F32
-            ).astype(BF16)
+            for side in range(2) if kind == 0 else (kind - 1,):
+                weight = beside[kind - 1, core] if kind else both[core, :, side * width : (side + 1) * width]
+                at = (2 * (kind > 0) + core) * width
+                outs[side][:, at : at + width] = jnp.dot(
+                    rows[side], weight, preferred_element_type=F32
+                ).astype(BF16)
 
 
 def leave(order, landed_x, landed_y, shared, heads, lines):
@@ -412,9 +444,10 @@
         in_specs=[smem] + [vmem] * 2 + [hbm] * len(arrays),
         out_specs=(vmem, vmem),
         scratch_shapes=[
-            pltpu.VMEM((2, 4, depth, width), BF16),
+            pltpu.VMEM((2, depth, 2 * width), BF16),
+            pltpu.VMEM((2, 2, depth, width), BF16),
             pltpu.VMEM((2, BLK, depth), BF16),
-            pltpu.SemaphoreType.DMA((8 * len(shared),)),
+            pltpu.SemaphoreType.DMA((6 * len(shared),)),
         ],
         compiler_params=pltpu.CompilerParams(vmem_limit_bytes=58 << 20),
         cost_estimate=pl.CostEstimate(
@@ -502,7 +535,7 @@
     planes = jnp.stack(planes).astype(jnp.int32)
     if fast:
         w_one, w_two = hop(qkv_weight, 1), hop(qkv_weight, 2)
-    normed = normalize(tokens, norm_gain, feature_order)
+    gain = norm_gain.reshape(1, -1)
     inside = (line_at == 1) | (line_at == 2)
     flag = jnp.where(inside, 0, 1).astype(jnp.int32).reshape(1)
     slots = 2 + layout.shape[1]
@@ -511,9 +544,10 @@
 
     if not fast:
         weight = lax.all_gather(qkv_weight, ("head", "rep"), axis=1, tiled=True)
-        rows = gathered(normed, "line", lines)
-        whole = begin(flag, rows, [weight], [(0, weight.shape[1])]).astype(BF16)
-        projected = whole.reshape(3, lines, BLK, heads, HEAD_DIM).transpose(3, 0, 1, 2, 4)
+        rows = gathered(normalize(tokens, gain, feature_order), "line", lines)
+        runs = [(0, weight.shape[1])]
+        whole, _ = begin(flag, feature_order, gain, rows, [weight], runs, [], False)
+        projected = whole.astype(BF16).reshape(3, lines, BLK, heads, HEAD_DIM).transpose(3, 0, 1, 2, 4)
         attended = attention(pair_gather(by_head(projected), reps), *table, buckets)
         landed = lax.all_to_all(attended, ("head", "line"), 0, 0, tiled=True)
         out_pieces = [
@@ -538,7 +572,7 @@
         width = part.shape[1] // 2
         return hop(part[:, :width], 2), hop(part[:, width:], 1)
 
-    near, across = along(normed, xor_pairs(4, 1)), along(normed, middle)
+    near, across = along(tokens, xor_pairs(4, 1)), along(tokens, middle)
     w_others = [pair(qkv_weight)]
     near, across, w_others[0], *table = barrier((near, across, w_others[0], *table))
     second, crossed = along(across, outward), along(near, middle)
@@ -552,17 +586,18 @@
     w_others += [pair(w) for w in (w_one, w_two)]
     size = qkv_weight.shape[1]
     near_runs, far_runs = [(0, 3 * size), (4 * size, 3 * size)], [(3 * size, size), (7 * size, size)]
-    chunks = [normed, near, (across, second)]
+    chunks = [tokens, near, (across, second)]
     near_weights = [qkv_weight, w_one, w_two, *w_others]
-    begun = begin(flag, chunks, near_weights, near_runs)
-    w_first, w_other, begun = barrier((w_first, w_other, begun))
+    begun, left = begin(flag, feature_order, gain, chunks, near_weights, near_runs, far_runs, True)
+    w_first, w_other, begun, left = barrier((w_first, w_other, begun, left))
     w_others = [pair(w) for w in (w_first, w_other)]
     third, o_own, *w_others = barrier((third, out_weight, *w_others))
-    chunks.append((crossed, third))
     o_near, o_across = along(o_own, xor_pairs(4, 1)), along(o_own, middle)
     weights = [w_first, w_other, *w_others, *near_weights]
     places = [0, half, 2 * half, 3 * half] + [2 * size + i * size for i in range(6)]
-    projected = enter(flag, begun, chunks, weights, places, far_runs, near_runs, heads)
+    projected = enter(
+        flag, feature_order, gain, begun, left, (crossed, third), weights, places, far_runs, near_runs, heads
+    )
     projected, o_near, o_across = barrier((projected, o_near, o_across))
     mine = by_head(projected)
     o_crossed, o_second = along(o_near, middle), along(o_across, outward)

time: 198 us -> 198 us (level)
  local copies, waits for them, and re-layouts: 11 us -> 8.64 us
    unnamed x52 -> x46, local copies, waits for them, and re-layouts: 5.27 us -> 3.2 us
    pallas_call x3 -> x2, Pallas kernels: 22.1 us -> 24 us  [the longest x1 12.5 us: begin(): pl.pallas_call(functools.partial(begin_kernel, counts, runs, rest, places...]
  transfers between devices with their start and end apart: 41 -> 41, of which waited for: 22 -> 21; matrix products, arithmetic and copies ran while one was open for 7% -> 6% of each run, Pallas kernels for 18% -> 19%
where the time goes in v5:
time: 198 us; the launch traced here: 197 us
  waiting for transfers between devices  88.3 us (45%)
  starting transfers between devices  46.3 us (23%)
  Pallas kernels  46.2 us (23%)
  local copies, waits for them, and re-layouts  8.64 us (4%)
  other arithmetic  7.01 us (4%)
    ppermute x14, waiting for transfers between devices, hop(): return lax.ppermute(part, 'head', xor_pairs(4, bit))  43.6 us
    ppermute x10, waiting for transfers between devices, along(): return lax.ppermute(part, 'line', pairs)  43.5 us
    ppermute x14, starting transfers between devices, hop(): return lax.ppermute(part, 'head', xor_pairs(4, bit))  19.1 us
    ppermute x10, starting transfers between devices, along(): return lax.ppermute(part, 'line', pairs)  13.8 us
    pallas_call x2, Pallas kernels, leave(): pl.pallas_call(functools.partial(leave_kernel, heads, lines, len(shared))...  13 us
    pallas_call x1, Pallas kernels, begin(): pl.pallas_call(functools.partial(begin_kernel, counts, runs, rest, places...  12.5 us
    pallas_call x1, Pallas kernels, enter(): pl.pallas_call(functools.partial(enter_kernel, heads, runs, rest, places)...  11.5 us
    pallas_call x1, Pallas kernels, attention(): pl.pallas_call(functools.partial(attention_kernel, (total, reps, heads, b...  7.64 us
  transfers between devices with their start and end apart: 41, of which 21 were waited for; matrix products, arithmetic and copies ran while one was open for 6% of the time, Pallas kernels for 19%

profile of v5, /device:TPU:0, one launch (start us, length us, event | category | flops | bytes accessed | tf_op | source)
XLA Modules:
  0.0 196.8 jit_solution(11580905224556067081)
XLA Ops:
  0.0 3.0 %collective-permute-start = (bf16[128,4096]{1,0:T(8,128)(2,1)}, bf16[128,4096]{1,0:T(8,128)(2,1)}, u32[]{:S(2)}, u32[]{:S(2)}) collective-permute-start(bf16[128,4096]{1,0:T(8,128)(2,1)} %refs_0_.1), channel_id=1, source_target_pairs={{0,1},{1,0},{2,3},{3,2},{4,5},{5,4},{6,7},{7,6},{8,9},{9,8},{10,11... | collective-permute-start | bytes 3145736 | tf_op jit(solution)/shard_map/ppermute | solution.py:566
  3.0 1.7 collective-permute-start.1
  4.8 1.5 collective-permute-start.5
  6.2 1.5 collective-permute-start.6
  7.8 0.7 dynamic-slice_bitcast_fusion.order
  8.8 1.1 select_reduce_fusion.2
  11.9 0.7 select_reduce_fusion.1
  13.9 12.6 %collective-permute-done.refs_1_ = bf16[128,4096]{1,0:T(8,128)(2,1)} collective-permute-done((bf16[128,4096]{1,0:T(8,128)(2,1)}, bf16[128,4096]{1,0:T(8,128)(2,1)}, u32[]{:S(2)}, u32[]{:S(2)}) %collective-permute-start) | collective-permute-done | bytes 1048608 | tf_op jit(solution)/shard_map/ppermute | solution.py:566
  26.5 1.3 collective-permute-start.3
  27.8 1.7 collective-permute-start.4
  29.5 12.3 %collective-permute-done.5.refs_5_.refs_7_ = bf16[3,512,512]{2,1,0:T(8,128)(2,1)S(1)} collective-permute-done((bf16[3,512,512]{2,1,0:T(8,128)(2,1)}, bf16[3,512,512]{2,1,0:T(8,128)(2,1)S(1)}, u32[]{:S(2)}, u32[]{:S(2)}) %collective-permute-start.5) | collective-permute-done | bytes 1572896 | tf_op jit(solution)/shard_map/ppermute | solution.py:51
  41.8 1.2 collective-permute-done.6.refs_6_.refs_8_
  43.0 1.4 fusion.18
  44.4 1.6 collective-permute-start.7
  46.0 0.6 collective-permute-start.8
  46.6 0.9 slice.32
  47.5 1.0 slice.33
  48.5 3.6 %collective-permute-done.7.refs_3_ = bf16[512,256]{1,0:T(8,128)(2,1)S(1)} collective-permute-done((bf16[512,256]{1,0:T(8,128)(2,1)S(1)}, bf16[512,256]{1,0:T(8,128)(2,1)S(1)}, u32[]{:S(2)}, u32[]{:S(2)}) %collective-permute-start.7) | collective-permute-done | bytes 262176 | tf_op jit(solution)/shard_map/ppermute | solution.py:51
  52.1 1.3 collective-permute-done.8.refs_4_
  53.4 1.6 collective-permute-done.3.refs_3_
  56.0 1.5 collective-permute-start.9
  57.5 1.5 collective-permute-start.10
  59.0 1.3 collective-permute-start.13
  60.3 0.6 stack.47.order
  60.9 12.5 %begin.1 = (f32[3,384,512]{2,1,0:T(8,128)}, bf16[384,1024]{1,0:T(8,128)(2,1)}) custom-call(s32[1]{0:T(128)} %bitcast.4.flag, s32[8]{0:T(128)} %stack.47.order, f32[1,4096]{1,0:T(1,128)} %bitcast.16, bf16[128,4096]{1,0:T(8,128)(2,1)} %refs_0_.1, bf16[128,4096]{1,0:T(8,128)(2,1)} %collective-permute-done.refs_1_, ...), custom_call_target="tpu_custom_call" | custom-call | flops 1 | bytes 1 | tf_op jit(solution)/shard_map/begin/pallas_call | solution.py:315
  73.4 2.1 %collective-permute-done.9.refs_2_ = bf16[3,256,512]{2,1,0:T(8,128)(2,1)} collective-permute-done((bf16[3,256,512]{2,1,0:T(8,128)(2,1)}, bf16[3,256,512]{2,1,0:T(8,128)(2,1)}, u32[]{:S(2)}, u32[]{:S(2)}) %collective-permute-start.9) | collective-permute-done | bytes 786464 | tf_op jit(solution)/shard_map/ppermute | solution.py:51
  75.5 1.2 collective-permute-done.10.refs_3_
  76.7 0.5 collective-permute-start.15
  77.2 9.6 %collective-permute-done.13.refs_1_ = bf16[128,4096]{1,0:T(8,128)(2,1)} collective-permute-done((bf16[128,4096]{1,0:T(8,128)(2,1)}, bf16[128,4096]{1,0:T(8,128)(2,1)}, u32[]{:S(2)}, u32[]{:S(2)}) %collective-permute-start.13) | collective-permute-done | bytes 1048608 | tf_op jit(solution)/shard_map/ppermute | solution.py:566
  86.9 0.7 collective-permute-start.17
  88.0 11.5 %enter.1 = bf16[4,3,4,128,128]{4,3,2,1,0:T(8,128)(2,1)} custom-call(s32[1]{0:T(128)} %bitcast.4.flag, s32[8]{0:T(128)} %stack.47.order, f32[1,4096]{1,0:T(1,128)} %bitcast.17, f32[3,384,512]{2,1,0:T(8,128)} %get-tuple-element.77.begun, bf16[384,1024]{1,0:T(8,128)(2,1)} %get-tuple-element.78.left, bf16[128,4096]{1,0:T(8,128)(2,1)} %collective-permute-done.4.refs_0_, ...), custom_call_target="tpu_custom_call" | custom-call | flops 1 | bytes 1 | tf_op jit(solution)/shard_map/enter/pallas_call | solution.py:379
  99.9 0.8 copy-done.21
  100.7 3.6 %all-to-all-start = ((bf16[4,3,4,128,128]{4,3,2,1,0:T(8,128)(2,1)}), bf16[4,3,4,128,128]{4,3,2,1,0:T(8,128)(2,1)S(1)}, u32[]{:S(2)}, u32[]{:S(2)}) async-start(bf16[4,3,4,128,128]{4,3,2,1,0:T(8,128)(2,1)} %enter.1), calls=%async_computation | async-start | bytes 3145728 | tf_op jit(solution)/shard_map/all_to_all | solution.py:484
  104.2 1.5 collective-permute-start.18
  105.7 1.3 collective-permute-start.19
  107.0 15.4 %collective-permute-done.19 = bf16[512,512]{1,0:T(8,128)(2,1)S(1)} collective-permute-done((bf16[512,512]{1,0:T(8,128)(2,1)}, bf16[512,512]{1,0:T(8,128)(2,1)S(1)}, u32[]{:S(2)}, u32[]{:S(2)}) %collective-permute-start.19) | collective-permute-done | bytes 524320 | tf_op jit(solution)/shard_map/ppermute | solution.py:566
  122.5 1.3 collective-permute-start.21
  124.0 1.7 collective-permute-start.22
  125.7 1.5 collective-permute-start.23
  127.1 1.1 pad_maximum_fusion.refs_8_
  128.3 0.6 collective-permute-start.25
  128.9 7.6 %attention.1 = bf16[16,128,128]{2,1,0:T(8,128)(2,1)} custom-call(s32[16,18]{1,0:T(8,128)S(1)} %fusion.7.places, f32[16,18]{1,0:T(8,128)S(1)} %multiply_select_fusion.biases, s32[16]{0:T(128)S(1)} %select_reduce_fusion.4.turns, s32[3]{0:T(128)S(1)} %convert_reduce_fusion.5.ends, s32[16]{0:T(128)S(1)} %add.174.targets, ...), custom_call_target="tpu_custom_call" | custom-call | flops 2415919104 | bytes 4194304 | tf_op jit(solution)/shard_map/attention/pallas_call | solution.py:158
  136.5 4.0 %collective-permute-done.21 = bf16[512,512]{1,0:T(8,128)(2,1)} collective-permute-done((bf16[512,512]{1,0:T(8,128)(2,1)}, bf16[512,512]{1,0:T(8,128)(2,1)}, u32[]{:S(2)}, u32[]{:S(2)}) %collective-permute-start.21) | collective-permute-done | bytes 524320 | tf_op jit(solution)/shard_map/ppermute | solution.py:566
  140.5 7.1 %all-to-all-start.1 = ((bf16[16,128,128]{2,1,0:T(8,128)(2,1)}), bf16[16,128,128]{2,1,0:T(8,128)(2,1)S(1)}, u32[]{:S(2)}, u32[]{:S(2)}) async-start(bf16[16,128,128]{2,1,0:T(8,128)(2,1)} %attention.1), calls=%async_computation.1 | async-start | bytes 1048576 | tf_op jit(solution)/shard_map/all_to_all | solution.py:611
  147.6 1.1 broadcast_select_fusion.refs_14_
  148.8 2.0 %collective-permute-start.31 = (bf16[512,256]{1,0:T(8,128)(2,1)S(1)}, bf16[512,256]{1,0:T(8,128)(2,1)S(1)}, u32[]{:S(2)}, u32[]{:S(2)}) collective-permute-start(bf16[512,256]{1,0:T(8,128)(2,1)S(1)} %get-tuple-element.124), channel_id=1, source_target_pairs={{0,16},{8,24},{16,0},{24,8},{1,17},{9,25},{17,1},{25,9},{2,18},{10... | collective-permute-start | bytes 786440 | tf_op jit(solution)/shard_map/ppermute | solution.py:51
  151.3 1.5 collective-permute-start.33
  152.8 7.9 %collective-permute-done.31.refs_15_ = bf16[512,256]{1,0:T(8,128)(2,1)S(1)} collective-permute-done((bf16[512,256]{1,0:T(8,128)(2,1)S(1)}, bf16[512,256]{1,0:T(8,128)(2,1)S(1)}, u32[]{:S(2)}, u32[]{:S(2)}) %collective-permute-start.31) | collective-permute-done | bytes 262176 | tf_op jit(solution)/shard_map/ppermute | solution.py:51
  160.7 1.1 collective-permute-done.33.refs_16_
  161.8 0.5 collective-permute-start.34
  162.6 0.8 collective-permute-done.32.refs_18_
  163.4 0.7 copy-done.15
  164.1 2.0 %collective-permute-start.35 = (bf16[16,128,128]{2,1,0:T(8,128)(2,1)S(1)}, bf16[16,128,128]{2,1,0:T(8,128)(2,1)S(1)}, u32[]{:S(2)}, u32[]{:S(2)}) collective-permute-start(bf16[16,128,128]{2,1,0:T(8,128)(2,1)S(1)} %all-to-all-done.1.refs_0_.refs_1_), channel_id=1, source_target_pairs={{0,8},{8,0},{16,24},{24,16},{1,9},{9,1},{17,25},{25,17},{2,10},{10... | collective-permute-start | bytes 1572872 | tf_op jit(solution)/shard_map/ppermute | solution.py:51
  166.2 0.9 collective-permute-start.36
  167.0 6.5 %leave.2 = (bf16[128,1024]{1,0:T(8,128)(2,1)}, bf16[128,1024]{1,0:T(8,128)(2,1)}) custom-call(s32[4]{0:T(128)} %copy-done.22, bf16[16,128,128]{2,1,0:T(8,128)(2,1)} %copy-done.6, bf16[16,128,128]{2,1,0:T(8,128)(2,1)} %copy-done.6, bf16[512,512]{1,0:T(8,128)(2,1)} %refs_2_.3, bf16[512,256]{1,0:T(8,128)(2,1)} %copy-done.12, ...), custom_call_target="tpu_custom_call" | custom-call | flops 1073741824 | bytes 8388608 | tf_op jit(solution)/shard_map/leave/pallas_call | solution.py:441
  173.6 4.8 %collective-permute-done.35.refs_0_ = bf16[16,128,128]{2,1,0:T(8,128)(2,1)S(1)} collective-permute-done((bf16[16,128,128]{2,1,0:T(8,128)(2,1)S(1)}, bf16[16,128,128]{2,1,0:T(8,128)(2,1)S(1)}, u32[]{:S(2)}, u32[]{:S(2)}) %collective-permute-start.35) | collective-permute-done | bytes 524320 | tf_op jit(solution)/shard_map/ppermute | solution.py:51
  178.4 1.5 collective-permute-done.36.refs_1_
  179.9 0.8 copy-done.20
  180.7 6.5 %leave.3 = (bf16[128,1024]{1,0:T(8,128)(2,1)}, bf16[128,1024]{1,0:T(8,128)(2,1)}) custom-call(s32[4]{0:T(128)} %copy-done.22, bf16[16,128,128]{2,1,0:T(8,128)(2,1)} %copy-done.19, bf16[16,128,128]{2,1,0:T(8,128)(2,1)} %copy-done.20, bf16[512,512]{1,0:T(8,128)(2,1)} %refs_2_.3, bf16[512,256]{1,0:T(8,128)(2,1)} %copy-done.12, ...), custom_call_target="tpu_custom_call" | custom-call | flops 1073741824 | bytes 8388608 | tf_op jit(solution)/shard_map/leave/pallas_call | solution.py:441
  187.2 0.6 collective-permute-start.37
  187.7 0.9 collective-permute-start.38
  188.7 6.0 %collective-permute-done.37.from_x = bf16[128,1024]{1,0:T(8,128)(2,1)S(1)} collective-permute-done((bf16[128,1024]{1,0:T(8,128)(2,1)}, bf16[128,1024]{1,0:T(8,128)(2,1)S(1)}, u32[]{:S(2)}, u32[]{:S(2)}) %collective-permute-start.37) | collective-permute-done | bytes 262176 | tf_op jit(solution)/shard_map/ppermute | solution.py:51
  194.6 0.6 collective-permute-done.38.from_y
  195.2 1.6 place.1
  (115 shorter events, 6.8 us)
Async XLA Ops:
  0.0 26.5 %collective-permute-start = (bf16[128,4096]{1,0:T(8,128)(2,1)}, bf16[128,4096]{1,0:T(8,128)(2,1)}, u32[]{:S(2)}, u32[]{:S(2)}) collective-permute-start(bf16[128,4096]{1,0:T(8,128)(2,1)} %refs_0_.1), channel_id=1, source_target_pairs={{0,1},{1,0},{2,3},{3,2},{4,5},{5,4},{6,7},{7,6},{8,9},{9,8},{10,11... | collective-permute-start | bytes 3145736 | tf_op jit(solution)/shard_map/ppermute | solution.py:566
  3.0 23.5 %collective-permute-start.1 = (bf16[128,4096]{1,0:T(8,128)(2,1)}, bf16[128,4096]{1,0:T(8,128)(2,1)}, u32[]{:S(2)}, u32[]{:S(2)}) collective-permute-start(bf16[128,4096]{1,0:T(8,128)(2,1)} %refs_0_.1), channel_id=1, source_target_pairs={{1,2},{2,1},{5,6},{6,5},{9,10},{10,9},{13,14},{14,13},{17,18},{18,... | collective-permute-start | bytes 3145736 | tf_op jit(solution)/shard_map/ppermute | solution.py:566
  4.8 21.8 %collective-permute-start.2 = (bf16[3,512,512]{2,1,0:T(8,128)(2,1)}, bf16[3,512,512]{2,1,0:T(8,128)(2,1)}, u32[]{:S(2)}, u32[]{:S(2)}) collective-permute-start(bf16[3,512,512]{2,1,0:T(8,128)(2,1)} %refs_6_.1), channel_id=1, source_target_pairs={{0,4},{4,0},{1,5},{5,1},{2,6},{6,2},{3,7},{7,3},{8,12},{12,8},{9,1... | collective-permute-start | bytes 4718600 | tf_op jit(solution)/shard_map/ppermute | solution.py:569
  4.8 37.0 %collective-permute-start.5 = (bf16[3,512,512]{2,1,0:T(8,128)(2,1)}, bf16[3,512,512]{2,1,0:T(8,128)(2,1)S(1)}, u32[]{:S(2)}, u32[]{:S(2)}) collective-permute-start(bf16[3,512,512]{2,1,0:T(8,128)(2,1)} %refs_6_.1), channel_id=1, source_target_pairs={{0,8},{8,0},{16,24},{24,16},{1,9},{9,1},{17,25},{25,17},{2,10},{10... | collective-permute-start | bytes 4718600 | tf_op jit(solution)/shard_map/ppermute | solution.py:51
  6.2 36.7 %collective-permute-start.6 = (bf16[3,512,512]{2,1,0:T(8,128)(2,1)}, bf16[3,512,512]{2,1,0:T(8,128)(2,1)S(1)}, u32[]{:S(2)}, u32[]{:S(2)}) collective-permute-start(bf16[3,512,512]{2,1,0:T(8,128)(2,1)} %refs_6_.1), channel_id=1, source_target_pairs={{0,16},{8,24},{16,0},{24,8},{1,17},{9,25},{17,1},{25,9},{2,18},{10... | collective-permute-start | bytes 4718600 | tf_op jit(solution)/shard_map/ppermute | solution.py:51
  8.5 39.0 %copy-start.22 = (s32[4]{0:T(128)}, s32[4]{0:T(128)S(1)}, u32[]{:S(2)}) copy-start(s32[4]{0:T(128)S(1)} %dynamic-slice_bitcast_fusion.order) | copy-start | bytes 52
  26.5 28.5 %collective-permute-start.3 = (bf16[128,4096]{1,0:T(8,128)(2,1)}, bf16[128,4096]{1,0:T(8,128)(2,1)S(1)}, u32[]{:S(2)}, u32[]{:S(2)}) collective-permute-start(bf16[128,4096]{1,0:T(8,128)(2,1)} %collective-permute-done.1.refs_2_), channel_id=1, source_target_pairs={{1,0},{2,3},{5,4},{6,7},{9,8},{10,11},{13,12},{14,15},{17,16},{18,... | collective-permute-start | bytes 3145736 | tf_op jit(solution)/shard_map/ppermute | solution.py:566
  27.8 27.2 %collective-permute-start.4 = (bf16[128,4096]{1,0:T(8,128)(2,1)}, bf16[128,4096]{1,0:T(8,128)(2,1)}, u32[]{:S(2)}, u32[]{:S(2)}) collective-permute-start(bf16[128,4096]{1,0:T(8,128)(2,1)} %collective-permute-done.refs_1_), channel_id=1, source_target_pairs={{1,2},{2,1},{5,6},{6,5},{9,10},{10,9},{13,14},{14,13},{17,18},{18,... | collective-permute-start | bytes 3145736 | tf_op jit(solution)/shard_map/ppermute | solution.py:566
  41.8 13.3 %copy-start.2 = (bf16[3,512,512]{2,1,0:T(8,128)(2,1)}, bf16[3,512,512]{2,1,0:T(8,128)(2,1)S(1)}, u32[]{:S(2)}) copy-start(bf16[3,512,512]{2,1,0:T(8,128)(2,1)S(1)} %collective-permute-done.5.refs_5_.refs_7_) | copy-start | bytes 4718596
  43.0 12.1 %copy-start.3 = (bf16[3,512,512]{2,1,0:T(8,128)(2,1)}, bf16[3,512,512]{2,1,0:T(8,128)(2,1)S(1)}, u32[]{:S(2)}) copy-start(bf16[3,512,512]{2,1,0:T(8,128)(2,1)S(1)} %collective-permute-done.6.refs_6_.refs_8_) | copy-start | bytes 4718596
  44.4 7.7 %collective-permute-start.7 = (bf16[512,256]{1,0:T(8,128)(2,1)S(1)}, bf16[512,256]{1,0:T(8,128)(2,1)S(1)}, u32[]{:S(2)}, u32[]{:S(2)}) collective-permute-start(bf16[512,256]{1,0:T(8,128)(2,1)S(1)} %get-tuple-element.126), channel_id=1, source_target_pairs={{0,16},{8,24},{16,0},{24,8},{1,17},{9,25},{17,1},{25,9},{2,18},{10... | collective-permute-start | bytes 786440 | tf_op jit(solution)/shard_map/ppermute | solution.py:51
  46.0 7.4 %collective-permute-start.8 = (bf16[512,256]{1,0:T(8,128)(2,1)S(1)}, bf16[512,256]{1,0:T(8,128)(2,1)}, u32[]{:S(2)}, u32[]{:S(2)}) collective-permute-start(bf16[512,256]{1,0:T(8,128)(2,1)S(1)} %get-tuple-element.125), channel_id=1, source_target_pairs={{0,8},{8,0},{16,24},{24,16},{1,9},{9,1},{17,25},{25,17},{2,10},{10... | collective-permute-start | bytes 786440 | tf_op jit(solution)/shard_map/ppermute | solution.py:51
  52.1 76.2 %copy-start.12 = (bf16[512,256]{1,0:T(8,128)(2,1)}, bf16[512,256]{1,0:T(8,128)(2,1)S(1)}, u32[]{:S(2)}) copy-start(bf16[512,256]{1,0:T(8,128)(2,1)S(1)} %collective-permute-done.7.refs_3_) | copy-start | bytes 786436
  55.0 1.0 copy-start.16
  55.0 5.9 %collective-permute-start.11 = (bf16[3,512,512]{2,1,0:T(8,128)(2,1)S(1)}, bf16[3,512,512]{2,1,0:T(8,128)(2,1)}, u32[]{:S(2)}, u32[]{:S(2)}) collective-permute-start(bf16[3,512,512]{2,1,0:T(8,128)(2,1)S(1)} %collective-permute-done.5.refs_5_.refs_7_), channel_id=1, source_target_pairs={{0,4},{4,0},{1,5},{5,1},{2,6},{6,2},{3,7},{7,3},{8,12},{12,8},{9,1... | collective-permute-start | bytes 4718600 | tf_op jit(solution)/shard_map/ppermute | solution.py:569
  55.1 5.8 %collective-permute-start.12 = (bf16[3,512,512]{2,1,0:T(8,128)(2,1)S(1)}, bf16[3,512,512]{2,1,0:T(8,128)(2,1)}, u32[]{:S(2)}, u32[]{:S(2)}) collective-permute-start(bf16[3,512,512]{2,1,0:T(8,128)(2,1)S(1)} %collective-permute-done.6.refs_6_.refs_8_), channel_id=1, source_target_pairs={{0,4},{4,0},{1,5},{5,1},{2,6},{6,2},{3,7},{7,3},{8,12},{12,8},{9,1... | collective-permute-start | bytes 4718600 | tf_op jit(solution)/shard_map/ppermute | solution.py:569
  56.0 19.5 %collective-permute-start.9 = (bf16[3,256,512]{2,1,0:T(8,128)(2,1)}, bf16[3,256,512]{2,1,0:T(8,128)(2,1)}, u32[]{:S(2)}, u32[]{:S(2)}) collective-permute-start(bf16[3,256,512]{2,1,0:T(8,128)(2,1)} %slice.32), channel_id=1, source_target_pairs={{0,8},{8,0},{16,24},{24,16},{1,9},{9,1},{17,25},{25,17},{2,10},{10... | collective-permute-start | bytes 2359304 | tf_op jit(solution)/shard_map/ppermute | solution.py:51
  57.5 19.2 %collective-permute-start.10 = (bf16[3,256,512]{2,1,0:T(8,128)(2,1)}, bf16[3,256,512]{2,1,0:T(8,128)(2,1)}, u32[]{:S(2)}, u32[]{:S(2)}) collective-permute-start(bf16[3,256,512]{2,1,0:T(8,128)(2,1)} %slice.33), channel_id=1, source_target_pairs={{0,16},{8,24},{16,0},{24,8},{1,17},{9,25},{17,1},{25,9},{2,18},{10... | collective-permute-start | bytes 2359304 | tf_op jit(solution)/shard_map/ppermute | solution.py:51
  59.0 27.8 %collective-permute-start.13 = (bf16[128,4096]{1,0:T(8,128)(2,1)}, bf16[128,4096]{1,0:T(8,128)(2,1)}, u32[]{:S(2)}, u32[]{:S(2)}) collective-permute-start(bf16[128,4096]{1,0:T(8,128)(2,1)} %collective-permute-done.4.refs_0_), channel_id=1, source_target_pairs={{1,0},{2,3},{5,4},{6,7},{9,8},{10,11},{13,12},{14,15},{17,16},{18,... | collective-permute-start | bytes 3145736 | tf_op jit(solution)/shard_map/ppermute | solution.py:566
  76.7 10.1 %collective-permute-start.14 = (bf16[3,256,512]{2,1,0:T(8,128)(2,1)}, bf16[3,256,512]{2,1,0:T(8,128)(2,1)S(1)}, u32[]{:S(2)}, u32[]{:S(2)}) collective-permute-start(bf16[3,256,512]{2,1,0:T(8,128)(2,1)} %collective-permute-done.9.refs_2_), channel_id=1, source_target_pairs={{0,4},{4,0},{1,5},{5,1},{2,6},{6,2},{3,7},{7,3},{8,12},{12,8},{9,1... | collective-permute-start | bytes 2359304 | tf_op jit(solution)/shard_map/ppermute | solution.py:569
  76.7 10.1 %collective-permute-start.15 = (bf16[3,256,512]{2,1,0:T(8,128)(2,1)}, bf16[3,256,512]{2,1,0:T(8,128)(2,1)S(1)}, u32[]{:S(2)}, u32[]{:S(2)}) collective-permute-start(bf16[3,256,512]{2,1,0:T(8,128)(2,1)} %collective-permute-done.10.refs_3_), channel_id=1, source_target_pairs={{0,4},{4,0},{1,5},{5,1},{2,6},{6,2},{3,7},{7,3},{8,12},{12,8},{9,1... | collective-permute-start | bytes 2359304 | tf_op jit(solution)/shard_map/ppermute | solution.py:569
  86.8 0.9 copy-start.17
  86.8 1.1 copy-start.18
  86.8 13.0 %collective-permute-start.16 = (bf16[512,512]{1,0:T(8,128)(2,1)}, bf16[512,512]{1,0:T(8,128)(2,1)S(1)}, u32[]{:S(2)}, u32[]{:S(2)}) collective-permute-start(bf16[512,512]{1,0:T(8,128)(2,1)} %refs_2_.3), channel_id=1, source_target_pairs={{0,1},{1,0},{2,3},{3,2},{4,5},{5,4},{6,7},{7,6},{8,9},{9,8},{10,11... | collective-permute-start | bytes 1572872 | tf_op jit(solution)/shard_map/ppermute | solution.py:566
  86.9 12.9 %collective-permute-start.17 = (bf16[512,512]{1,0:T(8,128)(2,1)}, bf16[512,512]{1,0:T(8,128)(2,1)S(1)}, u32[]{:S(2)}, u32[]{:S(2)}) collective-permute-start(bf16[512,512]{1,0:T(8,128)(2,1)} %refs_2_.3), channel_id=1, source_target_pairs={{1,2},{2,1},{5,6},{6,5},{9,10},{10,9},{13,14},{14,13},{17,18},{18,... | collective-permute-start | bytes 1572872 | tf_op jit(solution)/shard_map/ppermute | solution.py:566
  99.8 24.1 %copy-start.11 = (bf16[512,512]{1,0:T(8,128)(2,1)}, bf16[512,512]{1,0:T(8,128)(2,1)S(1)}, u32[]{:S(2)}) copy-start(bf16[512,512]{1,0:T(8,128)(2,1)S(1)} %collective-permute-done.16) | copy-start | bytes 1572868
  99.8 0.8 copy-start.21
  100.7 21.8 %all-to-all-start = ((bf16[4,3,4,128,128]{4,3,2,1,0:T(8,128)(2,1)}), bf16[4,3,4,128,128]{4,3,2,1,0:T(8,128)(2,1)S(1)}, u32[]{:S(2)}, u32[]{:S(2)}) async-start(bf16[4,3,4,128,128]{4,3,2,1,0:T(8,128)(2,1)} %enter.1), calls=%async_computation | async-start | bytes 3145728 | tf_op jit(solution)/shard_map/all_to_all | solution.py:484
  104.2 2.8 %collective-permute-start.18 = (bf16[512,512]{1,0:T(8,128)(2,1)S(1)}, bf16[512,512]{1,0:T(8,128)(2,1)}, u32[]{:S(2)}, u32[]{:S(2)}) collective-permute-start(bf16[512,512]{1,0:T(8,128)(2,1)S(1)} %collective-permute-done.16), channel_id=1, source_target_pairs={{1,2},{2,1},{5,6},{6,5},{9,10},{10,9},{13,14},{14,13},{17,18},{18,... | collective-permute-start | bytes 1572872 | tf_op jit(solution)/shard_map/ppermute | solution.py:566
  105.7 16.7 %collective-permute-start.19 = (bf16[512,512]{1,0:T(8,128)(2,1)}, bf16[512,512]{1,0:T(8,128)(2,1)S(1)}, u32[]{:S(2)}, u32[]{:S(2)}) collective-permute-start(bf16[512,512]{1,0:T(8,128)(2,1)} %copy-done.21), channel_id=1, source_target_pairs={{1,0},{2,3},{5,4},{6,7},{9,8},{10,11},{13,12},{14,15},{17,16},{18,... | collective-permute-start | bytes 1572872 | tf_op jit(solution)/shard_map/ppermute | solution.py:566
  122.5 5.7 %collective-permute-start.20 = (bf16[4,3,4,128,128]{4,3,2,1,0:T(8,128)(2,1)S(1)}, bf16[4,3,4,128,128]{4,3,2,1,0:T(8,128)(2,1)S(1)}, u32[]{:S(2)}, u32[]{:S(2)}) collective-permute-start(bf16[4,3,4,128,128]{4,3,2,1,0:T(8,128)(2,1)S(1)} %all-to-all-done.refs_0_), channel_id=1, source_target_pairs={{0,4},{4,0},{1,5},{5,1},{2,6},{6,2},{3,7},{7,3},{8,12},{12,8},{9,1... | collective-permute-start | bytes 4718600 | tf_op jit(solution)/shard_map/ppermute | solution.py:47
  122.5 17.9 %collective-permute-start.21 = (bf16[512,512]{1,0:T(8,128)(2,1)}, bf16[512,512]{1,0:T(8,128)(2,1)}, u32[]{:S(2)}, u32[]{:S(2)}) collective-permute-start(bf16[512,512]{1,0:T(8,128)(2,1)} %collective-permute-done.18), channel_id=1, source_target_pairs={{1,0},{2,3},{5,4},{6,7},{9,8},{10,11},{13,12},{14,15},{17,16},{18,... | collective-permute-start | bytes 1572872 | tf_op jit(solution)/shard_map/ppermute | solution.py:566
  124.0 16.5 %collective-permute-start.22 = (bf16[1024,256]{1,0:T(8,128)(2,1)S(1)}, bf16[1024,256]{1,0:T(8,128)(2,1)}, u32[]{:S(2)}, u32[]{:S(2)}) collective-permute-start(bf16[1024,256]{1,0:T(8,128)(2,1)S(1)} %get-tuple-element.122), channel_id=1, source_target_pairs={{0,16},{8,24},{16,0},{24,8},{1,17},{9,25},{17,1},{25,9},{2,18},{10... | collective-permute-start | bytes 1572872 | tf_op jit(solution)/shard_map/ppermute | solution.py:51
  125.7 14.8 %collective-permute-start.23 = (bf16[1024,256]{1,0:T(8,128)(2,1)S(1)}, bf16[1024,256]{1,0:T(8,128)(2,1)}, u32[]{:S(2)}, u32[]{:S(2)}) collective-permute-start(bf16[1024,256]{1,0:T(8,128)(2,1)S(1)} %get-tuple-element.121), channel_id=1, source_target_pairs={{0,8},{8,0},{16,24},{24,16},{1,9},{9,1},{17,25},{25,17},{2,10},{10... | collective-permute-start | bytes 1572872 | tf_op jit(solution)/shard_map/ppermute | solution.py:51
  127.1 23.7 %collective-permute-start.24 = (bf16[512,512]{1,0:T(8,128)(2,1)}, bf16[512,512]{1,0:T(8,128)(2,1)}, u32[]{:S(2)}, u32[]{:S(2)}) collective-permute-start(bf16[512,512]{1,0:T(8,128)(2,1)} %refs_2_.3), channel_id=1, source_target_pairs={{0,4},{4,0},{1,5},{5,1},{2,6},{6,2},{3,7},{7,3},{8,12},{12,8},{9,1... | collective-permute-start | bytes 1572872 | tf_op jit(solution)/shard_map/ppermute | solution.py:569
  128.2 19.3 %copy-start.4 = (bf16[1024,512]{1,0:T(8,128)(2,1)}, bf16[1024,512]{1,0:T(8,128)(2,1)S(1)}, u32[]{:S(2)}) copy-start(bf16[1024,512]{1,0:T(8,128)(2,1)S(1)} %pad_maximum_fusion.refs_8_) | copy-start | bytes 3145732
  128.3 22.7 %collective-permute-start.25 = (bf16[512,256]{1,0:T(8,128)(2,1)S(1)}, bf16[512,256]{1,0:T(8,128)(2,1)}, u32[]{:S(2)}, u32[]{:S(2)}) collective-permute-start(bf16[512,256]{1,0:T(8,128)(2,1)S(1)} %collective-permute-done.7.refs_3_), channel_id=1, source_target_pairs={{0,4},{4,0},{1,5},{5,1},{2,6},{6,2},{3,7},{7,3},{8,12},{12,8},{9,1... | collective-permute-start | bytes 786440 | tf_op jit(solution)/shard_map/ppermute | solution.py:569
  140.5 10.9 %collective-permute-start.26 = (bf16[512,256]{1,0:T(8,128)(2,1)}, bf16[512,256]{1,0:T(8,128)(2,1)}, u32[]{:S(2)}, u32[]{:S(2)}) collective-permute-start(bf16[512,256]{1,0:T(8,128)(2,1)} %collective-permute-done.8.refs_4_), channel_id=1, source_target_pairs={{0,4},{4,0},{1,5},{5,1},{2,6},{6,2},{3,7},{7,3},{8,12},{12,8},{9,1... | collective-permute-start | bytes 786440 | tf_op jit(solution)/shard_map/ppermute | solution.py:569
  140.5 23.6 %all-to-all-start.1 = ((bf16[16,128,128]{2,1,0:T(8,128)(2,1)}), bf16[16,128,128]{2,1,0:T(8,128)(2,1)S(1)}, u32[]{:S(2)}, u32[]{:S(2)}) async-start(bf16[16,128,128]{2,1,0:T(8,128)(2,1)} %attention.1), calls=%async_computation.1 | async-start | bytes 1048576 | tf_op jit(solution)/shard_map/all_to_all | solution.py:611
  147.6 16.6 %collective-permute-start.27 = (bf16[1024,512]{1,0:T(8,128)(2,1)S(1)}, bf16[1024,512]{1,0:T(8,128)(2,1)S(1)}, u32[]{:S(2)}, u32[]{:S(2)}) collective-permute-start(bf16[1024,512]{1,0:T(8,128)(2,1)S(1)} %pad_maximum_fusion.refs_8_), channel_id=1, source_target_pairs={{0,4},{4,0},{1,5},{5,1},{2,6},{6,2},{3,7},{7,3},{8,12},{12,8},{9,1... | collective-permute-start | bytes 3145736 | tf_op jit(solution)/shard_map/ppermute | solution.py:569
  148.8 18.3 %copy-start.5 = (bf16[512,512]{1,0:T(8,128)(2,1)}, bf16[512,512]{1,0:T(8,128)(2,1)S(1)}, u32[]{:S(2)}) copy-start(bf16[512,512]{1,0:T(8,128)(2,1)S(1)} %broadcast_select_fusion.refs_14_) | copy-start | bytes 1572868
  148.8 11.9 %collective-permute-start.31 = (bf16[512,256]{1,0:T(8,128)(2,1)S(1)}, bf16[512,256]{1,0:T(8,128)(2,1)S(1)}, u32[]{:S(2)}, u32[]{:S(2)}) collective-permute-start(bf16[512,256]{1,0:T(8,128)(2,1)S(1)} %get-tuple-element.124), channel_id=1, source_target_pairs={{0,16},{8,24},{16,0},{24,8},{1,17},{9,25},{17,1},{25,9},{2,18},{10... | collective-permute-start | bytes 786440 | tf_op jit(solution)/shard_map/ppermute | solution.py:51
  150.8 11.0 %collective-permute-start.28 = (bf16[1024,256]{1,0:T(8,128)(2,1)}, bf16[1024,256]{1,0:T(8,128)(2,1)S(1)}, u32[]{:S(2)}, u32[]{:S(2)}) collective-permute-start(bf16[1024,256]{1,0:T(8,128)(2,1)} %collective-permute-done.22.refs_9_), channel_id=1, source_target_pairs={{0,4},{4,0},{1,5},{5,1},{2,6},{6,2},{3,7},{7,3},{8,12},{12,8},{9,1... | collective-permute-start | bytes 1572872 | tf_op jit(solution)/shard_map/ppermute | solution.py:569
  151.0 11.3 %collective-permute-start.29 = (bf16[1024,256]{1,0:T(8,128)(2,1)}, bf16[1024,256]{1,0:T(8,128)(2,1)S(1)}, u32[]{:S(2)}, u32[]{:S(2)}) collective-permute-start(bf16[1024,256]{1,0:T(8,128)(2,1)} %collective-permute-done.23.refs_10_), channel_id=1, source_target_pairs={{0,4},{4,0},{1,5},{5,1},{2,6},{6,2},{3,7},{7,3},{8,12},{12,8},{9,1... | collective-permute-start | bytes 1572872 | tf_op jit(solution)/shard_map/ppermute | solution.py:569
  151.3 10.5 %collective-permute-start.33 = (bf16[512,256]{1,0:T(8,128)(2,1)S(1)}, bf16[512,256]{1,0:T(8,128)(2,1)S(1)}, u32[]{:S(2)}, u32[]{:S(2)}) collective-permute-start(bf16[512,256]{1,0:T(8,128)(2,1)S(1)} %get-tuple-element.123), channel_id=1, source_target_pairs={{0,8},{8,0},{16,24},{24,16},{1,9},{9,1},{17,25},{25,17},{2,10},{10... | collective-permute-start | bytes 786440 | tf_op jit(solution)/shard_map/ppermute | solution.py:51
  160.7 2.7 %copy-start.13 = (bf16[512,256]{1,0:T(8,128)(2,1)}, bf16[512,256]{1,0:T(8,128)(2,1)S(1)}, u32[]{:S(2)}) copy-start(bf16[512,256]{1,0:T(8,128)(2,1)S(1)} %collective-permute-done.31.refs_15_) | copy-start | bytes 786436
  160.7 1.9 collective-permute-start.30
  161.8 5.2 %copy-start.14 = (bf16[512,256]{1,0:T(8,128)(2,1)}, bf16[512,256]{1,0:T(8,128)(2,1)S(1)}, u32[]{:S(2)}) copy-start(bf16[512,256]{1,0:T(8,128)(2,1)S(1)} %collective-permute-done.33.refs_16_) | copy-start | bytes 786436
  161.8 1.5 collective-permute-start.32
  161.8 1.5 copy-start.8
  161.8 2.3 %collective-permute-start.34 = (bf16[512,256]{1,0:T(8,128)(2,1)S(1)}, bf16[512,256]{1,0:T(8,128)(2,1)}, u32[]{:S(2)}, u32[]{:S(2)}) collective-permute-start(bf16[512,256]{1,0:T(8,128)(2,1)S(1)} %collective-permute-done.33.refs_16_), channel_id=1, source_target_pairs={{0,4},{4,0},{1,5},{5,1},{2,6},{6,2},{3,7},{7,3},{8,12},{12,8},{9,1... | collective-permute-start | bytes 786440 | tf_op jit(solution)/shard_map/ppermute | solution.py:569
  162.3 1.0 copy-start.9
  162.6 0.8 copy-start.10
  163.4 0.7 copy-start.15
  164.1 2.9 %copy-start.6 = (bf16[16,128,128]{2,1,0:T(8,128)(2,1)}, bf16[16,128,128]{2,1,0:T(8,128)(2,1)S(1)}, u32[]{:S(2)}) copy-start(bf16[16,128,128]{2,1,0:T(8,128)(2,1)S(1)} %all-to-all-done.1.refs_0_.refs_1_) | copy-start | bytes 1572868
  164.1 2.9 %copy-start.7 = (bf16[1024,512]{1,0:T(8,128)(2,1)}, bf16[1024,512]{1,0:T(8,128)(2,1)S(1)}, u32[]{:S(2)}) copy-start(bf16[1024,512]{1,0:T(8,128)(2,1)S(1)} %collective-permute-done.27.refs_11_) | copy-start | bytes 3145732
  164.1 14.3 %collective-permute-start.35 = (bf16[16,128,128]{2,1,0:T(8,128)(2,1)S(1)}, bf16[16,128,128]{2,1,0:T(8,128)(2,1)S(1)}, u32[]{:S(2)}, u32[]{:S(2)}) collective-permute-start(bf16[16,128,128]{2,1,0:T(8,128)(2,1)S(1)} %all-to-all-done.1.refs_0_.refs_1_), channel_id=1, source_target_pairs={{0,8},{8,0},{16,24},{24,16},{1,9},{9,1},{17,25},{25,17},{2,10},{10... | collective-permute-start | bytes 1572872 | tf_op jit(solution)/shard_map/ppermute | solution.py:51
  166.2 13.7 %collective-permute-start.36 = (bf16[16,128,128]{2,1,0:T(8,128)(2,1)S(1)}, bf16[16,128,128]{2,1,0:T(8,128)(2,1)S(1)}, u32[]{:S(2)}, u32[]{:S(2)}) collective-permute-start(bf16[16,128,128]{2,1,0:T(8,128)(2,1)S(1)} %all-to-all-done.1.refs_0_.refs_1_), channel_id=1, source_target_pairs={{0,16},{8,24},{16,0},{24,8},{1,17},{9,25},{17,1},{25,9},{2,18},{10... | collective-permute-start | bytes 1572872 | tf_op jit(solution)/shard_map/ppermute | solution.py:51
  178.4 1.5 copy-start.19
  179.9 0.8 copy-start.20
  180.7 14.5 %copy-start = (bf16[128,1024]{1,0:T(8,128)(2,1)S(1)}, bf16[128,1024]{1,0:T(8,128)(2,1)}, u32[]{:S(2)}) copy-start(bf16[128,1024]{1,0:T(8,128)(2,1)} %get-tuple-element.111.own_x) | copy-start | bytes 786436
  180.7 14.5 %copy-start.1 = (bf16[128,1024]{1,0:T(8,128)(2,1)S(1)}, bf16[128,1024]{1,0:T(8,128)(2,1)}, u32[]{:S(2)}) copy-start(bf16[128,1024]{1,0:T(8,128)(2,1)} %get-tuple-element.112.own_y) | copy-start | bytes 786436
  187.2 7.5 %collective-permute-start.37 = (bf16[128,1024]{1,0:T(8,128)(2,1)}, bf16[128,1024]{1,0:T(8,128)(2,1)S(1)}, u32[]{:S(2)}, u32[]{:S(2)}) collective-permute-start(bf16[128,1024]{1,0:T(8,128)(2,1)} %get-tuple-element.115), channel_id=1, source_target_pairs={{0,8},{8,0},{16,24},{24,16},{1,9},{9,1},{17,25},{25,17},{2,10},{10... | collective-permute-start | bytes 786440 | tf_op jit(solution)/shard_map/ppermute | solution.py:51
  187.7 7.4 %collective-permute-start.38 = (bf16[128,1024]{1,0:T(8,128)(2,1)}, bf16[128,1024]{1,0:T(8,128)(2,1)S(1)}, u32[]{:S(2)}, u32[]{:S(2)}) collective-permute-start(bf16[128,1024]{1,0:T(8,128)(2,1)} %get-tuple-element.116), channel_id=1, source_target_pairs={{0,16},{8,24},{16,0},{24,8},{1,17},{9,25},{17,1},{25,9},{2,18},{10... | collective-permute-start | bytes 786440 | tf_op jit(solution)/shard_map/ppermute | solution.py:51

commit v6 on v5

--- a/solution.py
+++ b/solution.py
@@ -449,7 +449,7 @@
             pltpu.VMEM((2, BLK, depth), BF16),
             pltpu.SemaphoreType.DMA((6 * len(shared),)),
         ],
-        compiler_params=pltpu.CompilerParams(vmem_limit_bytes=58 << 20),
+        compiler_params=pltpu.CompilerParams(vmem_limit_bytes=48 << 20),
         cost_estimate=pl.CostEstimate(
             flops=16 * BLK * depth * width, bytes_accessed=16 * depth * width, transcendentals=0
         ),
@@ -611,9 +611,10 @@
     landed = lax.all_to_all(attended, ("head", "line"), 0, 0, tiled=True)
     last = jnp.where(inside, o_crossed, o_third)
     shared.append([last, *share(last)])
-    landed, *others = barrier((landed, *(pair(piece) for pieces in shared for piece in pieces)))
-    shared = [pieces + others[3 * i : 3 * i + 3] for i, pieces in enumerate(shared)]
+    landed, *rest = barrier((landed, *shared[2], *(pair(piece) for pieces in shared[:2] for piece in pieces)))
+    shared = [shared[0] + rest[3:6], shared[1] + rest[6:]]
     landed_x, landed_y = hop(landed, 1), hop(landed, 2)
+    shared.append(rest[:3] + [pair(piece) for piece in rest[:3]])
     own_x, own_y = leave(order, landed, landed, shared, heads, lines)
     own_x, own_y, landed_x, landed_y = barrier((own_x, own_y, landed_x, landed_y))
     to_x, to_y = leave(order, landed_x, landed_y, shared, heads, lines)

time: 198 us -> 193 us (0.975)
  local copies, waits for them, and re-layouts: 8.64 us -> 16.2 us
  waiting for transfers between devices: 88.3 us -> 83.3 us
  starting transfers between devices: 46.3 us -> 41.7 us
  Pallas kernels: 46.2 us -> 43.9 us
    unnamed x46 -> x44, local copies, waits for them, and re-layouts: 3.2 us -> 9.86 us
    ppermute x14, waiting for transfers between devices: 43.6 us -> 37.1 us  [hop(): return lax.ppermute(part, 'head', xor_pairs(4, bit))]
    pallas_call x2, Pallas kernels: 13 us -> 9.43 us  [leave(): pl.pallas_call(functools.partial(leave_kernel, heads, lines, len(shared))...]
    all_to_all x1, starting transfers between devices: 7.07 us -> 4.71 us  [shards(): landed = lax.all_to_all(attended, ('head', 'line'), 0, 0, tiled=True)]
  transfers between devices with their start and end apart: 41 -> 41, of which waited for: 21 -> 23; matrix products, arithmetic and copies ran while one was open for 6% -> 7% of each run, Pallas kernels for 19% -> 20%
where the time goes in v6:
time: 193 us; the launch traced here: 192 us
  waiting for transfers between devices  83.3 us (43%)
  Pallas kernels  43.9 us (23%)
  starting transfers between devices  41.7 us (22%)
  local copies, waits for them, and re-layouts  16.2 us (8%)
  other arithmetic  6.93 us (4%)
    ppermute x10, waiting for transfers between devices, along(): return lax.ppermute(part, 'line', pairs)  43.1 us
    ppermute x14, waiting for transfers between devices, hop(): return lax.ppermute(part, 'head', xor_pairs(4, bit))  37.1 us
    ppermute x14, starting transfers between devices, hop(): return lax.ppermute(part, 'head', xor_pairs(4, bit))  17.6 us
    ppermute x10, starting transfers between devices, along(): return lax.ppermute(part, 'line', pairs)  12.9 us
    pallas_call x1, Pallas kernels, begin(): pl.pallas_call(functools.partial(begin_kernel, counts, runs, rest, places...  12.5 us
    pallas_call x1, Pallas kernels, enter(): pl.pallas_call(functools.partial(enter_kernel, heads, runs, rest, places)...  11.5 us
    unnamed x44, local copies, waits for them, and re-layouts  9.86 us
    pallas_call x2, Pallas kernels, leave(): pl.pallas_call(functools.partial(leave_kernel, heads, lines, len(shared))...  9.43 us
  transfers between devices with their start and end apart: 41, of which 23 were waited for; matrix products, arithmetic and copies ran while one was open for 7% of the time, Pallas kernels for 20%

profile of v6, /device:TPU:0, one launch (start us, length us, event | category | flops | bytes accessed | tf_op | source)
XLA Modules:
  0.0 192.4 jit_solution(4641974688278932778)
XLA Ops:
  0.0 3.0 %collective-permute-start = (bf16[128,4096]{1,0:T(8,128)(2,1)}, bf16[128,4096]{1,0:T(8,128)(2,1)}, u32[]{:S(2)}, u32[]{:S(2)}) collective-permute-start(bf16[128,4096]{1,0:T(8,128)(2,1)} %refs_0_.1), channel_id=1, source_target_pairs={{0,1},{1,0},{2,3},{3,2},{4,5},{5,4},{6,7},{7,6},{8,9},{9,8},{10,11... | collective-permute-start | bytes 3145736 | tf_op jit(solution)/shard_map/ppermute | solution.py:566
  3.0 1.6 collective-permute-start.1
  4.6 1.5 collective-permute-start.5
  6.1 1.5 collective-permute-start.6
  8.7 1.0 select_reduce_fusion.2
  13.8 12.7 %collective-permute-done.refs_1_ = bf16[128,4096]{1,0:T(8,128)(2,1)} collective-permute-done((bf16[128,4096]{1,0:T(8,128)(2,1)}, bf16[128,4096]{1,0:T(8,128)(2,1)}, u32[]{:S(2)}, u32[]{:S(2)}) %collective-permute-start) | collective-permute-done | bytes 1048608 | tf_op jit(solution)/shard_map/ppermute | solution.py:566
  26.5 1.3 collective-permute-start.3
  27.8 1.7 collective-permute-start.4
  29.5 12.2 %collective-permute-done.5.refs_5_.refs_7_ = bf16[3,512,512]{2,1,0:T(8,128)(2,1)S(1)} collective-permute-done((bf16[3,512,512]{2,1,0:T(8,128)(2,1)}, bf16[3,512,512]{2,1,0:T(8,128)(2,1)S(1)}, u32[]{:S(2)}, u32[]{:S(2)}) %collective-permute-start.5) | collective-permute-done | bytes 1572896 | tf_op jit(solution)/shard_map/ppermute | solution.py:51
  41.7 1.3 collective-permute-done.6.refs_6_.refs_8_
  43.0 1.1 fusion.18
  44.0 1.6 collective-permute-start.7
  45.6 0.7 collective-permute-start.8
  46.4 2.1 %slice.32 = bf16[3,256,512]{2,1,0:T(8,128)(2,1)} slice(bf16[3,512,512]{2,1,0:T(8,128)(2,1)} %collective-permute-done.6.refs_6_.refs_8_), slice={[0:3], [0:256], [0:512]} | slice | bytes 1572864 | tf_op jit(solution)/shard_map/slice | solution.py:580
  48.5 0.9 slice.33
  49.4 2.3 %collective-permute-done.7.refs_3_ = bf16[512,256]{1,0:T(8,128)(2,1)S(1)} collective-permute-done((bf16[512,256]{1,0:T(8,128)(2,1)S(1)}, bf16[512,256]{1,0:T(8,128)(2,1)S(1)}, u32[]{:S(2)}, u32[]{:S(2)}) %collective-permute-start.7) | collective-permute-done | bytes 262176 | tf_op jit(solution)/shard_map/ppermute | solution.py:51
  51.7 1.3 collective-permute-done.8.refs_4_
  53.1 2.0 %collective-permute-done.3.refs_3_ = bf16[128,4096]{1,0:T(8,128)(2,1)S(1)} collective-permute-done((bf16[128,4096]{1,0:T(8,128)(2,1)}, bf16[128,4096]{1,0:T(8,128)(2,1)S(1)}, u32[]{:S(2)}, u32[]{:S(2)}) %collective-permute-start.3) | collective-permute-done | bytes 1048608 | tf_op jit(solution)/shard_map/ppermute | solution.py:566
  55.1 0.9 copy-done.17
  56.0 1.5 collective-permute-start.9
  57.5 1.5 collective-permute-start.10
  59.0 1.3 collective-permute-start.13
  61.1 1.0 copy-done.15
  62.1 12.5 %begin.1 = (f32[3,384,512]{2,1,0:T(8,128)}, bf16[384,1024]{1,0:T(8,128)(2,1)}) custom-call(s32[1]{0:T(128)} %bitcast.4.flag, s32[8]{0:T(128)} %stack.47.order, f32[1,4096]{1,0:T(1,128)} %bitcast.16, bf16[128,4096]{1,0:T(8,128)(2,1)} %refs_0_.1, bf16[128,4096]{1,0:T(8,128)(2,1)} %collective-permute-done.refs_1_, ...), custom_call_target="tpu_custom_call" | custom-call | flops 1 | bytes 1 | tf_op jit(solution)/shard_map/begin/pallas_call | solution.py:315
  74.6 1.7 collective-permute-done.9.refs_2_
  76.3 1.2 collective-permute-done.10.refs_3_
  78.0 8.8 %collective-permute-done.13.refs_1_ = bf16[128,4096]{1,0:T(8,128)(2,1)} collective-permute-done((bf16[128,4096]{1,0:T(8,128)(2,1)}, bf16[128,4096]{1,0:T(8,128)(2,1)}, u32[]{:S(2)}, u32[]{:S(2)}) %collective-permute-start.13) | collective-permute-done | bytes 1048608 | tf_op jit(solution)/shard_map/ppermute | solution.py:566
  86.9 0.7 collective-permute-start.17
  88.0 11.5 %enter.1 = bf16[4,3,4,128,128]{4,3,2,1,0:T(8,128)(2,1)} custom-call(s32[1]{0:T(128)} %bitcast.4.flag, s32[8]{0:T(128)} %stack.47.order, f32[1,4096]{1,0:T(1,128)} %bitcast.17, f32[3,384,512]{2,1,0:T(8,128)} %get-tuple-element.77.begun, bf16[384,1024]{1,0:T(8,128)(2,1)} %get-tuple-element.78.left, bf16[128,4096]{1,0:T(8,128)(2,1)} %collective-permute-done.4.refs_0_, ...), custom_call_target="tpu_custom_call" | custom-call | flops 1 | bytes 1 | tf_op jit(solution)/shard_map/enter/pallas_call | solution.py:379
  99.6 4.4 %all-to-all-start = ((bf16[4,3,4,128,128]{4,3,2,1,0:T(8,128)(2,1)}), bf16[4,3,4,128,128]{4,3,2,1,0:T(8,128)(2,1)}, u32[]{:S(2)}, u32[]{:S(2)}) async-start(bf16[4,3,4,128,128]{4,3,2,1,0:T(8,128)(2,1)} %enter.1), calls=%async_computation | async-start | bytes 3145728 | tf_op jit(solution)/shard_map/all_to_all | solution.py:484
  104.0 0.7 collective-permute-start.18
  104.7 1.3 collective-permute-start.19
  106.0 16.1 %collective-permute-done.19 = bf16[512,512]{1,0:T(8,128)(2,1)S(1)} collective-permute-done((bf16[512,512]{1,0:T(8,128)(2,1)S(1)}, bf16[512,512]{1,0:T(8,128)(2,1)S(1)}, u32[]{:S(2)}, u32[]{:S(2)}) %collective-permute-start.19) | collective-permute-done | bytes 524320 | tf_op jit(solution)/shard_map/ppermute | solution.py:566
  122.6 1.3 collective-permute-start.21
  124.1 1.5 collective-permute-start.22
  125.6 1.2 collective-permute-start.23
  126.9 1.0 pad_maximum_fusion.refs_8_
  127.9 8.8 %attention.1 = bf16[16,128,128]{2,1,0:T(8,128)(2,1)} custom-call(s32[16,18]{1,0:T(8,128)S(1)} %fusion.7.places, f32[16,18]{1,0:T(8,128)S(1)} %multiply_select_fusion.biases, s32[16]{0:T(128)S(1)} %select_reduce_fusion.4.turns, s32[3]{0:T(128)S(1)} %convert_reduce_fusion.5.ends, s32[16]{0:T(128)S(1)} %add.174.targets, ...), custom_call_target="tpu_custom_call" | custom-call | flops 2415919104 | bytes 4194304 | tf_op jit(solution)/shard_map/attention/pallas_call | solution.py:158
  136.8 3.4 %collective-permute-done.21 = bf16[512,512]{1,0:T(8,128)(2,1)S(1)} collective-permute-done((bf16[512,512]{1,0:T(8,128)(2,1)S(1)}, bf16[512,512]{1,0:T(8,128)(2,1)S(1)}, u32[]{:S(2)}, u32[]{:S(2)}) %collective-permute-start.21) | collective-permute-done | bytes 524320 | tf_op jit(solution)/shard_map/ppermute | solution.py:566
  140.2 0.8 copy-done.21
  141.0 4.7 %all-to-all-start.1 = ((bf16[16,128,128]{2,1,0:T(8,128)(2,1)}), bf16[16,128,128]{2,1,0:T(8,128)(2,1)S(1)}, u32[]{:S(2)}, u32[]{:S(2)}) async-start(bf16[16,128,128]{2,1,0:T(8,128)(2,1)} %attention.1), calls=%async_computation.1 | async-start | bytes 1048576 | tf_op jit(solution)/shard_map/all_to_all | solution.py:611
  146.8 1.1 broadcast_select_fusion.refs_14_
  148.0 0.8 copy-done.2
  148.7 1.9 collective-permute-start.24
  150.6 0.7 copy-done.4
  151.3 1.5 collective-permute-start.25
  152.8 6.8 %collective-permute-done.24.refs_15_ = bf16[512,256]{1,0:T(8,128)(2,1)S(1)} collective-permute-done((bf16[512,256]{1,0:T(8,128)(2,1)S(1)}, bf16[512,256]{1,0:T(8,128)(2,1)S(1)}, u32[]{:S(2)}, u32[]{:S(2)}) %collective-permute-start.24) | collective-permute-done | bytes 262176 | tf_op jit(solution)/shard_map/ppermute | solution.py:51
  159.6 1.5 collective-permute-done.25.refs_16_
  161.1 0.7 copy-done.9
  161.8 0.8 all-to-all-done.1.refs_0_.refs_1_
  162.6 1.0 collective-permute-start.35
  164.5 1.2 collective-permute-done.33.refs_18_
  166.1 0.8 copy-done.16
  166.9 0.9 copy-done.3
  167.8 0.9 copy-done.5
  168.8 0.9 copy-done.7
  169.7 0.9 copy-done.10
  170.7 4.7 %leave.2 = (bf16[128,1024]{1,0:T(8,128)(2,1)S(1)}, bf16[128,1024]{1,0:T(8,128)(2,1)S(1)}) custom-call(s32[4]{0:T(128)S(1)} %dynamic-slice_bitcast_fusion.order, bf16[16,128,128]{2,1,0:T(8,128)(2,1)S(1)} %all-to-all-done.1.refs_0_.refs_1_, bf16[16,128,128]{2,1,0:T(8,128)(2,1)S(1)} %all-to-all-done.1.refs_0_.refs_1_, bf16[512,512]{1,0:T(8,128)(2,1)S(1)} %copy-done, ...), custom_call_target="tpu_custom_call" | custom-call | flops 1073741824 | bytes 8388608 | tf_op jit(solution)/shard_map/leave/pallas_call | solution.py:441
  175.4 1.5 collective-permute-done.35.refs_0_
  177.5 4.7 %leave.3 = (bf16[128,1024]{1,0:T(8,128)(2,1)S(1)}, bf16[128,1024]{1,0:T(8,128)(2,1)S(1)}) custom-call(s32[4]{0:T(128)S(1)} %dynamic-slice_bitcast_fusion.order, bf16[16,128,128]{2,1,0:T(8,128)(2,1)S(1)} %collective-permute-done.35.refs_0_, bf16[16,128,128]{2,1,0:T(8,128)(2,1)S(1)} %collective-permute-done.36.refs_1_, bf16[512,512]{1,0:T(8,128)(2,1)S(1)} %copy-done, ...), custom_call_target="tpu_custom_call" | custom-call | flops 1073741824 | bytes 8388608 | tf_op jit(solution)/shard_map/leave/pallas_call | solution.py:441
  182.3 1.2 collective-permute-start.37
  184.1 5.8 %collective-permute-done.37.from_x = bf16[128,1024]{1,0:T(8,128)(2,1)S(1)} collective-permute-done((bf16[128,1024]{1,0:T(8,128)(2,1)S(1)}, bf16[128,1024]{1,0:T(8,128)(2,1)S(1)}, u32[]{:S(2)}, u32[]{:S(2)}) %collective-permute-start.37) | collective-permute-done | bytes 262176 | tf_op jit(solution)/shard_map/ppermute | solution.py:51
  189.9 0.9 collective-permute-done.38.from_y
  190.8 1.6 place.1
  (113 shorter events, 11.3 us)
Async XLA Ops:
  0.0 26.5 %collective-permute-start = (bf16[128,4096]{1,0:T(8,128)(2,1)}, bf16[128,4096]{1,0:T(8,128)(2,1)}, u32[]{:S(2)}, u32[]{:S(2)}) collective-permute-start(bf16[128,4096]{1,0:T(8,128)(2,1)} %refs_0_.1), channel_id=1, source_target_pairs={{0,1},{1,0},{2,3},{3,2},{4,5},{5,4},{6,7},{7,6},{8,9},{9,8},{10,11... | collective-permute-start | bytes 3145736 | tf_op jit(solution)/shard_map/ppermute | solution.py:566
  3.0 23.5 %collective-permute-start.1 = (bf16[128,4096]{1,0:T(8,128)(2,1)}, bf16[128,4096]{1,0:T(8,128)(2,1)}, u32[]{:S(2)}, u32[]{:S(2)}) collective-permute-start(bf16[128,4096]{1,0:T(8,128)(2,1)} %refs_0_.1), channel_id=1, source_target_pairs={{1,2},{2,1},{5,6},{6,5},{9,10},{10,9},{13,14},{14,13},{17,18},{18,... | collective-permute-start | bytes 3145736 | tf_op jit(solution)/shard_map/ppermute | solution.py:566
  4.6 21.9 %collective-permute-start.2 = (bf16[3,512,512]{2,1,0:T(8,128)(2,1)}, bf16[3,512,512]{2,1,0:T(8,128)(2,1)S(1)}, u32[]{:S(2)}, u32[]{:S(2)}) collective-permute-start(bf16[3,512,512]{2,1,0:T(8,128)(2,1)} %refs_6_.1), channel_id=1, source_target_pairs={{0,4},{4,0},{1,5},{5,1},{2,6},{6,2},{3,7},{7,3},{8,12},{12,8},{9,1... | collective-permute-start | bytes 4718600 | tf_op jit(solution)/shard_map/ppermute | solution.py:569
  4.6 37.0 %collective-permute-start.5 = (bf16[3,512,512]{2,1,0:T(8,128)(2,1)}, bf16[3,512,512]{2,1,0:T(8,128)(2,1)S(1)}, u32[]{:S(2)}, u32[]{:S(2)}) collective-permute-start(bf16[3,512,512]{2,1,0:T(8,128)(2,1)} %refs_6_.1), channel_id=1, source_target_pairs={{0,8},{8,0},{16,24},{24,16},{1,9},{9,1},{17,25},{25,17},{2,10},{10... | collective-permute-start | bytes 4718600 | tf_op jit(solution)/shard_map/ppermute | solution.py:51
  6.1 36.8 %collective-permute-start.6 = (bf16[3,512,512]{2,1,0:T(8,128)(2,1)}, bf16[3,512,512]{2,1,0:T(8,128)(2,1)}, u32[]{:S(2)}, u32[]{:S(2)}) collective-permute-start(bf16[3,512,512]{2,1,0:T(8,128)(2,1)} %refs_6_.1), channel_id=1, source_target_pairs={{0,16},{8,24},{16,0},{24,8},{1,17},{9,25},{17,1},{25,9},{2,18},{10... | collective-permute-start | bytes 4718600 | tf_op jit(solution)/shard_map/ppermute | solution.py:51
  26.5 22.9 %copy-start.14 = (bf16[3,512,512]{2,1,0:T(8,128)(2,1)}, bf16[3,512,512]{2,1,0:T(8,128)(2,1)S(1)}, u32[]{:S(2)}) copy-start(bf16[3,512,512]{2,1,0:T(8,128)(2,1)S(1)} %collective-permute-done.2.refs_7_.refs_9_) | copy-start | bytes 4718596
  26.5 28.5 %collective-permute-start.3 = (bf16[128,4096]{1,0:T(8,128)(2,1)}, bf16[128,4096]{1,0:T(8,128)(2,1)S(1)}, u32[]{:S(2)}, u32[]{:S(2)}) collective-permute-start(bf16[128,4096]{1,0:T(8,128)(2,1)} %collective-permute-done.1.refs_2_), channel_id=1, source_target_pairs={{1,0},{2,3},{5,4},{6,7},{9,8},{10,11},{13,12},{14,15},{17,16},{18,... | collective-permute-start | bytes 3145736 | tf_op jit(solution)/shard_map/ppermute | solution.py:566
  27.8 27.2 %collective-permute-start.4 = (bf16[128,4096]{1,0:T(8,128)(2,1)}, bf16[128,4096]{1,0:T(8,128)(2,1)}, u32[]{:S(2)}, u32[]{:S(2)}) collective-permute-start(bf16[128,4096]{1,0:T(8,128)(2,1)} %collective-permute-done.refs_1_), channel_id=1, source_target_pairs={{1,2},{2,1},{5,6},{6,5},{9,10},{10,9},{13,14},{14,13},{17,18},{18,... | collective-permute-start | bytes 3145736 | tf_op jit(solution)/shard_map/ppermute | solution.py:566
  41.7 13.4 %copy-start.12 = (bf16[3,512,512]{2,1,0:T(8,128)(2,1)}, bf16[3,512,512]{2,1,0:T(8,128)(2,1)S(1)}, u32[]{:S(2)}) copy-start(bf16[3,512,512]{2,1,0:T(8,128)(2,1)S(1)} %collective-permute-done.5.refs_5_.refs_7_) | copy-start | bytes 4718596
  44.0 7.7 %collective-permute-start.7 = (bf16[512,256]{1,0:T(8,128)(2,1)S(1)}, bf16[512,256]{1,0:T(8,128)(2,1)S(1)}, u32[]{:S(2)}, u32[]{:S(2)}) collective-permute-start(bf16[512,256]{1,0:T(8,128)(2,1)S(1)} %get-tuple-element.126), channel_id=1, source_target_pairs={{0,16},{8,24},{16,0},{24,8},{1,17},{9,25},{17,1},{25,9},{2,18},{10... | collective-permute-start | bytes 786440 | tf_op jit(solution)/shard_map/ppermute | solution.py:51
  45.6 7.4 %collective-permute-start.8 = (bf16[512,256]{1,0:T(8,128)(2,1)S(1)}, bf16[512,256]{1,0:T(8,128)(2,1)}, u32[]{:S(2)}, u32[]{:S(2)}) collective-permute-start(bf16[512,256]{1,0:T(8,128)(2,1)S(1)} %get-tuple-element.125), channel_id=1, source_target_pairs={{0,8},{8,0},{16,24},{24,16},{1,9},{9,1},{17,25},{25,17},{2,10},{10... | collective-permute-start | bytes 786440 | tf_op jit(solution)/shard_map/ppermute | solution.py:51
  55.0 1.0 copy-start.17
  55.0 5.9 %collective-permute-start.11 = (bf16[3,512,512]{2,1,0:T(8,128)(2,1)S(1)}, bf16[3,512,512]{2,1,0:T(8,128)(2,1)S(1)}, u32[]{:S(2)}, u32[]{:S(2)}) collective-permute-start(bf16[3,512,512]{2,1,0:T(8,128)(2,1)S(1)} %collective-permute-done.5.refs_5_.refs_7_), channel_id=1, source_target_pairs={{0,4},{4,0},{1,5},{5,1},{2,6},{6,2},{3,7},{7,3},{8,12},{12,8},{9,1... | collective-permute-start | bytes 4718600 | tf_op jit(solution)/shard_map/ppermute | solution.py:569
  56.0 5.1 %collective-permute-start.12 = (bf16[3,512,512]{2,1,0:T(8,128)(2,1)}, bf16[3,512,512]{2,1,0:T(8,128)(2,1)}, u32[]{:S(2)}, u32[]{:S(2)}) collective-permute-start(bf16[3,512,512]{2,1,0:T(8,128)(2,1)} %collective-permute-done.6.refs_6_.refs_8_), channel_id=1, source_target_pairs={{0,4},{4,0},{1,5},{5,1},{2,6},{6,2},{3,7},{7,3},{8,12},{12,8},{9,1... | collective-permute-start | bytes 4718600 | tf_op jit(solution)/shard_map/ppermute | solution.py:569
  56.0 20.3 %collective-permute-start.9 = (bf16[3,256,512]{2,1,0:T(8,128)(2,1)}, bf16[3,256,512]{2,1,0:T(8,128)(2,1)}, u32[]{:S(2)}, u32[]{:S(2)}) collective-permute-start(bf16[3,256,512]{2,1,0:T(8,128)(2,1)} %slice.32), channel_id=1, source_target_pairs={{0,8},{8,0},{16,24},{24,16},{1,9},{9,1},{17,25},{25,17},{2,10},{10... | collective-permute-start | bytes 2359304 | tf_op jit(solution)/shard_map/ppermute | solution.py:51
  57.5 20.0 %collective-permute-start.10 = (bf16[3,256,512]{2,1,0:T(8,128)(2,1)}, bf16[3,256,512]{2,1,0:T(8,128)(2,1)}, u32[]{:S(2)}, u32[]{:S(2)}) collective-permute-start(bf16[3,256,512]{2,1,0:T(8,128)(2,1)} %slice.33), channel_id=1, source_target_pairs={{0,16},{8,24},{16,0},{24,8},{1,17},{9,25},{17,1},{25,9},{2,18},{10... | collective-permute-start | bytes 2359304 | tf_op jit(solution)/shard_map/ppermute | solution.py:51
  59.0 27.8 %collective-permute-start.13 = (bf16[128,4096]{1,0:T(8,128)(2,1)}, bf16[128,4096]{1,0:T(8,128)(2,1)}, u32[]{:S(2)}, u32[]{:S(2)}) collective-permute-start(bf16[128,4096]{1,0:T(8,128)(2,1)} %collective-permute-done.4.refs_0_), channel_id=1, source_target_pairs={{1,0},{2,3},{5,4},{6,7},{9,8},{10,11},{13,12},{14,15},{17,16},{18,... | collective-permute-start | bytes 3145736 | tf_op jit(solution)/shard_map/ppermute | solution.py:566
  61.0 1.2 copy-start.15
  62.1 24.7 %copy-start = (bf16[512,512]{1,0:T(8,128)(2,1)S(1)}, bf16[512,512]{1,0:T(8,128)(2,1)}, u32[]{:S(2)}) copy-start(bf16[512,512]{1,0:T(8,128)(2,1)} %refs_2_.3) | copy-start | bytes 1572868
  77.5 9.3 %collective-permute-start.14 = (bf16[3,256,512]{2,1,0:T(8,128)(2,1)}, bf16[3,256,512]{2,1,0:T(8,128)(2,1)S(1)}, u32[]{:S(2)}, u32[]{:S(2)}) collective-permute-start(bf16[3,256,512]{2,1,0:T(8,128)(2,1)} %collective-permute-done.9.refs_2_), channel_id=1, source_target_pairs={{0,4},{4,0},{1,5},{5,1},{2,6},{6,2},{3,7},{7,3},{8,12},{12,8},{9,1... | collective-permute-start | bytes 2359304 | tf_op jit(solution)/shard_map/ppermute | solution.py:569
  77.5 9.3 %collective-permute-start.15 = (bf16[3,256,512]{2,1,0:T(8,128)(2,1)}, bf16[3,256,512]{2,1,0:T(8,128)(2,1)S(1)}, u32[]{:S(2)}, u32[]{:S(2)}) collective-permute-start(bf16[3,256,512]{2,1,0:T(8,128)(2,1)} %collective-permute-done.10.refs_3_), channel_id=1, source_target_pairs={{0,4},{4,0},{1,5},{5,1},{2,6},{6,2},{3,7},{7,3},{8,12},{12,8},{9,1... | collective-permute-start | bytes 2359304 | tf_op jit(solution)/shard_map/ppermute | solution.py:569
  86.8 0.9 copy-start.18
  86.8 1.2 copy-start.19
  86.8 12.8 %collective-permute-start.16 = (bf16[512,512]{1,0:T(8,128)(2,1)S(1)}, bf16[512,512]{1,0:T(8,128)(2,1)S(1)}, u32[]{:S(2)}, u32[]{:S(2)}) collective-permute-start(bf16[512,512]{1,0:T(8,128)(2,1)S(1)} %copy-done), channel_id=1, source_target_pairs={{0,1},{1,0},{2,3},{3,2},{4,5},{5,4},{6,7},{7,6},{8,9},{9,8},{10,11... | collective-permute-start | bytes 1572872 | tf_op jit(solution)/shard_map/ppermute | solution.py:566
  86.9 12.7 %collective-permute-start.17 = (bf16[512,512]{1,0:T(8,128)(2,1)S(1)}, bf16[512,512]{1,0:T(8,128)(2,1)S(1)}, u32[]{:S(2)}, u32[]{:S(2)}) collective-permute-start(bf16[512,512]{1,0:T(8,128)(2,1)S(1)} %copy-done), channel_id=1, source_target_pairs={{1,2},{2,1},{5,6},{6,5},{9,10},{10,9},{13,14},{14,13},{17,18},{18,... | collective-permute-start | bytes 1572872 | tf_op jit(solution)/shard_map/ppermute | solution.py:566
  99.6 23.0 %all-to-all-start = ((bf16[4,3,4,128,128]{4,3,2,1,0:T(8,128)(2,1)}), bf16[4,3,4,128,128]{4,3,2,1,0:T(8,128)(2,1)}, u32[]{:S(2)}, u32[]{:S(2)}) async-start(bf16[4,3,4,128,128]{4,3,2,1,0:T(8,128)(2,1)} %enter.1), calls=%async_computation | async-start | bytes 3145728 | tf_op jit(solution)/shard_map/all_to_all | solution.py:484
  104.0 2.0 %collective-permute-start.18 = (bf16[512,512]{1,0:T(8,128)(2,1)S(1)}, bf16[512,512]{1,0:T(8,128)(2,1)S(1)}, u32[]{:S(2)}, u32[]{:S(2)}) collective-permute-start(bf16[512,512]{1,0:T(8,128)(2,1)S(1)} %collective-permute-done.16), channel_id=1, source_target_pairs={{1,2},{2,1},{5,6},{6,5},{9,10},{10,9},{13,14},{14,13},{17,18},{18,... | collective-permute-start | bytes 1572872 | tf_op jit(solution)/shard_map/ppermute | solution.py:566
  104.7 17.5 %collective-permute-start.19 = (bf16[512,512]{1,0:T(8,128)(2,1)S(1)}, bf16[512,512]{1,0:T(8,128)(2,1)S(1)}, u32[]{:S(2)}, u32[]{:S(2)}) collective-permute-start(bf16[512,512]{1,0:T(8,128)(2,1)S(1)} %collective-permute-done.17), channel_id=1, source_target_pairs={{1,0},{2,3},{5,4},{6,7},{9,8},{10,11},{13,12},{14,15},{17,16},{18,... | collective-permute-start | bytes 1572872 | tf_op jit(solution)/shard_map/ppermute | solution.py:566
  106.0 18.1 %copy-start.20 = (bf16[512,512]{1,0:T(8,128)(2,1)}, bf16[512,512]{1,0:T(8,128)(2,1)S(1)}, u32[]{:S(2)}) copy-start(bf16[512,512]{1,0:T(8,128)(2,1)S(1)} %collective-permute-done.18) | copy-start | bytes 1572868
  122.6 5.3 %collective-permute-start.20 = (bf16[4,3,4,128,128]{4,3,2,1,0:T(8,128)(2,1)}, bf16[4,3,4,128,128]{4,3,2,1,0:T(8,128)(2,1)S(1)}, u32[]{:S(2)}, u32[]{:S(2)}) collective-permute-start(bf16[4,3,4,128,128]{4,3,2,1,0:T(8,128)(2,1)} %all-to-all-done.refs_0_), channel_id=1, source_target_pairs={{0,4},{4,0},{1,5},{5,1},{2,6},{6,2},{3,7},{7,3},{8,12},{12,8},{9,1... | collective-permute-start | bytes 4718600 | tf_op jit(solution)/shard_map/ppermute | solution.py:47
  122.6 17.6 %collective-permute-start.21 = (bf16[512,512]{1,0:T(8,128)(2,1)S(1)}, bf16[512,512]{1,0:T(8,128)(2,1)S(1)}, u32[]{:S(2)}, u32[]{:S(2)}) collective-permute-start(bf16[512,512]{1,0:T(8,128)(2,1)S(1)} %collective-permute-done.18), channel_id=1, source_target_pairs={{1,0},{2,3},{5,4},{6,7},{9,8},{10,11},{13,12},{14,15},{17,16},{18,... | collective-permute-start | bytes 1572872 | tf_op jit(solution)/shard_map/ppermute | solution.py:566
  124.1 16.1 %collective-permute-start.22 = (bf16[1024,256]{1,0:T(8,128)(2,1)S(1)}, bf16[1024,256]{1,0:T(8,128)(2,1)S(1)}, u32[]{:S(2)}, u32[]{:S(2)}) collective-permute-start(bf16[1024,256]{1,0:T(8,128)(2,1)S(1)} %get-tuple-element.122), channel_id=1, source_target_pairs={{0,16},{8,24},{16,0},{24,8},{1,17},{9,25},{17,1},{25,9},{2,18},{10... | collective-permute-start | bytes 1572872 | tf_op jit(solution)/shard_map/ppermute | solution.py:51
  125.6 14.6 %collective-permute-start.23 = (bf16[1024,256]{1,0:T(8,128)(2,1)S(1)}, bf16[1024,256]{1,0:T(8,128)(2,1)S(1)}, u32[]{:S(2)}, u32[]{:S(2)}) collective-permute-start(bf16[1024,256]{1,0:T(8,128)(2,1)S(1)} %get-tuple-element.121), channel_id=1, source_target_pairs={{0,8},{8,0},{16,24},{24,16},{1,9},{9,1},{17,25},{25,17},{2,10},{10... | collective-permute-start | bytes 1572872 | tf_op jit(solution)/shard_map/ppermute | solution.py:51
  126.9 19.6 %collective-permute-start.26 = (bf16[512,512]{1,0:T(8,128)(2,1)S(1)}, bf16[512,512]{1,0:T(8,128)(2,1)S(1)}, u32[]{:S(2)}, u32[]{:S(2)}) collective-permute-start(bf16[512,512]{1,0:T(8,128)(2,1)S(1)} %copy-done), channel_id=1, source_target_pairs={{0,4},{4,0},{1,5},{5,1},{2,6},{6,2},{3,7},{7,3},{8,12},{12,8},{9,1... | collective-permute-start | bytes 1572872 | tf_op jit(solution)/shard_map/ppermute | solution.py:569
  140.2 0.8 copy-start.21
  141.0 21.6 %collective-permute-start.29 = (bf16[1024,512]{1,0:T(8,128)(2,1)}, bf16[1024,512]{1,0:T(8,128)(2,1)}, u32[]{:S(2)}, u32[]{:S(2)}) collective-permute-start(bf16[1024,512]{1,0:T(8,128)(2,1)} %pad_maximum_fusion.refs_8_), channel_id=1, source_target_pairs={{0,4},{4,0},{1,5},{5,1},{2,6},{6,2},{3,7},{7,3},{8,12},{12,8},{9,1... | collective-permute-start | bytes 3145736 | tf_op jit(solution)/shard_map/ppermute | solution.py:569
  141.0 21.6 %all-to-all-start.1 = ((bf16[16,128,128]{2,1,0:T(8,128)(2,1)}), bf16[16,128,128]{2,1,0:T(8,128)(2,1)S(1)}, u32[]{:S(2)}, u32[]{:S(2)}) async-start(bf16[16,128,128]{2,1,0:T(8,128)(2,1)} %attention.1), calls=%async_computation.1 | async-start | bytes 1048576 | tf_op jit(solution)/shard_map/all_to_all | solution.py:611
  145.7 2.3 %collective-permute-start.27 = (bf16[512,256]{1,0:T(8,128)(2,1)S(1)}, bf16[512,256]{1,0:T(8,128)(2,1)S(1)}, u32[]{:S(2)}, u32[]{:S(2)}) collective-permute-start(bf16[512,256]{1,0:T(8,128)(2,1)S(1)} %collective-permute-done.7.refs_3_), channel_id=1, source_target_pairs={{0,4},{4,0},{1,5},{5,1},{2,6},{6,2},{3,7},{7,3},{8,12},{12,8},{9,1... | collective-permute-start | bytes 786440 | tf_op jit(solution)/shard_map/ppermute | solution.py:569
  146.0 4.6 %collective-permute-start.28 = (bf16[512,256]{1,0:T(8,128)(2,1)}, bf16[512,256]{1,0:T(8,128)(2,1)S(1)}, u32[]{:S(2)}, u32[]{:S(2)}) collective-permute-start(bf16[512,256]{1,0:T(8,128)(2,1)} %collective-permute-done.8.refs_4_), channel_id=1, source_target_pairs={{0,4},{4,0},{1,5},{5,1},{2,6},{6,2},{3,7},{7,3},{8,12},{12,8},{9,1... | collective-permute-start | bytes 786440 | tf_op jit(solution)/shard_map/ppermute | solution.py:569
  146.3 14.8 %collective-permute-start.30 = (bf16[1024,256]{1,0:T(8,128)(2,1)S(1)}, bf16[1024,256]{1,0:T(8,128)(2,1)S(1)}, u32[]{:S(2)}, u32[]{:S(2)}) collective-permute-start(bf16[1024,256]{1,0:T(8,128)(2,1)S(1)} %collective-permute-done.22.refs_9_), channel_id=1, source_target_pairs={{0,4},{4,0},{1,5},{5,1},{2,6},{6,2},{3,7},{7,3},{8,12},{12,8},{9,1... | collective-permute-start | bytes 1572872 | tf_op jit(solution)/shard_map/ppermute | solution.py:569
  146.5 15.3 %collective-permute-start.31 = (bf16[1024,256]{1,0:T(8,128)(2,1)S(1)}, bf16[1024,256]{1,0:T(8,128)(2,1)}, u32[]{:S(2)}, u32[]{:S(2)}) collective-permute-start(bf16[1024,256]{1,0:T(8,128)(2,1)S(1)} %collective-permute-done.23.refs_10_), channel_id=1, source_target_pairs={{0,4},{4,0},{1,5},{5,1},{2,6},{6,2},{3,7},{7,3},{8,12},{12,8},{9,1... | collective-permute-start | bytes 1572872 | tf_op jit(solution)/shard_map/ppermute | solution.py:569
  147.9 13.2 %copy-start.13 = (bf16[512,512]{1,0:T(8,128)(2,1)}, bf16[512,512]{1,0:T(8,128)(2,1)S(1)}, u32[]{:S(2)}) copy-start(bf16[512,512]{1,0:T(8,128)(2,1)S(1)} %broadcast_select_fusion.refs_14_) | copy-start | bytes 1572868
  148.0 0.8 copy-start.2
  148.7 10.8 %collective-permute-start.24 = (bf16[512,256]{1,0:T(8,128)(2,1)S(1)}, bf16[512,256]{1,0:T(8,128)(2,1)S(1)}, u32[]{:S(2)}, u32[]{:S(2)}) collective-permute-start(bf16[512,256]{1,0:T(8,128)(2,1)S(1)} %get-tuple-element.124), channel_id=1, source_target_pairs={{0,16},{8,24},{16,0},{24,8},{1,17},{9,25},{17,1},{25,9},{2,18},{10... | collective-permute-start | bytes 786440 | tf_op jit(solution)/shard_map/ppermute | solution.py:51
  150.6 0.7 copy-start.4
  151.3 9.8 %collective-permute-start.25 = (bf16[512,256]{1,0:T(8,128)(2,1)S(1)}, bf16[512,256]{1,0:T(8,128)(2,1)S(1)}, u32[]{:S(2)}, u32[]{:S(2)}) collective-permute-start(bf16[512,256]{1,0:T(8,128)(2,1)S(1)} %get-tuple-element.123), channel_id=1, source_target_pairs={{0,8},{8,0},{16,24},{24,16},{1,9},{9,1},{17,25},{25,17},{2,10},{10... | collective-permute-start | bytes 786440 | tf_op jit(solution)/shard_map/ppermute | solution.py:51
  159.6 1.5 copy-start.6
  161.1 0.7 copy-start.9
  161.8 13.6 %copy-start.1 = (bf16[1024,256]{1,0:T(8,128)(2,1)}, bf16[1024,256]{1,0:T(8,128)(2,1)S(1)}, u32[]{:S(2)}) copy-start(bf16[1024,256]{1,0:T(8,128)(2,1)S(1)} %collective-permute-done.30.refs_12_) | copy-start | bytes 1572868
  162.6 3.5 %collective-permute-start.32 = (bf16[512,512]{1,0:T(8,128)(2,1)}, bf16[512,512]{1,0:T(8,128)(2,1)S(1)}, u32[]{:S(2)}, u32[]{:S(2)}) collective-permute-start(bf16[512,512]{1,0:T(8,128)(2,1)} %copy-done.13), channel_id=1, source_target_pairs={{0,4},{4,0},{1,5},{5,1},{2,6},{6,2},{3,7},{7,3},{8,12},{12,8},{9,1... | collective-permute-start | bytes 1572872 | tf_op jit(solution)/shard_map/ppermute | solution.py:569
  162.6 14.3 %collective-permute-start.35 = (bf16[16,128,128]{2,1,0:T(8,128)(2,1)S(1)}, bf16[16,128,128]{2,1,0:T(8,128)(2,1)S(1)}, u32[]{:S(2)}, u32[]{:S(2)}) collective-permute-start(bf16[16,128,128]{2,1,0:T(8,128)(2,1)S(1)} %all-to-all-done.1.refs_0_.refs_1_), channel_id=1, source_target_pairs={{0,8},{8,0},{16,24},{24,16},{1,9},{9,1},{17,25},{25,17},{2,10},{10... | collective-permute-start | bytes 1572872 | tf_op jit(solution)/shard_map/ppermute | solution.py:51
  163.5 14.0 %collective-permute-start.36 = (bf16[16,128,128]{2,1,0:T(8,128)(2,1)S(1)}, bf16[16,128,128]{2,1,0:T(8,128)(2,1)S(1)}, u32[]{:S(2)}, u32[]{:S(2)}) collective-permute-start(bf16[16,128,128]{2,1,0:T(8,128)(2,1)S(1)} %all-to-all-done.1.refs_0_.refs_1_), channel_id=1, source_target_pairs={{0,16},{8,24},{16,0},{24,8},{1,17},{9,25},{17,1},{25,9},{2,18},{10... | collective-permute-start | bytes 1572872 | tf_op jit(solution)/shard_map/ppermute | solution.py:51
  164.0 1.7 collective-permute-start.33
  164.0 2.1 %collective-permute-start.34 = (bf16[512,256]{1,0:T(8,128)(2,1)}, bf16[512,256]{1,0:T(8,128)(2,1)S(1)}, u32[]{:S(2)}, u32[]{:S(2)}) collective-permute-start(bf16[512,256]{1,0:T(8,128)(2,1)} %copy-done.9), channel_id=1, source_target_pairs={{0,4},{4,0},{1,5},{5,1},{2,6},{6,2},{3,7},{7,3},{8,12},{12,8},{9,1... | collective-permute-start | bytes 786440 | tf_op jit(solution)/shard_map/ppermute | solution.py:569
  166.1 0.8 copy-start.16
  166.9 0.9 copy-start.3
  167.8 0.9 copy-start.5
  168.8 0.9 copy-start.7
  169.7 0.9 copy-start.10
  170.7 6.9 %copy-start.8 = (bf16[512,256]{1,0:T(8,128)(2,1)S(1)}, bf16[512,256]{1,0:T(8,128)(2,1)}, u32[]{:S(2)}) copy-start(bf16[512,256]{1,0:T(8,128)(2,1)} %copy-done.6) | copy-start | bytes 786436
  170.7 6.9 %copy-start.11 = (bf16[512,256]{1,0:T(8,128)(2,1)S(1)}, bf16[512,256]{1,0:T(8,128)(2,1)}, u32[]{:S(2)}) copy-start(bf16[512,256]{1,0:T(8,128)(2,1)} %copy-done.9) | copy-start | bytes 786436
  182.3 7.6 %collective-permute-start.37 = (bf16[128,1024]{1,0:T(8,128)(2,1)S(1)}, bf16[128,1024]{1,0:T(8,128)(2,1)S(1)}, u32[]{:S(2)}, u32[]{:S(2)}) collective-permute-start(bf16[128,1024]{1,0:T(8,128)(2,1)S(1)} %get-tuple-element.115), channel_id=1, source_target_pairs={{0,8},{8,0},{16,24},{24,16},{1,9},{9,1},{17,25},{25,17},{2,10},{10... | collective-permute-start | bytes 786440 | tf_op jit(solution)/shard_map/ppermute | solution.py:51
  183.4 7.3 %collective-permute-start.38 = (bf16[128,1024]{1,0:T(8,128)(2,1)S(1)}, bf16[128,1024]{1,0:T(8,128)(2,1)S(1)}, u32[]{:S(2)}, u32[]{:S(2)}) collective-permute-start(bf16[128,1024]{1,0:T(8,128)(2,1)S(1)} %get-tuple-element.116), channel_id=1, source_target_pairs={{0,16},{8,24},{16,0},{24,8},{1,17},{9,25},{17,1},{25,9},{2,18},{10... | collective-permute-start | bytes 786440 | tf_op jit(solution)/shard_map/ppermute | solution.py:51
